TPU v7x, 32 devices: a whole 2x2x4 slice. The times are simulated.
32 devices in a mesh: groups: 2 (over y), dp: 4 (over z), seq: 2 (over x), head: 2 (over core).
Axes of the slice: x: 2, y: 2, z: 4, core: 2. Of those that a mesh axis runs over, the one named last changes fastest.
Arguments:
- tokens: bfloat16 [8, 768, 6144], P(('groups', 'dp'), 'seq'), parts along dimension 0, may hold values from -8 to 8
- ln_gain: float32 [6144], replicated, may hold values from 0.1 to 1.9
- qkv_weight: bfloat16 [6144, 24, 384], P('dp', ('seq', 'head')), may hold values from -8 to 8
Outputs:
- attended: bfloat16 [8, 768, 3072], P(('groups', 'dp'), 'seq', 'head'), parts along dimension 0
There are 2 independent parts, one for each index of `groups`. A program takes and returns all parts, laid end to end along the dimension named above; an argument that names none is the same for every part. Nothing has to cross between parts.
All inputs are finite; a program needn't handle non-finite values.
Results may differ from a plain program's by a relative error of at most 0.012.
Values may be sent and summed in bfloat16 or wider, within the bound.
No kernel may reach another device: no remote copies, remote signals or barrier semaphores. Data moves between devices by JAX's collectives and lax.ppermute only.
A program may use at most 128 MiB of HBM per device.

v0:
```python
import functools
import math

import jax
import jax.numpy as jnp
from jax import lax
from jax.experimental import pallas as pl
from jax.experimental.pallas import tpu as pltpu
from jax.sharding import PartitionSpec as P


def normalize(array, gain):
    widened = array.astype(jnp.float32)
    centered = widened - jnp.mean(widened, axis=-1, keepdims=True)
    variance = jnp.mean(centered * centered, axis=-1, keepdims=True)
    return (centered * lax.rsqrt(variance + 1e-06) * gain).astype(jnp.bfloat16)


def attend(projected):
    width = projected.shape[2] // 3
    queries = projected[:, :, :width]
    key_rows = projected[:, :, width : 2 * width]
    value_rows = projected[:, :, 2 * width :]
    scores = jnp.einsum("qhd,khd->hqk", queries, key_rows, preferred_element_type=jnp.float32) * (
        1.0 / math.sqrt(width)
    )
    highest = jnp.max(scores, axis=-1, keepdims=True)
    expo = jnp.exp(scores - highest)
    probs = (expo / jnp.sum(expo, axis=-1, keepdims=True)).astype(jnp.bfloat16)
    mixed = jnp.einsum("hqk,khd->qhd", probs, value_rows, preferred_element_type=jnp.float32)
    return mixed.astype(jnp.bfloat16).reshape(projected.shape[0], -1)


def plain(tokens, ln_gain, qkv_weight):
    images = tokens.shape[0]
    width = tokens.shape[2]
    heads_here = qkv_weight.shape[1]
    columns = heads_here * qkv_weight.shape[2]
    source = normalize(tokens, ln_gain)
    half_width = width // lax.axis_size("head")
    core_index = lax.axis_index("head")
    own_half = lax.dynamic_slice_in_dim(source, core_index * half_width, half_width, 2)
    fetched = lax.all_gather(own_half, "seq", axis=1, tiled=True)
    gathered = lax.all_gather(fetched, "head", axis=2, tiled=True)
    full_tokens = gathered.shape[1]
    features = gathered.reshape(images * full_tokens, width)
    piece = lax.all_gather(qkv_weight, "dp", axis=0, tiled=True)
    projected = jnp.dot(
        features, piece.reshape(piece.shape[0], columns), preferred_element_type=jnp.float32
    )
    projected = projected.astype(jnp.bfloat16).reshape(
        images, full_tokens, heads_here, qkv_weight.shape[2]
    )
    mixed = lax.map(attend, projected)
    return lax.all_to_all(mixed, "seq", split_axis=1, concat_axis=2, tiled=True)


def normalize_kernel(place_ref, tokens_ref, gain_ref, *normed_refs):
    rows, width = tokens_ref.shape[1:]
    lanes = 128
    slab, span = width // 4, width // 2

    def widened(begin):
        return tokens_ref[0, :, pl.ds(begin, lanes)].astype(jnp.float32)

    total = jnp.zeros((rows, lanes), jnp.float32)
    for begin in range(0, width, lanes):
        total += widened(begin)
    mean = jnp.sum(total, axis=-1, keepdims=True) / width
    total = jnp.zeros((rows, lanes), jnp.float32)
    for begin in range(0, width, lanes):
        centered = widened(begin) - mean
        total += centered * centered
    scale = lax.rsqrt(jnp.sum(total, axis=-1, keepdims=True) / width + 1e-06)
    for i in range(4):
        source = place_ref[i + 1] * slab
        for begin in range(0, slab, lanes):
            column = pl.multiple_of(source + begin, lanes)
            part = (widened(column) - mean) * scale * gain_ref[:, pl.ds(column, lanes)]
            target = i * slab % span + begin
            normed_refs[i * slab // span][:, target : target + lanes] = part.astype(jnp.bfloat16)


def normalize_part(tokens, ln_gain, part, core, order):
    width = tokens.shape[2]
    step, count = 64 if part % 64 == 0 else 32, 2
    steps = part // step
    place = jnp.stack([jnp.asarray(v, jnp.int32) for v in (core, *order)])
    return pl.pallas_call(
        normalize_kernel,
        out_shape=[jax.ShapeDtypeStruct((part, width // count), jnp.bfloat16)] * count,
        grid_spec=pltpu.PrefetchScalarGridSpec(
            num_scalar_prefetch=1,
            grid=(steps,),
            in_specs=[
                pl.BlockSpec((1, step, width), lambda i, place: (0, place[0] * steps + i, 0)),
                pl.BlockSpec((1, width), lambda i, place: (0, 0)),
            ],
            out_specs=[pl.BlockSpec((step, width // count), lambda i, place: (i, 0))] * count,
        ),
        compiler_params=pltpu.CompilerParams(vmem_limit_bytes=62 << 20),
        cost_estimate=pl.CostEstimate(
            flops=8 * part * width, bytes_accessed=4 * part * width, transcendentals=part
        ),
    )(place, tokens, ln_gain[None])


def attend_rows(projected_ref, parts, column):
    width = projected_ref.shape[1] // 3
    key_rows = projected_ref[:, width : 2 * width]
    value_rows = projected_ref[:, 2 * width :]
    begin = 0
    for part in parts:
        step = part.shape[0]
        queries = projected_ref[begin : begin + step, :width]
        scores = lax.dot_general(
            queries, key_rows, (((1,), (1,)), ((), ())), preferred_element_type=jnp.float32
        )
        highest = jnp.max(scores, axis=-1, keepdims=True)
        expo = jnp.exp2((scores - highest) * (math.log2(math.e) / math.sqrt(width)))
        mixed = jnp.dot(expo.astype(jnp.bfloat16), value_rows, preferred_element_type=jnp.float32)
        mixed = mixed / jnp.sum(expo, axis=-1, keepdims=True)
        part[:, column : column + width] = mixed.astype(jnp.bfloat16)
        begin += step


class Jobs:
    def __init__(self, **numbers):
        self.__dict__.update(numbers)

    def jobs(self, image):
        return sorted({j for use in self.uses[image] if use for j in range(*use)})


def job_kernel(plan, role_ref, *refs):
    refs = list(refs)
    take = lambda n: [refs.pop(0) for _ in range(n)]
    images, ns = range(len(plan.uses)), range(len(plan.slots))
    pieces = [[[take(2) for _ in place] for place in image] for image in plan.origins]
    weights = [[take(1) * 2 if alike else take(2) for alike in row] for row in plan.same]
    partials = [{j: take(1)[0] for j in plan.added[i]} for i in images]
    carried = [[take(plan.carried[i]) for _ in range(2)] for i in images]
    outs = [
        {j: take(2) if j in plan.finished[i] else take(1)[0] for j in plan.jobs(i)} for i in images
    ]
    features_ref, weight_ref, total_ref, projected_ref = take(4)
    token_sems, weight_sems, sum_sems, out_sems, carry_sems = take(5)
    core, inner = role_ref[0], role_ref[1]
    slab = pieces[0][0][0][0].shape[1] // 2
    tokens, wide = projected_ref.shape
    part = tokens // 4

    def features(i, n):
        return features_ref.at[pl.ds(i * tokens, tokens), pl.ds(n * slab, slab)]

    def weight(n, j):
        return weight_ref.at[pl.ds(n * slab, slab), pl.ds(j * wide, wide)]

    def total(i, j):
        return total_ref.at[pl.ds(i * tokens, tokens), pl.ds(j * wide, wide)]

    def start_tokens(i, n):
        cut, begin = plan.slots[n] // 2, plan.slots[n] % 2 * slab
        for place in range(2):
            split = len(plan.origins[i][place])
            for owner in range(split):
                row = i * tokens + 2 * place * part
                if split == 2:
                    row += (1 - core if owner else core) * part
                count = 2 * part // split
                from_rows = pl.ds(plan.origins[i][place][owner][cut], count)
                rows = pl.ds(pl.multiple_of(row, 32), count)
                pltpu.make_async_copy(
                    pieces[i][place][owner][cut].at[from_rows, pl.ds(begin, slab)],
                    features_ref.at[rows, pl.ds(n * slab, slab)],
                    token_sems.at[i, n],
                ).start()

    def start_weight(n, j, role):
        source = weights[n][j - plan.first[n]][role]
        if source.shape[0] == slab:
            pltpu.make_async_copy(source, weight(n, j), weight_sems.at[n, j]).start()
            return
        for b in range(source.shape[1] // wide):
            pltpu.make_async_copy(
                source.at[:, pl.ds(b * wide, wide)],
                weight_ref.at[pl.ds(n * slab + b * part, part), pl.ds(j * wide, wide)],
                weight_sems.at[n, j],
            ).start()

    def start_role_weight(n, j):
        if plan.same[n][j - plan.first[n]]:
            start_weight(n, j, 0)
            return

        @pl.when(inner == 1)
        def _():
            start_weight(n, j, 0)

        @pl.when(inner != 1)
        def _():
            start_weight(n, j, 1)

    def partial_copy(i, j):
        return pltpu.make_async_copy(partials[i][j], total(i, j), sum_sems.at[i, j])

    def out_copy(i, j):
        return pltpu.make_async_copy(total(i, j), outs[i][j], out_sems.at[i, j])

    def carry_copies():
        for i in images:
            for place in range(2):
                for k in range(plan.carried[i]):
                    (finished,) = plan.finished[i]
                    target = outs[i][finished][place].at[:, pl.ds(k * wide // 3, wide // 3)]
                    yield pltpu.make_async_copy(
                        carried[i][place][k], target, carry_sems.at[i, place, k]
                    )

    stages = [(i, n) for i in images for n in ns if plan.uses[i][n]]
    held = set()

    def start_stage(i, n):
        start_tokens(i, n)
        for j in range(*plan.uses[i][n]):
            if (n, j) not in held:
                held.add((n, j))
                start_role_weight(n, j)
        if not any((i, n) > (i, m) and plan.uses[i][m] for m in ns):
            for j in plan.added[i]:
                partial_copy(i, j).start()

    ahead = 2
    for stage in stages[:ahead]:
        start_stage(*stage)
    for copy in carry_copies():
        copy.start()
    ready = set()
    for index, (i, n) in enumerate(stages):
        low, high = plan.uses[i][n]
        pltpu.make_async_copy(features(i, n), features(i, n), token_sems.at[i, n]).wait()
        for j in range(low, high):
            if (n, j) not in ready:
                ready.add((n, j))
                pltpu.make_async_copy(weight(n, j), weight(n, j), weight_sems.at[n, j]).wait()
        if index + ahead < len(stages):
            start_stage(*stages[index + ahead])
        term = jnp.dot(
            features(i, n)[...],
            weight_ref[n * slab : (n + 1) * slab, low * wide : high * wide],
            preferred_element_type=jnp.float32,
        )
        for j in range(low, high):
            value = term[:, (j - low) * wide : (j - low + 1) * wide]
            mine = [m for m in ns if plan.uses[i][m] and j in range(*plan.uses[i][m])]
            if n == mine[0] and j in plan.added[i]:
                partial_copy(i, j).wait()
            if n != mine[0] or j in plan.added[i]:
                value += total(i, j)[...]
            if n == mine[-1] and j in plan.finished[i]:
                projected_ref[...] = value.astype(jnp.bfloat16)
                attend_rows(projected_ref, outs[i][j], plan.carried[i] * wide // 3)
                continue
            total(i, j)[...] = value
            if n == mine[-1]:
                out_copy(i, j).start()
    for copy in carry_copies():
        copy.wait()
    for i in images:
        for j in plan.jobs(i):
            if j not in plan.finished[i]:
                out_copy(i, j).wait()


def run_jobs(core, inner, tokens, wide, images, weights):
    images = [
        dict(
            image,
            pieces=[
                [[x if isinstance(x, tuple) else (x, 0) for x in owner] for owner in place]
                for place in image["pieces"]
            ],
            sums=image.get("sums", {}),
            finish=image.get("finish", ()),
            carry=image.get("carry", ((), ())),
        )
        for image in images
    ]
    plan = Jobs(
        origins=[[[[r for _, r in o] for o in p] for p in image["pieces"]] for image in images],
        slots=[slot for slot, _, _ in weights],
        first=[first for _, first, _ in weights],
        same=[[not isinstance(w, tuple) for w in row] for _, _, row in weights],
        uses=[image["uses"] for image in images],
        added=[tuple(image["sums"]) for image in images],
        finished=[image["finish"] for image in images],
        carried=[len(image["carry"][0]) for image in images],
    )
    operands = [x for i in images for place in i["pieces"] for owner in place for x, _ in owner]
    slab = operands[0].shape[1] // 2
    for _, _, row in weights:
        for w in row:
            operands += list(w) if isinstance(w, tuple) else [w]
    operands += [x for image in images for x in image["sums"].values()]
    operands += [x for image in images for place in image["carry"] for x in place]
    anywhere, vmem = pl.BlockSpec(memory_space=pl.ANY), pl.BlockSpec(memory_space=pltpu.VMEM)
    head = wide // 3
    shapes, specs = [], []
    for i in range(len(images)):
        for j in plan.jobs(i):
            if j in plan.finished[i]:
                shape = (tokens // 2, head * (plan.carried[i] + 1))
                shapes += [jax.ShapeDtypeStruct(shape, jnp.bfloat16)] * 2
                specs += [vmem] * 2
            else:
                shapes.append(jax.ShapeDtypeStruct((tokens, wide), jnp.float32))
                specs.append(anywhere)
    jobs = 1 + max(j for i in range(len(images)) for j in plan.jobs(i))
    count, depth, total = len(images), len(weights) * slab, len(images) * tokens
    added = sum(high - low for uses in plan.uses for low, high in filter(None, uses))
    got = pl.pallas_call(
        functools.partial(job_kernel, plan),
        out_shape=shapes,
        in_specs=[pl.BlockSpec(memory_space=pltpu.SMEM)] + [anywhere] * len(operands),
        out_specs=specs,
        scratch_shapes=[
            pltpu.VMEM((total, depth), jnp.bfloat16),
            pltpu.VMEM((depth, jobs * wide), jnp.bfloat16),
            pltpu.VMEM((total, jobs * wide), jnp.float32),
            pltpu.VMEM((tokens, wide), jnp.bfloat16),
            pltpu.SemaphoreType.DMA((count, len(weights))),
            pltpu.SemaphoreType.DMA((len(weights), jobs)),
            pltpu.SemaphoreType.DMA((count, jobs)),
            pltpu.SemaphoreType.DMA((count, jobs)),
            pltpu.SemaphoreType.DMA((count, 2, max(*plan.carried, 1))),
        ],
        compiler_params=pltpu.CompilerParams(vmem_limit_bytes=62 << 20),
        cost_estimate=pl.CostEstimate(
            flops=2 * tokens * slab * wide * added, bytes_accessed=0, transcendentals=0
        ),
    )(jnp.stack([core, inner]).astype(jnp.int32), *operands)
    got = list(got)
    return [
        {
            j: (got.pop(0), got.pop(0)) if j in plan.finished[i] else got.pop(0)
            for j in plan.jobs(i)
        }
        for i in range(count)
    ]


def join_kernel(place_ref, *refs):
    *parts, out_ref, sems = refs
    count = len(parts) // 2
    inner = place_ref[count]
    wide, head = parts[0].shape[1], parts[count].shape[1]

    def copies(i, role):
        begin = pl.multiple_of(place_ref[i] * wide, wide)
        if role:
            yield parts[i], out_ref.at[:, pl.ds(begin, wide)], sems.at[i, 0]
            return
        kept = wide - head
        yield parts[i].at[:, pl.ds(head, kept)], out_ref.at[:, pl.ds(begin, kept)], sems.at[i, 0]
        last = pl.multiple_of(begin + kept, head)
        yield parts[count + i], out_ref.at[:, pl.ds(last, head)], sems.at[i, 1]

    for role in (1, 0):

        @pl.when((inner == 1) == (role == 1))
        def _():
            every = [pltpu.make_async_copy(*c) for i in range(count) for c in copies(i, role)]
            for copy in every:
                copy.start()
            for copy in every:
                copy.wait()


def join(places, inner, parts, back):
    rows, wide = parts[0].shape
    anywhere = pl.BlockSpec(memory_space=pl.ANY)
    return pl.pallas_call(
        join_kernel,
        out_shape=jax.ShapeDtypeStruct((rows, wide * len(parts)), jnp.bfloat16),
        in_specs=[pl.BlockSpec(memory_space=pltpu.SMEM)] + [anywhere] * (2 * len(parts)),
        out_specs=pl.BlockSpec(memory_space=pltpu.VMEM),
        scratch_shapes=[pltpu.SemaphoreType.DMA((len(parts), 2))],
        cost_estimate=pl.CostEstimate(
            flops=0, bytes_accessed=4 * rows * wide * len(parts), transcendentals=0
        ),
    )(jnp.stack([*places, inner]).astype(jnp.int32), *parts, *back)


def shared(tokens, ln_gain, qkv_weight):
    groups, planes, seqs, cores = (lax.axis_size(a) for a in ("groups", "dp", "seq", "head"))
    group, plane, seq, core = (lax.axis_index(a) for a in ("groups", "dp", "seq", "head"))
    _, rows, _ = tokens.shape
    slab, heads, columns = qkv_weight.shape
    heads, part = heads // groups, rows // cores
    inner = (plane == 1) | (plane == 2)
    wait = lax.optimization_barrier

    def fold(piece):
        piece = piece.reshape(-1, part, columns).transpose(1, 0, 2)
        return piece.reshape(part, -1)

    def weight_piece(weight, j):
        return lax.dynamic_slice_in_dim(weight, group * heads + j, 1, 1)[:, 0]

    def pick(for_inner, for_ends):
        return jnp.where(inner, for_inner, for_ends)

    def pair(value):
        return lax.ppermute(value, "dp", [(0, 1), (1, 0), (2, 3), (3, 2)])

    def outward(value):
        return lax.ppermute(value, "dp", [(1, 0), (2, 3)])

    def middle(value):
        return lax.ppermute(value, "dp", [(1, 2), (2, 1)])

    swap = [(0, 1), (1, 0)]
    beside = lambda value: lax.ppermute(value, "seq", swap)
    across = lambda value: lax.ppermute(value, "groups", swap)

    def others(*values):
        got = []
        for value in values:
            if got:
                value, got[-1] = wait((value, got[-1]))
            got.append(lax.ppermute(value, "head", swap))
        return got

    beside_plane, far_inner = plane ^ 1, 2 - plane // 2
    order = (
        plane,
        pick(beside_plane, far_inner),
        pick(far_inner, beside_plane),
        3 - 3 * (plane // 2),
    )
    run = functools.partial(run_jobs, core, inner, seqs * rows, columns)

    def exchange(mixed):
        got = []
        for a in range(groups):
            for b in range(seqs):
                sent = mixed[a * seqs + b]
                if a or b:
                    steps = [
                        (g * seqs + s, (g + a) % groups * seqs + (s + b) % seqs)
                        for g in range(groups)
                        for s in range(seqs)
                    ]
                    sent = lax.ppermute(sent, ("groups", "seq"), steps)
                got.append(sent)
        return got

    normed = normalize_part(tokens, ln_gain, part, core, order)
    normed, qkv_weight = wait((normed, qkv_weight))
    cut0, cut1 = normed
    beside1, across1 = beside(cut0), across(cut0)
    own0 = weight_piece(qkv_weight, 0)
    pair1, middle1 = pair(own0), middle(own0)
    own1, own2 = weight_piece(qkv_weight, 1), weight_piece(qkv_weight, 2)
    give = pick(fold(own1), cut0)
    pair1, middle1, beside1, across1, own1, own2, cut0, cut1, tokens, give = wait(
        (pair1, middle1, beside1, across1, own1, own2, cut0, cut1, tokens, give)
    )

    pair2, middle2 = pair(give), middle(pair1)
    beside2, across2 = beside(cut1), across(cut1)
    give = pick(fold(middle1), cut1)
    far_normed = normalize_part(tokens, ln_gain, part, 1 - core, order)
    far1 = others(beside1, across1)
    pair2, middle2, beside2, across2, across1, own1, own2, far_normed, far1, give = wait(
        (pair2, middle2, beside2, across2, across1, own1, own2, far_normed, far1, give)
    )

    pair3, middle3 = pair(give), middle(own1)
    beside3, across3 = beside(across1), across(beside2)
    give = pick(middle2, own1)
    far2 = others(beside2, across2)
    pair3, middle3, beside3, across3, pair1, pair2, own2, far2, give = wait(
        (pair3, middle3, beside3, across3, pair1, pair2, own2, far2, give)
    )

    pair4, middle4 = pair(give), middle(own2)
    beside4, across4 = beside(pair2), across(pair2)
    give = pick(middle3, own2)
    pieces0 = ((normed, far_normed), ((beside1, beside2), (far1[0], far2[0])))
    owns = [own0, (own1, own0), (own2, own1)]
    ((head0, sum20, sum30),) = [
        tuple(got.values())
        for got in run(
            [dict(pieces=pieces0, uses=[(0, 3), (0, 2), (0, 1), (0, 1)], finish=(0,))],
            [(0, 0, owns), (2, 0, [middle1, (middle3, pair1)]), (1, 0, [pair1]), (3, 0, [middle2])],
        )
    ]
    far3 = others(beside3, across3)
    lent = jnp.concatenate([pair2, pair3])
    pair4, middle4, beside4, across4, own2, pair3, lent, head0, sum20, sum30, far3, give = wait(
        (pair4, middle4, beside4, across4, own2, pair3, lent, head0, sum20, sum30, far3, give)
    )

    pair5, middle5 = pair(give), middle(pair4)
    beside5, across5 = beside(pair3), across(pair3)
    pieces1 = (((across1, across2), (far1[1], far2[1])), ((beside3, across3), far3))
    image1, image0 = run(
        [
            dict(pieces=pieces1, uses=[(0, 3), (0, 3), (0, 2), (0, 1)], finish=(0,)),
            dict(pieces=pieces0, uses=[None, (2, 3), (1, 2), None], sums={1: sum20, 2: sum30}),
        ],
        [
            (0, 0, owns),
            (2, 0, [middle1, (middle3, pair1), (middle4, pair2)]),
            (1, 0, [pair1, (pair4, pair3)]),
            (3, 0, [middle2]),
        ],
    )
    far_lent, far4 = others(lent, beside4)
    pair5, middle5, beside5, across5, across4, image0, image1, far_lent, far4 = wait(
        (
            *(pair5, middle5, beside5, across5, across4),
            *(image0, image1, far_lent, far4),
        )
    )

    pair6, middle6 = outward(middle5), middle(pair5)
    beside6, across6 = beside(across4), across(beside5)
    far5, far_across4 = others(beside5, across4)
    ahead0, ahead1 = run(
        [
            dict(
                pieces=pieces,
                uses=[(0, 1), (1, 2)],
                sums={0: image[1], 1: image[2]},
                finish=(0,),
            )
            for pieces, image in ((pieces0, image0), (pieces1, image1))
        ],
        [(3, 0, [(middle5, pair4)]), (1, 1, [pair5])],
    )
    lent0 = (((pair2, pair3), (far_lent, (far_lent, part))), ((beside4, beside5), (far4, far5)))
    lent_weights = [(0, 0, [pair5]), (1, 0, [middle4]), (2, 0, [own2])]
    ((sum4,),) = [
        tuple(got.values()) for got in run([dict(pieces=lent0, uses=[(0, 1)] * 3)], lent_weights)
    ]
    pair6, middle6, beside6, across6, across5, ahead0, ahead1, sum4, far_across4 = wait(
        (pair6, middle6, beside6, across6, across5, ahead0, ahead1, sum4, far_across4)
    )

    far_across5, *far6 = [
        lax.ppermute(value, "head", swap) for value in (across5, beside6, across6)
    ]
    done0, done1, lent0 = run(
        [
            dict(pieces=p, uses=[(0, 1)], sums={0: x[1]}, finish=(0,), carry=tuple(zip(h, x[0])))
            for p, h, x in ((pieces0, head0, ahead0), (pieces1, image1[0], ahead1))
        ]
        + [dict(pieces=lent0, uses=[(0, 1)], sums={0: sum4}, finish=(0,))],
        [(3, 0, [(middle6, pair6)])],
    )
    sent = exchange((*done0[0], *done1[0]))
    lent1 = (((across4, across5), (far_across4, far_across5)), ((beside6, across6), far6))
    (lent1,) = run(
        [dict(pieces=lent1, uses=[(0, 1)] * 4, finish=(0,))], [*lent_weights, (3, 0, [middle6])]
    )

    def hand_back(mixed):
        got = []
        for a in range(groups):
            for b in range(seqs):
                steps = [
                    (
                        (g * planes + z) * seqs + s,
                        ((g + a) % groups * planes + (z ^ 1)) * seqs + (s + b) % seqs,
                    )
                    for g in range(groups)
                    for z in (1, 2)
                    for s in range(seqs)
                ]
                sent = mixed[a * seqs + b]
                got.append(lax.ppermute(sent, ("groups", "dp", "seq"), steps))
        return got

    back = hand_back((*lent0[0], *lent1[0]))
    places = [
        (seq - b) % seqs * groups + (group - a) % groups
        for a in range(groups)
        for b in range(seqs)
    ]
    return join(places, inner, sent, back)[None]


def per_device(tokens, ln_gain, qkv_weight):
    groups, planes, seqs, cores = (lax.axis_size(a) for a in ("groups", "dp", "seq", "head"))
    images, rows, width = tokens.shape
    slab, heads, _ = qkv_weight.shape
    if (groups, planes, seqs, cores) == (2, 4, 2, 2) and images == 1 and heads == 3 * groups:
        part = rows // cores
        if rows % (32 * cores) == 0 and slab % part == 0 and 2 * slab == qkv_weight.shape[2] * slab // part:
            return shared(tokens, ln_gain, qkv_weight)
    return plain(tokens, ln_gain, qkv_weight)


def solution(mesh):
    return jax.shard_map(
        per_device,
        mesh=mesh,
        in_specs=(P(("groups", "dp"), "seq", None), P(), P("dp", ("seq", "head"), None)),
        out_specs=P(("groups", "dp"), "seq", "head"),
        check_vma=False,
    )
```

profile of v0, /device:TPU:0, one launch (start us, length us, event | category | flops | bytes accessed | tf_op | source)
XLA Modules:
  0.0 251.7 jit_solution(6205317124076157135)
XLA Ops:
  0.0 0.6 stack.82.place_ref
  0.6 5.4 %shard_map.37 = (bf16[192,3072]{1,0:T(8,128)(2,1)}, bf16[192,3072]{1,0:T(8,128)(2,1)}) custom-call(s32[5]{0:T(128)} %stack.82.place_ref, bf16[1,384,6144]{2,1,0:T(8,128)(2,1)} %tokens_ref.2, f32[1,6144]{1,0:T(1,128)} %bitcast.38), custom_call_target="tpu_custom_call" | custom-call | flops 9437184 | bytes 4718592 | tf_op jit(solution)/shard_map/pallas_call | solution.py:89
  6.0 3.5 %dynamic-slice_bitcast_fusion = (bf16[1536,384]{1,0:T(8,128)(2,1)}, bf16[1536,1,384]{2,0,1:T(8,128)(2,1)S(1)}, bf16[1536,384]{1,0:T(8,128)(2,1)S(1)}) fusion(bf16[1536,6,384]{2,0,1:T(8,128)(2,1)} %param.5, s32[]{:T(128)S(6)} %select_n.80, s32[]{:T(128)S(6)} %select_n.79, s32[]{:T(128)S(6)} %select_n.78), kind=kLoop, calls=%fused_computation.1 | loop fusion | bytes 7077900 | tf_op jit(solution)/shard_map/squeeze | solution.py:408
  9.5 3.0 %collective-permute-start = (bf16[1536,384]{1,0:T(8,128)(2,1)S(1)}, bf16[1536,384]{1,0:T(8,128)(2,1)}, u32[]{:S(2)}, u32[]{:S(2)}) collective-permute-start(bf16[1536,384]{1,0:T(8,128)(2,1)S(1)} %get-tuple-element.231.refs_8_.refs_10_.refs_16_.refs_18_), channel_id=1, source_target_pairs={{0,4},{4,0},{8,12},{12,8},{1,5},{5,1},{9,13},{13,9},{2,6},{6,2},{1... | collective-permute-start | bytes 3538952 | tf_op jit(solution)/shard_map/ppermute | solution.py:414
  12.5 0.7 collective-permute-start.1
  13.3 1.6 collective-permute-start.2
  14.8 1.5 collective-permute-start.3
  16.5 1.2 broadcast_select_fusion.3
  17.7 20.8 %collective-permute-done.refs_15_.refs_16_.refs_23_.refs_26_ = bf16[1536,384]{1,0:T(8,128)(2,1)} collective-permute-done((bf16[1536,384]{1,0:T(8,128)(2,1)S(1)}, bf16[1536,384]{1,0:T(8,128)(2,1)}, u32[]{:S(2)}, u32[]{:S(2)}) %collective-permute-start) | collective-permute-done | bytes 1179680 | tf_op jit(solution)/shard_map/ppermute | solution.py:414
  38.6 2.2 collective-permute-done.2.refs_4_.refs_12_
  40.8 1.3 collective-permute-done.3.refs_0_.refs_8_
  42.1 1.2 collective-permute-start.6
  43.3 1.5 collective-permute-start.7
  44.8 4.0 %collective-permute-start.4 = (bf16[192,3072]{1,0:T(8,128)(2,1)}, bf16[192,3072]{1,0:T(8,128)(2,1)}, u32[]{:S(2)}, u32[]{:S(2)}) collective-permute-start(bf16[192,3072]{1,0:T(8,128)(2,1)} %broadcast_select_fusion.3), channel_id=1, source_target_pairs={{0,4},{4,0},{8,12},{12,8},{1,5},{5,1},{9,13},{13,9},{2,6},{6,2},{1... | collective-permute-start | bytes 3538952 | tf_op jit(solution)/shard_map/ppermute | solution.py:414
  48.8 1.7 collective-permute-start.5
  50.5 1.1 copy-done.5
  51.6 0.6 stack.84.place_ref
  52.2 1.2 copy.8
  53.4 5.4 %shard_map.38 = (bf16[192,3072]{1,0:T(8,128)(2,1)}, bf16[192,3072]{1,0:T(8,128)(2,1)}) custom-call(s32[5]{0:T(128)} %stack.84.place_ref, bf16[1,384,6144]{2,1,0:T(8,128)(2,1)} %tokens_ref.2, f32[1,6144]{1,0:T(1,128)} %bitcast.39), custom_call_target="tpu_custom_call" | custom-call | flops 9437184 | bytes 4718592 | tf_op jit(solution)/shard_map/pallas_call | solution.py:89
  58.8 1.4 broadcast_select_fusion.2
  60.2 15.0 %collective-permute-done.4.refs_25_.refs_0_.refs_16_ = bf16[192,3072]{1,0:T(8,128)(2,1)} collective-permute-done((bf16[192,3072]{1,0:T(8,128)(2,1)}, bf16[192,3072]{1,0:T(8,128)(2,1)}, u32[]{:S(2)}, u32[]{:S(2)}) %collective-permute-start.4) | collective-permute-done | bytes 1179680 | tf_op jit(solution)/shard_map/ppermute | solution.py:414
  75.3 0.6 collective-permute-start.13
  75.9 3.6 %collective-permute-start.10 = (bf16[192,3072]{1,0:T(8,128)(2,1)S(1)}, bf16[192,3072]{1,0:T(8,128)(2,1)S(1)}, u32[]{:S(2)}, u32[]{:S(2)}) collective-permute-start(bf16[192,3072]{1,0:T(8,128)(2,1)S(1)} %broadcast_select_fusion.2), channel_id=1, source_target_pairs={{0,4},{4,0},{8,12},{12,8},{1,5},{5,1},{9,13},{13,9},{2,6},{6,2},{1... | collective-permute-start | bytes 3538952 | tf_op jit(solution)/shard_map/ppermute | solution.py:414
  79.5 0.7 collective-permute-start.11
  80.2 0.9 collective-permute-start.12
  81.2 1.2 broadcast_select_fusion.1
  82.4 23.4 %collective-permute-done.10.refs_28_.refs_1_.refs_17_ = bf16[192,3072]{1,0:T(8,128)(2,1)S(1)} collective-permute-done((bf16[192,3072]{1,0:T(8,128)(2,1)S(1)}, bf16[192,3072]{1,0:T(8,128)(2,1)S(1)}, u32[]{:S(2)}, u32[]{:S(2)}) %collective-permute-start.10) | collective-permute-done | bytes 1179680 | tf_op jit(solution)/shard_map/ppermute | solution.py:414
  105.8 2.6 %collective-permute-done.12.refs_4_.refs_12_ = bf16[192,3072]{1,0:T(8,128)(2,1)} collective-permute-done((bf16[192,3072]{1,0:T(8,128)(2,1)}, bf16[192,3072]{1,0:T(8,128)(2,1)}, u32[]{:S(2)}, u32[]{:S(2)}) %collective-permute-start.12) | collective-permute-done | bytes 1179680 | tf_op jit(solution)/shard_map/ppermute | solution.py:423
  108.5 0.6 pad_add_fusion.role_ref
  109.1 0.8 collective-permute-start.18
  109.9 1.5 collective-permute-start.19
  111.4 2.0 collective-permute-start.16
  113.4 2.2 collective-permute-start.17
  115.8 3.2 %pad_maximum_fusion = bf16[384,3072]{1,0:T(8,128)(2,1)} fusion(bf16[192,3072]{1,0:T(8,128)(2,1)S(1)} %collective-permute-done.10.refs_28_.refs_1_.refs_17_, bf16[192,3072]{1,0:T(8,128)(2,1)} %collective-permute-done.4.refs_25_.refs_0_.refs_16_), kind=kLoop, calls=%fused_computation | loop fusion | flops 4718592 | bytes 4718592 | tf_op jit(solution)/shard_map/concatenate | solution.py:500
  118.9 2.5 broadcast_select_fusion
  121.4 15.0 %shard_map.39 = (bf16[384,128]{1,0:T(8,128)(2,1)}, bf16[384,128]{1,0:T(8,128)(2,1)}, f32[768,384]{1,0:T(8,128)}, f32[768,384]{1,0:T(8,128)}) custom-call(s32[2]{0:T(128)} %pad_add_fusion.role_ref, bf16[192,3072]{1,0:T(8,128)(2,1)} %get-tuple-element.119.refs_0_.refs_8_, bf16[192,3072]{1,0:T(8,128)(2,1)} %get-tuple-element.124.refs_1_.refs_9_, ...), custom_call_target="tpu_custom_call" | custom-call | flops 6341787648 | tf_op jit(solution)/shard_map/pallas_call | solution.py:321
  136.4 3.4 %collective-permute-done.16.refs_27_.refs_17_ = bf16[1536,384]{1,0:T(8,128)(2,1)} collective-permute-done((bf16[1536,384]{1,0:T(8,128)(2,1)}, bf16[1536,384]{1,0:T(8,128)(2,1)}, u32[]{:S(2)}, u32[]{:S(2)}) %collective-permute-start.16) | collective-permute-done | bytes 1179680 | tf_op jit(solution)/shard_map/ppermute | solution.py:414
  139.9 1.2 collective-permute-start.24
  141.2 0.5 collective-permute-start.25
  141.7 3.6 %collective-permute-start.22 = (bf16[1536,384]{1,0:T(8,128)(2,1)}, bf16[1536,384]{1,0:T(8,128)(2,1)}, u32[]{:S(2)}, u32[]{:S(2)}) collective-permute-start(bf16[1536,384]{1,0:T(8,128)(2,1)} %broadcast_select_fusion), channel_id=1, source_target_pairs={{0,4},{4,0},{8,12},{12,8},{1,5},{5,1},{9,13},{13,9},{2,6},{6,2},{1... | collective-permute-start | bytes 3538952 | tf_op jit(solution)/shard_map/ppermute | solution.py:414
  145.3 1.9 collective-permute-start.23
  147.3 22.7 %shard_map.40 = (bf16[384,128]{1,0:T(8,128)(2,1)}, bf16[384,128]{1,0:T(8,128)(2,1)}, f32[768,384]{1,0:T(8,128)}, f32[768,384]{1,0:T(8,128)}, f32[768,384]{1,0:T(8,128)}, /*index=5*/f32[768,384]{1,0:T(8,128)}) custom-call(s32[2]{0:T(128)} %pad_add_fusion.role_ref, bf16[192,3072]{1,0:T(8,128)(2,1)} %collective-permute-done.3.refs_0_.refs_8_, ...), custom_call_target="tpu_custom_call" | custom-call | flops 9965666304 | tf_op jit(solution)/shard_map/pallas_call | solution.py:321
  170.0 1.6 collective-permute-done.22.refs_18_.refs_8_
  171.7 1.6 collective-permute-start.32
  173.3 1.3 collective-permute-start.29
  174.6 1.9 collective-permute-start.30
  176.5 0.9 collective-permute-start.31
  177.4 14.1 %shard_map.41 = (bf16[384,128]{1,0:T(8,128)(2,1)}, bf16[384,128]{1,0:T(8,128)(2,1)}, f32[768,384]{1,0:T(8,128)}, bf16[384,128]{1,0:T(8,128)(2,1)}, bf16[384,128]{1,0:T(8,128)(2,1)}, /*index=5*/f32[768,384]{1,0:T(8,128)}) custom-call(s32[2]{0:T(128)} %pad_add_fusion.role_ref, bf16[192,3072]{1,0:T(8,128)(2,1)} %get-tuple-element.119.refs_0_.refs_8_, ...), custom_call_target="tpu_custom_call" | custom-call | flops 3623878656 | tf_op jit(solution)/shard_map/pallas_call | solution.py:321
  191.5 8.0 %shard_map.42.refs_28_ = f32[768,384]{1,0:T(8,128)} custom-call(s32[2]{0:T(128)} %pad_add_fusion.role_ref, bf16[192,3072]{1,0:T(8,128)(2,1)} %collective-permute-done.4.refs_25_.refs_0_.refs_16_, bf16[192,3072]{1,0:T(8,128)(2,1)} %copy-done.2, bf16[384,3072]{1,0:T(8,128)(2,1)} %collective-permute-done.26.refs_2_.refs_3_.refs_18_.refs_19_, ...), custom_call_target="tpu_custom_call" | custom-call | flops 2717908992 | tf_op jit(solution)/shard_map/pallas_call | solution.py:321
  199.5 5.3 %collective-permute-done.29.refs_25_ = bf16[1536,384]{1,0:T(8,128)(2,1)} collective-permute-done((bf16[1536,384]{1,0:T(8,128)(2,1)}, bf16[1536,384]{1,0:T(8,128)(2,1)}, u32[]{:S(2)}, u32[]{:S(2)}) %collective-permute-start.29) | collective-permute-done | bytes 1179680 | tf_op jit(solution)/shard_map/ppermute | solution.py:417
  205.5 13.8 %shard_map.43 = (bf16[384,384]{1,0:T(8,128)(2,1)}, bf16[384,384]{1,0:T(8,128)(2,1)}, bf16[384,384]{1,0:T(8,128)(2,1)}, bf16[384,384]{1,0:T(8,128)(2,1)}, bf16[38...) custom-call(s32[2]{0:T(128)} %pad_add_fusion.role_ref, bf16[192,3072]{1,0:T(8,128)(2,1)} %get-tuple-element.119.refs_0_.refs_8_, ...), custom_call_target="tpu_custom_call" | custom-call | flops 2717908992 | tf_op jit(solution)/shard_map/pallas_call | solution.py:321
  219.3 0.9 collective-permute-start.34
  220.2 0.5 collective-permute-start.35
  220.8 2.1 collective-permute-start.36
  222.9 1.3 collective-permute-start.37
  224.2 1.3 collective-permute-start.38
  225.5 10.2 %shard_map.44 = (bf16[384,128]{1,0:T(8,128)(2,1)}, bf16[384,128]{1,0:T(8,128)(2,1)}) custom-call(s32[2]{0:T(128)} %pad_add_fusion.role_ref, bf16[192,3072]{1,0:T(8,128)(2,1)} %collective-permute-done.19.refs_0_, bf16[192,3072]{1,0:T(8,128)(2,1)} %collective-permute-done.25.refs_1_, bf16[192,3072]{1,0:T(8,128)(2,1)} %collective-permute-done.33.refs_2_, ...), custom_call_target="tpu_custom_call" | custom-call | flops 3623878656 | tf_op jit(solution)/shard_map/pallas_call | solution.py:321
  235.8 1.3 collective-permute-start.42
  237.1 1.3 collective-permute-start.43
  238.4 0.6 stack.75.place_ref
  239.1 6.8 %collective-permute-done.42.refs_6_ = bf16[384,128]{1,0:T(8,128)(2,1)S(1)} collective-permute-done((bf16[384,128]{1,0:T(8,128)(2,1)}, bf16[384,128]{1,0:T(8,128)(2,1)S(1)}, u32[]{:S(2)}, u32[]{:S(2)}) %collective-permute-start.42) | collective-permute-done | bytes 98336 | tf_op jit(solution)/shard_map/ppermute | solution.py:583
  245.9 1.6 collective-permute-done.43.refs_7_
  247.5 0.6 copy-done.18
  248.1 3.1 %shard_map.45 = bf16[384,1536]{1,0:T(8,128)(2,1)} custom-call(s32[5]{0:T(128)} %stack.75.place_ref, bf16[384,384]{1,0:T(8,128)(2,1)} %get-tuple-element.217.refs_0_, bf16[384,384]{1,0:T(8,128)(2,1)} %copy-done.13, bf16[384,384]{1,0:T(8,128)(2,1)} %copy-done.14, bf16[384,384]{1,0:T(8,128)(2,1)} %collective-permute-done.36.refs_3_, ...), custom_call_target="tpu_custom_call" | custom-call | bytes 2359296 | tf_op jit(solution)/shard_map/pallas_call | solution.py:382
  (83 shorter events, 1.5 us)
Async XLA Ops:
  6.0 7.3 %copy-start.1 = (bf16[192,3072]{1,0:T(8,128)(2,1)S(1)}, bf16[192,3072]{1,0:T(8,128)(2,1)}, u32[]{:S(2)}) copy-start(bf16[192,3072]{1,0:T(8,128)(2,1)} %get-tuple-element.119.refs_0_.refs_8_) | copy-start | bytes 3538948
  9.5 7.1 %copy-start.7 = (bf16[1536,384]{1,0:T(8,128)(2,1)}, bf16[1536,384]{1,0:T(8,128)(2,1)S(1)}, u32[]{:S(2)}) copy-start(bf16[1536,384]{1,0:T(8,128)(2,1)S(1)} %get-tuple-element.231.refs_8_.refs_10_.refs_16_.refs_18_) | copy-start | bytes 3538948
  9.5 71.7 %copy-start = (bf16[1536,1,384]{2,0,1:T(8,128)(2,1)}, bf16[1536,1,384]{2,0,1:T(8,128)(2,1)S(1)}, u32[]{:S(2)}) copy-start(bf16[1536,1,384]{2,0,1:T(8,128)(2,1)S(1)} %get-tuple-element.230) | copy-start | bytes 3538948
  9.5 29.1 %collective-permute-start = (bf16[1536,384]{1,0:T(8,128)(2,1)S(1)}, bf16[1536,384]{1,0:T(8,128)(2,1)}, u32[]{:S(2)}, u32[]{:S(2)}) collective-permute-start(bf16[1536,384]{1,0:T(8,128)(2,1)S(1)} %get-tuple-element.231.refs_8_.refs_10_.refs_16_.refs_18_), channel_id=1, source_target_pairs={{0,4},{4,0},{8,12},{12,8},{1,5},{5,1},{9,13},{13,9},{2,6},{6,2},{1... | collective-permute-start | bytes 3538952 | tf_op jit(solution)/shard_map/ppermute | solution.py:414
  12.5 26.1 %collective-permute-start.1 = (bf16[1536,384]{1,0:T(8,128)(2,1)S(1)}, bf16[1536,384]{1,0:T(8,128)(2,1)S(1)}, u32[]{:S(2)}, u32[]{:S(2)}) collective-permute-start(bf16[1536,384]{1,0:T(8,128)(2,1)S(1)} %get-tuple-element.231.refs_8_.refs_10_.refs_16_.refs_18_), channel_id=1, source_target_pairs={{4,8},{8,4},{5,9},{9,5},{6,10},{10,6},{7,11},{11,7},{20,24},{24,20... | collective-permute-start | bytes 3538952 | tf_op jit(solution)/shard_map/ppermute | solution.py:420
  13.3 27.5 %collective-permute-start.2 = (bf16[192,3072]{1,0:T(8,128)(2,1)S(1)}, bf16[192,3072]{1,0:T(8,128)(2,1)S(1)}, u32[]{:S(2)}, u32[]{:S(2)}) collective-permute-start(bf16[192,3072]{1,0:T(8,128)(2,1)S(1)} %copy-done.1), channel_id=1, source_target_pairs={{0,2},{2,0},{1,3},{3,1},{4,6},{6,4},{5,7},{7,5},{8,10},{10,8},{9,1... | collective-permute-start | bytes 3538952 | tf_op jit(solution)/shard_map/ppermute | solution.py:423
  14.8 27.3 %collective-permute-start.3 = (bf16[192,3072]{1,0:T(8,128)(2,1)S(1)}, bf16[192,3072]{1,0:T(8,128)(2,1)}, u32[]{:S(2)}, u32[]{:S(2)}) collective-permute-start(bf16[192,3072]{1,0:T(8,128)(2,1)S(1)} %copy-done.1), channel_id=1, source_target_pairs={{0,16},{16,0},{1,17},{17,1},{2,18},{18,2},{3,19},{19,3},{4,20},{20... | collective-permute-start | bytes 3538952 | tf_op jit(solution)/shard_map/ppermute | solution.py:424
  38.6 13.6 %copy-start.9 = (bf16[1536,384]{1,0:T(8,128)(2,1)}, bf16[1536,384]{1,0:T(8,128)(2,1)S(1)}, u32[]{:S(2)}) copy-start(bf16[1536,384]{1,0:T(8,128)(2,1)S(1)} %collective-permute-done.1.refs_13_.refs_21_) | copy-start | bytes 3538948
  40.8 1.3 copy-start.4
  42.1 8.4 %collective-permute-start.8 = (bf16[192,3072]{1,0:T(8,128)(2,1)S(1)}, bf16[192,3072]{1,0:T(8,128)(2,1)S(1)}, u32[]{:S(2)}, u32[]{:S(2)}) collective-permute-start(bf16[192,3072]{1,0:T(8,128)(2,1)S(1)} %collective-permute-done.2.refs_4_.refs_12_), channel_id=1, source_target_pairs={{0,1},{1,0},{2,3},{3,2},{4,5},{5,4},{6,7},{7,6},{8,9},{9,8},{10,11... | collective-permute-start | bytes 3538952 | tf_op jit(solution)/shard_map/ppermute | solution.py:431
  42.1 33.1 %collective-permute-start.6 = (bf16[192,3072]{1,0:T(8,128)(2,1)}, bf16[192,3072]{1,0:T(8,128)(2,1)}, u32[]{:S(2)}, u32[]{:S(2)}) collective-permute-start(bf16[192,3072]{1,0:T(8,128)(2,1)} %get-tuple-element.124.refs_1_.refs_9_), channel_id=1, source_target_pairs={{0,2},{2,0},{1,3},{3,1},{4,6},{6,4},{5,7},{7,5},{8,10},{10,8},{9,1... | collective-permute-start | bytes 3538952 | tf_op jit(solution)/shard_map/ppermute | solution.py:423
  43.3 32.0 %collective-permute-start.7 = (bf16[192,3072]{1,0:T(8,128)(2,1)}, bf16[192,3072]{1,0:T(8,128)(2,1)}, u32[]{:S(2)}, u32[]{:S(2)}) collective-permute-start(bf16[192,3072]{1,0:T(8,128)(2,1)} %get-tuple-element.124.refs_1_.refs_9_), channel_id=1, source_target_pairs={{0,16},{16,0},{1,17},{17,1},{2,18},{18,2},{3,19},{19,3},{4,20},{20... | collective-permute-start | bytes 3538952 | tf_op jit(solution)/shard_map/ppermute | solution.py:424
  44.8 30.4 %collective-permute-start.4 = (bf16[192,3072]{1,0:T(8,128)(2,1)}, bf16[192,3072]{1,0:T(8,128)(2,1)}, u32[]{:S(2)}, u32[]{:S(2)}) collective-permute-start(bf16[192,3072]{1,0:T(8,128)(2,1)} %broadcast_select_fusion.3), channel_id=1, source_target_pairs={{0,4},{4,0},{8,12},{12,8},{1,5},{5,1},{9,13},{13,9},{2,6},{6,2},{1... | collective-permute-start | bytes 3538952 | tf_op jit(solution)/shard_map/ppermute | solution.py:414
  48.8 26.4 %collective-permute-start.5 = (bf16[1536,384]{1,0:T(8,128)(2,1)}, bf16[1536,384]{1,0:T(8,128)(2,1)}, u32[]{:S(2)}, u32[]{:S(2)}) collective-permute-start(bf16[1536,384]{1,0:T(8,128)(2,1)} %collective-permute-done.refs_15_.refs_16_.refs_23_.refs_26_), channel_id=1, source_target_pairs={{4,8},{8,4},{5,9},{9,5},{6,10},{10,6},{7,11},{11,7},{20,24},{24,20... | collective-permute-start | bytes 3538952 | tf_op jit(solution)/shard_map/ppermute | solution.py:420
  50.5 1.1 copy-start.5
  51.6 23.7 %collective-permute-start.9 = (bf16[192,3072]{1,0:T(8,128)(2,1)}, bf16[192,3072]{1,0:T(8,128)(2,1)}, u32[]{:S(2)}, u32[]{:S(2)}) collective-permute-start(bf16[192,3072]{1,0:T(8,128)(2,1)} %collective-permute-done.3.refs_0_.refs_8_), channel_id=1, source_target_pairs={{0,1},{1,0},{2,3},{3,2},{4,5},{5,4},{6,7},{7,6},{8,9},{9,8},{10,11... | collective-permute-start | bytes 3538952 | tf_op jit(solution)/shard_map/ppermute | solution.py:431
  75.2 5.9 %collective-permute-start.14 = (bf16[192,3072]{1,0:T(8,128)(2,1)}, bf16[192,3072]{1,0:T(8,128)(2,1)}, u32[]{:S(2)}, u32[]{:S(2)}) collective-permute-start(bf16[192,3072]{1,0:T(8,128)(2,1)} %collective-permute-done.6.refs_5_.refs_13_), channel_id=1, source_target_pairs={{0,1},{1,0},{2,3},{3,2},{4,5},{5,4},{6,7},{7,6},{8,9},{9,8},{10,11... | collective-permute-start | bytes 3538952 | tf_op jit(solution)/shard_map/ppermute | solution.py:431
  75.3 33.1 %collective-permute-start.13 = (bf16[192,3072]{1,0:T(8,128)(2,1)}, bf16[192,3072]{1,0:T(8,128)(2,1)}, u32[]{:S(2)}, u32[]{:S(2)}) collective-permute-start(bf16[192,3072]{1,0:T(8,128)(2,1)} %collective-permute-done.6.refs_5_.refs_13_), channel_id=1, source_target_pairs={{0,16},{16,0},{1,17},{17,1},{2,18},{18,2},{3,19},{19,3},{4,20},{20... | collective-permute-start | bytes 3538952 | tf_op jit(solution)/shard_map/ppermute | solution.py:424
  75.9 29.9 %collective-permute-start.10 = (bf16[192,3072]{1,0:T(8,128)(2,1)S(1)}, bf16[192,3072]{1,0:T(8,128)(2,1)S(1)}, u32[]{:S(2)}, u32[]{:S(2)}) collective-permute-start(bf16[192,3072]{1,0:T(8,128)(2,1)S(1)} %broadcast_select_fusion.2), channel_id=1, source_target_pairs={{0,4},{4,0},{8,12},{12,8},{1,5},{5,1},{9,13},{13,9},{2,6},{6,2},{1... | collective-permute-start | bytes 3538952 | tf_op jit(solution)/shard_map/ppermute | solution.py:414
  79.5 26.3 %collective-permute-start.11 = (bf16[1536,384]{1,0:T(8,128)(2,1)S(1)}, bf16[1536,384]{1,0:T(8,128)(2,1)S(1)}, u32[]{:S(2)}, u32[]{:S(2)}) collective-permute-start(bf16[1536,384]{1,0:T(8,128)(2,1)S(1)} %bitcast.29), channel_id=1, source_target_pairs={{4,8},{8,4},{5,9},{9,5},{6,10},{10,6},{7,11},{11,7},{20,24},{24,20... | collective-permute-start | bytes 3538952 | tf_op jit(solution)/shard_map/ppermute | solution.py:420
  80.2 28.1 %collective-permute-start.12 = (bf16[192,3072]{1,0:T(8,128)(2,1)}, bf16[192,3072]{1,0:T(8,128)(2,1)}, u32[]{:S(2)}, u32[]{:S(2)}) collective-permute-start(bf16[192,3072]{1,0:T(8,128)(2,1)} %collective-permute-done.3.refs_0_.refs_8_), channel_id=1, source_target_pairs={{0,2},{2,0},{1,3},{3,1},{4,6},{6,4},{5,7},{7,5},{8,10},{10,8},{9,1... | collective-permute-start | bytes 3538952 | tf_op jit(solution)/shard_map/ppermute | solution.py:423
  81.2 27.2 %collective-permute-start.15 = (bf16[192,3072]{1,0:T(8,128)(2,1)}, bf16[192,3072]{1,0:T(8,128)(2,1)}, u32[]{:S(2)}, u32[]{:S(2)}) collective-permute-start(bf16[192,3072]{1,0:T(8,128)(2,1)} %collective-permute-done.7.refs_1_.refs_9_), channel_id=1, source_target_pairs={{0,1},{1,0},{2,3},{3,2},{4,5},{5,4},{6,7},{7,6},{8,9},{9,8},{10,11... | collective-permute-start | bytes 3538952 | tf_op jit(solution)/shard_map/ppermute | solution.py:431
  105.8 13.1 %copy-start.2 = (bf16[192,3072]{1,0:T(8,128)(2,1)}, bf16[192,3072]{1,0:T(8,128)(2,1)S(1)}, u32[]{:S(2)}) copy-start(bf16[192,3072]{1,0:T(8,128)(2,1)S(1)} %collective-permute-done.10.refs_28_.refs_1_.refs_17_) | copy-start | bytes 3538948
  105.8 2.6 %copy-start.10 = (bf16[1536,384]{1,0:T(8,128)(2,1)}, bf16[1536,384]{1,0:T(8,128)(2,1)S(1)}, u32[]{:S(2)}) copy-start(bf16[1536,384]{1,0:T(8,128)(2,1)S(1)} %collective-permute-done.11.refs_14_.refs_22_) | copy-start | bytes 3538948
  108.4 7.3 %collective-permute-start.20 = (bf16[192,3072]{1,0:T(8,128)(2,1)}, bf16[192,3072]{1,0:T(8,128)(2,1)S(1)}, u32[]{:S(2)}, u32[]{:S(2)}) collective-permute-start(bf16[192,3072]{1,0:T(8,128)(2,1)} %collective-permute-done.12.refs_4_.refs_12_), channel_id=1, source_target_pairs={{0,1},{1,0},{2,3},{3,2},{4,5},{5,4},{6,7},{7,6},{8,9},{9,8},{10,11... | collective-permute-start | bytes 3538952 | tf_op jit(solution)/shard_map/ppermute | solution.py:431
  109.1 9.9 %copy-start.11 = (bf16[1536,384]{1,0:T(8,128)(2,1)S(1)}, bf16[1536,384]{1,0:T(8,128)(2,1)}, u32[]{:S(2)}) copy-start(bf16[1536,384]{1,0:T(8,128)(2,1)} %copy-done.10) | copy-start | bytes 3538948
  109.1 30.8 %collective-permute-start.18 = (bf16[192,3072]{1,0:T(8,128)(2,1)}, bf16[192,3072]{1,0:T(8,128)(2,1)}, u32[]{:S(2)}, u32[]{:S(2)}) collective-permute-start(bf16[192,3072]{1,0:T(8,128)(2,1)} %collective-permute-done.4.refs_25_.refs_0_.refs_16_), channel_id=1, source_target_pairs={{0,2},{2,0},{1,3},{3,1},{4,6},{6,4},{5,7},{7,5},{8,10},{10,8},{9,1... | collective-permute-start | bytes 3538952 | tf_op jit(solution)/shard_map/ppermute | solution.py:423
  109.9 29.9 %collective-permute-start.19 = (bf16[192,3072]{1,0:T(8,128)(2,1)}, bf16[192,3072]{1,0:T(8,128)(2,1)}, u32[]{:S(2)}, u32[]{:S(2)}) collective-permute-start(bf16[192,3072]{1,0:T(8,128)(2,1)} %collective-permute-done.4.refs_25_.refs_0_.refs_16_), channel_id=1, source_target_pairs={{0,16},{16,0},{1,17},{17,1},{2,18},{18,2},{3,19},{19,3},{4,20},{20... | collective-permute-start | bytes 3538952 | tf_op jit(solution)/shard_map/ppermute | solution.py:424
  111.4 28.4 %collective-permute-start.16 = (bf16[1536,384]{1,0:T(8,128)(2,1)}, bf16[1536,384]{1,0:T(8,128)(2,1)}, u32[]{:S(2)}, u32[]{:S(2)}) collective-permute-start(bf16[1536,384]{1,0:T(8,128)(2,1)} %broadcast_select_fusion.1), channel_id=1, source_target_pairs={{0,4},{4,0},{8,12},{12,8},{1,5},{5,1},{9,13},{13,9},{2,6},{6,2},{1... | collective-permute-start | bytes 3538952 | tf_op jit(solution)/shard_map/ppermute | solution.py:414
  113.4 26.4 %collective-permute-start.17 = (bf16[1536,384]{1,0:T(8,128)(2,1)}, bf16[1536,384]{1,0:T(8,128)(2,1)}, u32[]{:S(2)}, u32[]{:S(2)}) collective-permute-start(bf16[1536,384]{1,0:T(8,128)(2,1)} %get-tuple-element.202.refs_11_.refs_19_.refs_10_), channel_id=1, source_target_pairs={{4,8},{8,4},{5,9},{9,5},{6,10},{10,6},{7,11},{11,7},{20,24},{24,20... | collective-permute-start | bytes 3538952 | tf_op jit(solution)/shard_map/ppermute | solution.py:420
  115.7 3.3 %copy-start.6 = (bf16[192,3072]{1,0:T(8,128)(2,1)}, bf16[192,3072]{1,0:T(8,128)(2,1)S(1)}, u32[]{:S(2)}) copy-start(bf16[192,3072]{1,0:T(8,128)(2,1)S(1)} %collective-permute-done.20.refs_6_.refs_14_) | copy-start | bytes 3538948
  115.7 24.2 %collective-permute-start.21 = (bf16[192,3072]{1,0:T(8,128)(2,1)}, bf16[192,3072]{1,0:T(8,128)(2,1)}, u32[]{:S(2)}, u32[]{:S(2)}) collective-permute-start(bf16[192,3072]{1,0:T(8,128)(2,1)} %collective-permute-done.13.refs_5_.refs_13_), channel_id=1, source_target_pairs={{0,1},{1,0},{2,3},{3,2},{4,5},{5,4},{6,7},{7,6},{8,9},{9,8},{10,11... | collective-permute-start | bytes 3538952 | tf_op jit(solution)/shard_map/ppermute | solution.py:431
  121.4 18.5 %copy-start.3 = (bf16[192,3072]{1,0:T(8,128)(2,1)S(1)}, bf16[192,3072]{1,0:T(8,128)(2,1)}, u32[]{:S(2)}) copy-start(bf16[192,3072]{1,0:T(8,128)(2,1)} %copy-done.2) | copy-start | bytes 3538948
  139.8 7.3 %collective-permute-start.26 = (bf16[384,3072]{1,0:T(8,128)(2,1)}, bf16[384,3072]{1,0:T(8,128)(2,1)}, u32[]{:S(2)}, u32[]{:S(2)}) collective-permute-start(bf16[384,3072]{1,0:T(8,128)(2,1)} %pad_maximum_fusion), channel_id=1, source_target_pairs={{0,1},{1,0},{2,3},{3,2},{4,5},{5,4},{6,7},{7,6},{8,9},{9,8},{10,11... | collective-permute-start | bytes 7077896 | tf_op jit(solution)/shard_map/ppermute | solution.py:431
  139.9 31.7 %collective-permute-start.24 = (bf16[192,3072]{1,0:T(8,128)(2,1)S(1)}, bf16[192,3072]{1,0:T(8,128)(2,1)}, u32[]{:S(2)}, u32[]{:S(2)}) collective-permute-start(bf16[192,3072]{1,0:T(8,128)(2,1)S(1)} %copy-done.3), channel_id=1, source_target_pairs={{0,2},{2,0},{1,3},{3,1},{4,6},{6,4},{5,7},{7,5},{8,10},{10,8},{9,1... | collective-permute-start | bytes 3538952 | tf_op jit(solution)/shard_map/ppermute | solution.py:423
  141.2 30.5 %collective-permute-start.25 = (bf16[192,3072]{1,0:T(8,128)(2,1)S(1)}, bf16[192,3072]{1,0:T(8,128)(2,1)}, u32[]{:S(2)}, u32[]{:S(2)}) collective-permute-start(bf16[192,3072]{1,0:T(8,128)(2,1)S(1)} %copy-done.3), channel_id=1, source_target_pairs={{0,16},{16,0},{1,17},{17,1},{2,18},{18,2},{3,19},{19,3},{4,20},{20... | collective-permute-start | bytes 3538952 | tf_op jit(solution)/shard_map/ppermute | solution.py:424
  141.7 29.9 %collective-permute-start.22 = (bf16[1536,384]{1,0:T(8,128)(2,1)}, bf16[1536,384]{1,0:T(8,128)(2,1)}, u32[]{:S(2)}, u32[]{:S(2)}) collective-permute-start(bf16[1536,384]{1,0:T(8,128)(2,1)} %broadcast_select_fusion), channel_id=1, source_target_pairs={{0,4},{4,0},{8,12},{12,8},{1,5},{5,1},{9,13},{13,9},{2,6},{6,2},{1... | collective-permute-start | bytes 3538952 | tf_op jit(solution)/shard_map/ppermute | solution.py:414
  145.3 26.3 %collective-permute-start.23 = (bf16[1536,384]{1,0:T(8,128)(2,1)}, bf16[1536,384]{1,0:T(8,128)(2,1)}, u32[]{:S(2)}, u32[]{:S(2)}) collective-permute-start(bf16[1536,384]{1,0:T(8,128)(2,1)} %collective-permute-done.16.refs_27_.refs_17_), channel_id=1, source_target_pairs={{4,8},{8,4},{5,9},{9,5},{6,10},{10,6},{7,11},{11,7},{20,24},{24,20... | collective-permute-start | bytes 3538952 | tf_op jit(solution)/shard_map/ppermute | solution.py:420
  147.2 24.5 %collective-permute-start.27 = (bf16[192,3072]{1,0:T(8,128)(2,1)}, bf16[192,3072]{1,0:T(8,128)(2,1)}, u32[]{:S(2)}, u32[]{:S(2)}) collective-permute-start(bf16[192,3072]{1,0:T(8,128)(2,1)} %collective-permute-done.18.refs_4_.refs_20_), channel_id=1, source_target_pairs={{0,1},{1,0},{2,3},{3,2},{4,5},{5,4},{6,7},{7,6},{8,9},{9,8},{10,11... | collective-permute-start | bytes 3538952 | tf_op jit(solution)/shard_map/ppermute | solution.py:431
  171.7 5.7 %collective-permute-start.28 = (bf16[192,3072]{1,0:T(8,128)(2,1)}, bf16[192,3072]{1,0:T(8,128)(2,1)S(1)}, u32[]{:S(2)}, u32[]{:S(2)}) collective-permute-start(bf16[192,3072]{1,0:T(8,128)(2,1)} %collective-permute-done.24.refs_5_.refs_21_), channel_id=1, source_target_pairs={{0,1},{1,0},{2,3},{3,2},{4,5},{5,4},{6,7},{7,6},{8,9},{9,8},{10,11... | collective-permute-start | bytes 3538952 | tf_op jit(solution)/shard_map/ppermute | solution.py:431
  171.7 33.2 %collective-permute-start.32 = (bf16[192,3072]{1,0:T(8,128)(2,1)}, bf16[192,3072]{1,0:T(8,128)(2,1)}, u32[]{:S(2)}, u32[]{:S(2)}) collective-permute-start(bf16[192,3072]{1,0:T(8,128)(2,1)} %collective-permute-done.24.refs_5_.refs_21_), channel_id=1, source_target_pairs={{0,16},{16,0},{1,17},{17,1},{2,18},{18,2},{3,19},{19,3},{4,20},{20... | collective-permute-start | bytes 3538952 | tf_op jit(solution)/shard_map/ppermute | solution.py:424
  173.3 31.5 %collective-permute-start.29 = (bf16[1536,384]{1,0:T(8,128)(2,1)}, bf16[1536,384]{1,0:T(8,128)(2,1)}, u32[]{:S(2)}, u32[]{:S(2)}) collective-permute-start(bf16[1536,384]{1,0:T(8,128)(2,1)} %collective-permute-done.23.refs_16_), channel_id=1, source_target_pairs={{4,0},{8,12},{5,1},{9,13},{6,2},{10,14},{7,3},{11,15},{20,16},{24,... | collective-permute-start | bytes 3538952 | tf_op jit(solution)/shard_map/ppermute | solution.py:417
  174.6 30.2 %collective-permute-start.30 = (bf16[1536,384]{1,0:T(8,128)(2,1)}, bf16[1536,384]{1,0:T(8,128)(2,1)}, u32[]{:S(2)}, u32[]{:S(2)}) collective-permute-start(bf16[1536,384]{1,0:T(8,128)(2,1)} %collective-permute-done.22.refs_18_.refs_8_), channel_id=1, source_target_pairs={{4,8},{8,4},{5,9},{9,5},{6,10},{10,6},{7,11},{11,7},{20,24},{24,20... | collective-permute-start | bytes 3538952 | tf_op jit(solution)/shard_map/ppermute | solution.py:420
  176.5 28.4 %collective-permute-start.31 = (bf16[192,3072]{1,0:T(8,128)(2,1)}, bf16[192,3072]{1,0:T(8,128)(2,1)}, u32[]{:S(2)}, u32[]{:S(2)}) collective-permute-start(bf16[192,3072]{1,0:T(8,128)(2,1)} %collective-permute-done.19.refs_0_), channel_id=1, source_target_pairs={{0,2},{2,0},{1,3},{3,1},{4,6},{6,4},{5,7},{7,5},{8,10},{10,8},{9,1... | collective-permute-start | bytes 3538952 | tf_op jit(solution)/shard_map/ppermute | solution.py:423
  177.4 14.1 %copy-start.8 = (bf16[192,3072]{1,0:T(8,128)(2,1)}, bf16[192,3072]{1,0:T(8,128)(2,1)S(1)}, u32[]{:S(2)}) copy-start(bf16[192,3072]{1,0:T(8,128)(2,1)S(1)} %collective-permute-done.28.refs_7_.refs_23_) | copy-start | bytes 3538948
  177.4 27.5 %collective-permute-start.33 = (bf16[192,3072]{1,0:T(8,128)(2,1)}, bf16[192,3072]{1,0:T(8,128)(2,1)}, u32[]{:S(2)}, u32[]{:S(2)}) collective-permute-start(bf16[192,3072]{1,0:T(8,128)(2,1)} %collective-permute-done.19.refs_0_), channel_id=1, source_target_pairs={{0,1},{1,0},{2,3},{3,2},{4,5},{5,4},{6,7},{7,6},{8,9},{9,8},{10,11... | collective-permute-start | bytes 3538952 | tf_op jit(solution)/shard_map/ppermute | solution.py:431
  204.9 15.8 %collective-permute-start.39 = (bf16[192,3072]{1,0:T(8,128)(2,1)}, bf16[192,3072]{1,0:T(8,128)(2,1)S(1)}, u32[]{:S(2)}, u32[]{:S(2)}) collective-permute-start(bf16[192,3072]{1,0:T(8,128)(2,1)} %collective-permute-done.25.refs_1_), channel_id=1, source_target_pairs={{0,1},{1,0},{2,3},{3,2},{4,5},{5,4},{6,7},{7,6},{8,9},{9,8},{10,11... | collective-permute-start | bytes 3538952 | tf_op jit(solution)/shard_map/ppermute | solution.py:553
  205.0 18.0 %collective-permute-start.40 = (bf16[192,3072]{1,0:T(8,128)(2,1)}, bf16[192,3072]{1,0:T(8,128)(2,1)}, u32[]{:S(2)}, u32[]{:S(2)}) collective-permute-start(bf16[192,3072]{1,0:T(8,128)(2,1)} %collective-permute-done.31.refs_4_), channel_id=1, source_target_pairs={{0,1},{1,0},{2,3},{3,2},{4,5},{5,4},{6,7},{7,6},{8,9},{9,8},{10,11... | collective-permute-start | bytes 3538952 | tf_op jit(solution)/shard_map/ppermute | solution.py:553
  205.5 18.7 %collective-permute-start.41 = (bf16[192,3072]{1,0:T(8,128)(2,1)}, bf16[192,3072]{1,0:T(8,128)(2,1)}, u32[]{:S(2)}, u32[]{:S(2)}) collective-permute-start(bf16[192,3072]{1,0:T(8,128)(2,1)} %collective-permute-done.32.refs_5_), channel_id=1, source_target_pairs={{0,1},{1,0},{2,3},{3,2},{4,5},{5,4},{6,7},{7,6},{8,9},{9,8},{10,11... | collective-permute-start | bytes 3538952 | tf_op jit(solution)/shard_map/ppermute | solution.py:553
  219.3 19.7 %collective-permute-start.34 = (bf16[384,384]{1,0:T(8,128)(2,1)}, bf16[384,384]{1,0:T(8,128)(2,1)S(1)}, u32[]{:S(2)}, u32[]{:S(2)}) collective-permute-start(bf16[384,384]{1,0:T(8,128)(2,1)} %get-tuple-element.218), channel_id=1, source_target_pairs={{0,2},{2,0},{16,18},{18,16},{1,3},{3,1},{17,19},{19,17},{4,6},{6,4... | collective-permute-start | bytes 884744 | tf_op jit(solution)/shard_map/ppermute | solution.py:454
  220.2 18.8 %collective-permute-start.35 = (bf16[384,384]{1,0:T(8,128)(2,1)}, bf16[384,384]{1,0:T(8,128)(2,1)S(1)}, u32[]{:S(2)}, u32[]{:S(2)}) collective-permute-start(bf16[384,384]{1,0:T(8,128)(2,1)} %get-tuple-element.219), channel_id=1, source_target_pairs={{0,16},{2,18},{16,0},{18,2},{1,17},{3,19},{17,1},{19,3},{4,20},{6,... | collective-permute-start | bytes 884744 | tf_op jit(solution)/shard_map/ppermute | solution.py:454
  220.8 4.8 %copy-start.12 = (bf16[192,3072]{1,0:T(8,128)(2,1)}, bf16[192,3072]{1,0:T(8,128)(2,1)S(1)}, u32[]{:S(2)}) copy-start(bf16[192,3072]{1,0:T(8,128)(2,1)S(1)} %collective-permute-done.39.refs_3_) | copy-start | bytes 3538948
  220.8 18.3 %collective-permute-start.36 = (bf16[384,384]{1,0:T(8,128)(2,1)}, bf16[384,384]{1,0:T(8,128)(2,1)}, u32[]{:S(2)}, u32[]{:S(2)}) collective-permute-start(bf16[384,384]{1,0:T(8,128)(2,1)} %get-tuple-element.220), channel_id=1, source_target_pairs={{0,18},{2,16},{16,2},{18,0},{1,19},{3,17},{17,3},{19,1},{4,22},{6,... | collective-permute-start | bytes 884744 | tf_op jit(solution)/shard_map/ppermute | solution.py:454
  222.9 12.8 %collective-permute-start.37 = (bf16[384,128]{1,0:T(8,128)(2,1)}, bf16[384,128]{1,0:T(8,128)(2,1)S(1)}, u32[]{:S(2)}, u32[]{:S(2)}) collective-permute-start(bf16[384,128]{1,0:T(8,128)(2,1)} %get-tuple-element.221), channel_id=1, source_target_pairs={{4,0},{6,2},{8,12},{10,14},{20,16},{22,18},{24,28},{26,30},{5,1},{... | collective-permute-start | bytes 294920 | tf_op jit(solution)/shard_map/ppermute | solution.py:583
  224.2 12.8 %collective-permute-start.38 = (bf16[384,128]{1,0:T(8,128)(2,1)}, bf16[384,128]{1,0:T(8,128)(2,1)S(1)}, u32[]{:S(2)}, u32[]{:S(2)}) collective-permute-start(bf16[384,128]{1,0:T(8,128)(2,1)} %get-tuple-element.222), channel_id=1, source_target_pairs={{4,2},{6,0},{8,14},{10,12},{20,18},{22,16},{24,30},{26,28},{5,3},{... | collective-permute-start | bytes 294920 | tf_op jit(solution)/shard_map/ppermute | solution.py:583
  235.7 11.7 %copy-start.15 = (bf16[384,128]{1,0:T(8,128)(2,1)}, bf16[384,128]{1,0:T(8,128)(2,1)S(1)}, u32[]{:S(2)}) copy-start(bf16[384,128]{1,0:T(8,128)(2,1)S(1)} %collective-permute-done.37.refs_4_) | copy-start | bytes 294916
  235.8 10.1 %collective-permute-start.42 = (bf16[384,128]{1,0:T(8,128)(2,1)}, bf16[384,128]{1,0:T(8,128)(2,1)S(1)}, u32[]{:S(2)}, u32[]{:S(2)}) collective-permute-start(bf16[384,128]{1,0:T(8,128)(2,1)} %get-tuple-element.227), channel_id=1, source_target_pairs={{4,16},{6,18},{8,28},{10,30},{20,0},{22,2},{24,12},{26,14},{5,17},... | collective-permute-start | bytes 294920 | tf_op jit(solution)/shard_map/ppermute | solution.py:583
  237.1 10.4 %copy-start.16 = (bf16[384,128]{1,0:T(8,128)(2,1)}, bf16[384,128]{1,0:T(8,128)(2,1)S(1)}, u32[]{:S(2)}) copy-start(bf16[384,128]{1,0:T(8,128)(2,1)S(1)} %collective-permute-done.38.refs_5_) | copy-start | bytes 294916
  237.1 10.4 %collective-permute-start.43 = (bf16[384,128]{1,0:T(8,128)(2,1)}, bf16[384,128]{1,0:T(8,128)(2,1)S(1)}, u32[]{:S(2)}, u32[]{:S(2)}) collective-permute-start(bf16[384,128]{1,0:T(8,128)(2,1)} %get-tuple-element.228), channel_id=1, source_target_pairs={{4,18},{6,16},{8,30},{10,28},{20,2},{22,0},{24,14},{26,12},{5,19},... | collective-permute-start | bytes 294920 | tf_op jit(solution)/shard_map/ppermute | solution.py:583
  239.0 8.4 %copy-start.13 = (bf16[384,384]{1,0:T(8,128)(2,1)}, bf16[384,384]{1,0:T(8,128)(2,1)S(1)}, u32[]{:S(2)}) copy-start(bf16[384,384]{1,0:T(8,128)(2,1)S(1)} %collective-permute-done.34.refs_1_) | copy-start | bytes 884740
  239.0 8.4 %copy-start.14 = (bf16[384,384]{1,0:T(8,128)(2,1)}, bf16[384,384]{1,0:T(8,128)(2,1)S(1)}, u32[]{:S(2)}) copy-start(bf16[384,384]{1,0:T(8,128)(2,1)S(1)} %collective-permute-done.35.refs_2_) | copy-start | bytes 884740
  245.9 1.6 copy-start.17
  247.5 0.6 copy-start.18
where the time goes:
time: 256 us; the launch traced here: 252 us
  Pallas kernels  97.7 us (38%)
  waiting for transfers between devices  84.3 us (33%)
  starting transfers between devices  50.3 us (20%)
  other arithmetic  10 us (4%)
  local copies, waits for them, and re-layouts  8.45 us (3%)
    pallas_call x6, Pallas kernels, run_jobs(): pl.pallas_call(functools.partial(job_kernel, plan), out_shape=shapes, in_...  83.8 us
    ppermute x5, waiting for transfers between devices, pair(): return lax.ppermute(value, 'dp', [(0, 1), (1, 0), (2, 3), (3, 2)])  64.4 us
    ppermute x5, starting transfers between devices, pair(): return lax.ppermute(value, 'dp', [(0, 1), (1, 0), (2, 3), (3, 2)])  16.3 us
    pallas_call x2, Pallas kernels, normalize_part(): pl.pallas_call(normalize_kernel, out_shape=[jax.ShapeDtypeStruct((part, w...  10.8 us
    ppermute x6, starting transfers between devices, middle(): return lax.ppermute(value, 'dp', [(1, 2), (2, 1)])  9.07 us
    ppermute x4, waiting for transfers between devices, hand_back(): got.append(lax.ppermute(sent, ('groups', 'dp', 'seq'), steps))  8.4 us
    ppermute x6, starting transfers between devices, shared(): across = lambda value: lax.ppermute(value, 'groups', swap)  7.22 us
    ppermute x6, starting transfers between devices, shared(): beside = lambda value: lax.ppermute(value, 'seq', swap)  6.65 us
  transfers between devices with their start and end apart: 44, of which 12 were waited for; matrix products, arithmetic and copies ran while one was open for 5% of the time, Pallas kernels for 35%

commit v1 on v0

--- a/solution.py
+++ b/solution.py
@@ -55,10 +55,31 @@
     return lax.all_to_all(mixed, "seq", split_axis=1, concat_axis=2, tiled=True)
 
 
-def normalize_kernel(place_ref, tokens_ref, gain_ref, *normed_refs):
+def slab_order(plane):
+    inner = (plane == 1) | (plane == 2)
+    near, far = plane ^ 1, 2 - plane // 2
+    return plane, jnp.where(inner, near, far), jnp.where(inner, far, near), 3 - 3 * (plane // 2)
+
+
+def normalize_kernel(place_ref, tokens_ref, gain_ref, weight_ref, *refs):
+    normed_refs, rest = refs[:2], refs[2:]
     rows, width = tokens_ref.shape[1:]
     lanes = 128
     slab, span = width // 4, width // 2
+    step, steps = pl.program_id(0), pl.num_programs(0)
+    if rest:
+        own_ref, own_buf, own_sems = rest
+        own_in = pltpu.make_async_copy(weight_ref.at[place_ref[5]], own_buf, own_sems.at[0])
+        own_out = pltpu.make_async_copy(own_buf, own_ref, own_sems.at[1])
+
+        @pl.when(step == 0)
+        def _():
+            own_in.start()
+
+        @pl.when(step == 1)
+        def _():
+            own_in.wait()
+            own_out.start()
 
     def widened(begin):
         return tokens_ref[0, :, pl.ds(begin, lanes)].astype(jnp.float32)
@@ -80,35 +101,52 @@
             target = i * slab % span + begin
             normed_refs[i * slab // span][:, target : target + lanes] = part.astype(jnp.bfloat16)
 
-
-def normalize_part(tokens, ln_gain, part, core, order):
+    if rest:
+
+        @pl.when(step == steps - 1)
+        def _():
+            own_out.wait()
+
+
+def normalize_part(tokens, ln_gain, weight, part, core, order, head=None):
     width = tokens.shape[2]
-    step, count = 64 if part % 64 == 0 else 32, 2
+    piece = weight.shape[1:]
+    step = 64 if part % 64 == 0 else 32
     steps = part // step
-    place = jnp.stack([jnp.asarray(v, jnp.int32) for v in (core, *order)])
-    return pl.pallas_call(
+    place = [core, *order] + ([] if head is None else [head])
+    place = jnp.stack([jnp.asarray(v, jnp.int32) for v in place])
+    half = jax.ShapeDtypeStruct((part, width // 2), jnp.bfloat16)
+    anywhere = pl.BlockSpec(memory_space=pl.ANY)
+    got = pl.pallas_call(
         normalize_kernel,
-        out_shape=[jax.ShapeDtypeStruct((part, width // count), jnp.bfloat16)] * count,
+        out_shape=[half] * 2 + [jax.ShapeDtypeStruct(piece, jnp.bfloat16)] * (head is not None),
         grid_spec=pltpu.PrefetchScalarGridSpec(
             num_scalar_prefetch=1,
             grid=(steps,),
             in_specs=[
                 pl.BlockSpec((1, step, width), lambda i, place: (0, place[0] * steps + i, 0)),
                 pl.BlockSpec((1, width), lambda i, place: (0, 0)),
+                anywhere,
             ],
-            out_specs=[pl.BlockSpec((step, width // count), lambda i, place: (i, 0))] * count,
+            out_specs=[pl.BlockSpec((step, width // 2), lambda i, place: (i, 0))] * 2
+            + [anywhere] * (head is not None),
+            scratch_shapes=[pltpu.VMEM(piece, jnp.bfloat16), pltpu.SemaphoreType.DMA((2,))]
+            if head is not None
+            else [],
         ),
         compiler_params=pltpu.CompilerParams(vmem_limit_bytes=62 << 20),
         cost_estimate=pl.CostEstimate(
             flops=8 * part * width, bytes_accessed=4 * part * width, transcendentals=part
         ),
-    )(place, tokens, ln_gain[None])
+    )(place, tokens, ln_gain[None], weight)
+    return got[:2], got[2:]
 
 
 def attend_rows(projected_ref, parts, column):
     width = projected_ref.shape[1] // 3
     key_rows = projected_ref[:, width : 2 * width]
     value_rows = projected_ref[:, 2 * width :]
+    value_rows = jnp.concatenate([value_rows, jnp.ones_like(value_rows)], axis=1)
     begin = 0
     for part in parts:
         step = part.shape[0]
@@ -119,7 +157,7 @@
         highest = jnp.max(scores, axis=-1, keepdims=True)
         expo = jnp.exp2((scores - highest) * (math.log2(math.e) / math.sqrt(width)))
         mixed = jnp.dot(expo.astype(jnp.bfloat16), value_rows, preferred_element_type=jnp.float32)
-        mixed = mixed / jnp.sum(expo, axis=-1, keepdims=True)
+        mixed = mixed[:, :width] / mixed[:, width:]
         part[:, column : column + width] = mixed.astype(jnp.bfloat16)
         begin += step
 
@@ -404,9 +442,6 @@
         piece = piece.reshape(-1, part, columns).transpose(1, 0, 2)
         return piece.reshape(part, -1)
 
-    def weight_piece(weight, j):
-        return lax.dynamic_slice_in_dim(weight, group * heads + j, 1, 1)[:, 0]
-
     def pick(for_inner, for_ends):
         return jnp.where(inner, for_inner, for_ends)
 
@@ -431,13 +466,6 @@
             got.append(lax.ppermute(value, "head", swap))
         return got
 
-    beside_plane, far_inner = plane ^ 1, 2 - plane // 2
-    order = (
-        plane,
-        pick(beside_plane, far_inner),
-        pick(far_inner, beside_plane),
-        3 - 3 * (plane // 2),
-    )
     run = functools.partial(run_jobs, core, inner, seqs * rows, columns)
 
     def exchange(mixed):
@@ -455,13 +483,18 @@
                 got.append(sent)
         return got
 
-    normed = normalize_part(tokens, ln_gain, part, core, order)
-    normed, qkv_weight = wait((normed, qkv_weight))
+    weight = qkv_weight.transpose(1, 0, 2)
+    order = slab_order(plane)
+    normed, (own0,) = normalize_part(
+        tokens, ln_gain, weight, part, core, order, group * heads
+    )
+    normed, own0, later_weight = wait((normed, own0, weight))
     cut0, cut1 = normed
+    pair1, middle1 = pair(own0), middle(own0)
     beside1, across1 = beside(cut0), across(cut0)
-    own0 = weight_piece(qkv_weight, 0)
-    pair1, middle1 = pair(own0), middle(own0)
-    own1, own2 = weight_piece(qkv_weight, 1), weight_piece(qkv_weight, 2)
+    own1, own2 = [
+        lax.dynamic_index_in_dim(later_weight, group * heads + j, 0, keepdims=False) for j in (1, 2)
+    ]
     give = pick(fold(own1), cut0)
     pair1, middle1, beside1, across1, own1, own2, cut0, cut1, tokens, give = wait(
         (pair1, middle1, beside1, across1, own1, own2, cut0, cut1, tokens, give)
@@ -470,7 +503,7 @@
     pair2, middle2 = pair(give), middle(pair1)
     beside2, across2 = beside(cut1), across(cut1)
     give = pick(fold(middle1), cut1)
-    far_normed = normalize_part(tokens, ln_gain, part, 1 - core, order)
+    far_normed, _ = normalize_part(tokens, ln_gain, weight, part, 1 - core, order)
     far1 = others(beside1, across1)
     pair2, middle2, beside2, across2, across1, own1, own2, far_normed, far1, give = wait(
         (pair2, middle2, beside2, across2, across1, own1, own2, far_normed, far1, give)
@@ -560,7 +593,6 @@
         + [dict(pieces=lent0, uses=[(0, 1)], sums={0: sum4}, finish=(0,))],
         [(3, 0, [(middle6, pair6)])],
     )
-    sent = exchange((*done0[0], *done1[0]))
     lent1 = (((across4, across5), (far_across4, far_across5)), ((beside6, across6), far6))
     (lent1,) = run(
         [dict(pieces=lent1, uses=[(0, 1)] * 4, finish=(0,))], [*lent_weights, (3, 0, [middle6])]
@@ -583,6 +615,7 @@
                 got.append(lax.ppermute(sent, ("groups", "dp", "seq"), steps))
         return got
 
+    sent = exchange((*done0[0], *done1[0]))
     back = hand_back((*lent0[0], *lent1[0]))
     places = [
         (seq - b) % seqs * groups + (group - a) % groups

time: 256 us -> 253 us (0.988)
  waiting for transfers between devices: 84.3 us -> 79 us
    ppermute x5, waiting for transfers between devices: 64.4 us -> 58.2 us  [pair(): return lax.ppermute(value, 'dp', [(0, 1), (1, 0), (2, 3), (3, 2)])]
    unnamed x38 -> x35, local copies, waits for them, and re-layouts: 1.73 us -> 5.67 us
  transfers between devices with their start and end apart: 44 -> 44, of which waited for: 12 -> 12; matrix products, arithmetic and copies ran while one was open for 5% -> 7% of each run, Pallas kernels for 35% -> 36%
where the time goes in v1:
time: 253 us; the launch traced here: 248 us
  Pallas kernels  97.6 us (39%)
  waiting for transfers between devices  79 us (31%)
  starting transfers between devices  50.4 us (20%)
  local copies, waits for them, and re-layouts  10.7 us (4%)
  other arithmetic  10 us (4%)
    pallas_call x6, Pallas kernels, run_jobs(): pl.pallas_call(functools.partial(job_kernel, plan), out_shape=shapes, in_...  83.4 us
    ppermute x5, waiting for transfers between devices, pair(): return lax.ppermute(value, 'dp', [(0, 1), (1, 0), (2, 3), (3, 2)])  58.2 us
    ppermute x5, starting transfers between devices, pair(): return lax.ppermute(value, 'dp', [(0, 1), (1, 0), (2, 3), (3, 2)])  15.5 us
    pallas_call x2, Pallas kernels, normalize_part(): pl.pallas_call(normalize_kernel, out_shape=[half] * 2 + [jax.ShapeDtypeSt...  11.1 us
    ppermute x6, starting transfers between devices, middle(): return lax.ppermute(value, 'dp', [(1, 2), (2, 1)])  10 us
    ppermute x4, waiting for transfers between devices, hand_back(): got.append(lax.ppermute(sent, ('groups', 'dp', 'seq'), steps))  8.37 us
    ppermute x6, starting transfers between devices, shared(): across = lambda value: lax.ppermute(value, 'groups', swap)  7.22 us
    ppermute x6, starting transfers between devices, shared(): beside = lambda value: lax.ppermute(value, 'seq', swap)  6.59 us
  transfers between devices with their start and end apart: 44, of which 12 were waited for; matrix products, arithmetic and copies ran while one was open for 7% of the time, Pallas kernels for 36%

profile of v1, /device:TPU:0, one launch (start us, length us, event | category | flops | bytes accessed | tf_op | source)
XLA Modules:
  0.0 248.5 jit_solution(15963043642868276101)
XLA Ops:
  0.0 0.7 stack.86.place_ref
  0.7 5.7 %shard_map.37 = (bf16[192,3072]{1,0:T(8,128)(2,1)}, bf16[192,3072]{1,0:T(8,128)(2,1)}, bf16[1536,384]{1,0:T(8,128)(2,1)}) custom-call(s32[6]{0:T(128)} %stack.86.place_ref, bf16[1,384,6144]{2,1,0:T(8,128)(2,1)} %tokens_ref.2, f32[1,6144]{1,0:T(1,128)} %bitcast.41, bf16[6,1536,384]{2,1,0:T(8,128)(2,1)} %bitcast.29), custom_call_target="tpu_custom_call" | custom-call | flops 9437184 | bytes 4718592 | tf_op jit(solution)/shard_map/pallas_call | solution.py:120
  6.4 3.1 %collective-permute-start = (bf16[1536,384]{1,0:T(8,128)(2,1)}, bf16[1536,384]{1,0:T(8,128)(2,1)}, u32[]{:S(2)}, u32[]{:S(2)}) collective-permute-start(bf16[1536,384]{1,0:T(8,128)(2,1)} %get-tuple-element.124.refs_8_.refs_10_.refs_16_.refs_18_), channel_id=1, source_target_pairs={{0,4},{4,0},{8,12},{12,8},{1,5},{5,1},{9,13},{13,9},{2,6},{6,2},{1... | collective-permute-start | bytes 3538952 | tf_op jit(solution)/shard_map/ppermute | solution.py:449
  9.4 1.7 collective-permute-start.1
  11.1 1.5 collective-permute-start.2
  12.6 1.5 collective-permute-start.3
  14.1 2.9 %dynamic-slice_bitcast_fusion = (bf16[1536,384]{1,0:T(8,128)(2,1)}, bf16[1,1536,384]{2,1,0:T(8,128)(2,1)S(1)}) fusion(bf16[6,1536,384]{2,1,0:T(8,128)(2,1)} %bitcast.30, s32[]{:T(128)S(6)} %select_n.77, s32[]{:T(128)S(6)} %select_n.76), kind=kLoop, calls=%fused_computation.1 | loop fusion | bytes 4718600 | tf_op jit(solution)/shard_map/jit(dynamic_index_in_dim)/squeeze | solution.py:496
  17.3 1.5 copy-done.1
  18.7 1.2 broadcast_select_fusion.3
  19.9 15.8 %collective-permute-done.refs_15_.refs_16_.refs_23_.refs_26_ = bf16[1536,384]{1,0:T(8,128)(2,1)} collective-permute-done((bf16[1536,384]{1,0:T(8,128)(2,1)}, bf16[1536,384]{1,0:T(8,128)(2,1)}, u32[]{:S(2)}, u32[]{:S(2)}) %collective-permute-start) | collective-permute-done | bytes 1179680 | tf_op jit(solution)/shard_map/ppermute | solution.py:449
  35.7 3.0 %collective-permute-done.2.refs_4_.refs_12_ = bf16[192,3072]{1,0:T(8,128)(2,1)S(1)} collective-permute-done((bf16[192,3072]{1,0:T(8,128)(2,1)}, bf16[192,3072]{1,0:T(8,128)(2,1)S(1)}, u32[]{:S(2)}, u32[]{:S(2)}) %collective-permute-start.2) | collective-permute-done | bytes 1179680 | tf_op jit(solution)/shard_map/ppermute | solution.py:458
  38.8 1.3 collective-permute-done.3.refs_0_.refs_8_
  40.1 1.2 collective-permute-start.6
  41.3 1.5 collective-permute-start.7
  42.8 3.2 %collective-permute-start.4 = (bf16[192,3072]{1,0:T(8,128)(2,1)}, bf16[192,3072]{1,0:T(8,128)(2,1)}, u32[]{:S(2)}, u32[]{:S(2)}) collective-permute-start(bf16[192,3072]{1,0:T(8,128)(2,1)} %broadcast_select_fusion.3), channel_id=1, source_target_pairs={{0,4},{4,0},{8,12},{12,8},{1,5},{5,1},{9,13},{13,9},{2,6},{6,2},{1... | collective-permute-start | bytes 3538952 | tf_op jit(solution)/shard_map/ppermute | solution.py:449
  45.9 1.7 collective-permute-start.5
  47.6 1.0 copy-done.5
  48.7 0.6 stack.88.place_ref
  49.3 2.5 copy.8
  51.8 5.4 %shard_map.38 = (bf16[192,3072]{1,0:T(8,128)(2,1)}, bf16[192,3072]{1,0:T(8,128)(2,1)}) custom-call(s32[5]{0:T(128)} %stack.88.place_ref, bf16[1,384,6144]{2,1,0:T(8,128)(2,1)} %tokens_ref.2, f32[1,6144]{1,0:T(1,128)} %bitcast.42, bf16[6,1536,384]{2,1,0:T(8,128)(2,1)} %bitcast.31), custom_call_target="tpu_custom_call" | custom-call | flops 9437184 | bytes 4718592 | tf_op jit(solution)/shard_map/pallas_call | solution.py:120
  57.1 1.4 broadcast_select_fusion.2
  58.5 13.8 %collective-permute-done.4.refs_25_.refs_0_.refs_16_ = bf16[192,3072]{1,0:T(8,128)(2,1)} collective-permute-done((bf16[192,3072]{1,0:T(8,128)(2,1)}, bf16[192,3072]{1,0:T(8,128)(2,1)}, u32[]{:S(2)}, u32[]{:S(2)}) %collective-permute-start.4) | collective-permute-done | bytes 1179680 | tf_op jit(solution)/shard_map/ppermute | solution.py:449
  72.4 0.6 collective-permute-start.13
  73.0 3.6 %collective-permute-start.10 = (bf16[192,3072]{1,0:T(8,128)(2,1)S(1)}, bf16[192,3072]{1,0:T(8,128)(2,1)S(1)}, u32[]{:S(2)}, u32[]{:S(2)}) collective-permute-start(bf16[192,3072]{1,0:T(8,128)(2,1)S(1)} %broadcast_select_fusion.2), channel_id=1, source_target_pairs={{0,4},{4,0},{8,12},{12,8},{1,5},{5,1},{9,13},{13,9},{2,6},{6,2},{1... | collective-permute-start | bytes 3538952 | tf_op jit(solution)/shard_map/ppermute | solution.py:449
  76.6 0.7 collective-permute-start.11
  77.4 0.9 collective-permute-start.12
  78.3 1.2 broadcast_select_fusion.1
  79.5 23.4 %collective-permute-done.10.refs_28_.refs_1_.refs_17_ = bf16[192,3072]{1,0:T(8,128)(2,1)S(1)} collective-permute-done((bf16[192,3072]{1,0:T(8,128)(2,1)S(1)}, bf16[192,3072]{1,0:T(8,128)(2,1)S(1)}, u32[]{:S(2)}, u32[]{:S(2)}) %collective-permute-start.10) | collective-permute-done | bytes 1179680 | tf_op jit(solution)/shard_map/ppermute | solution.py:449
  102.9 2.6 %collective-permute-done.12.refs_4_.refs_12_ = bf16[192,3072]{1,0:T(8,128)(2,1)} collective-permute-done((bf16[192,3072]{1,0:T(8,128)(2,1)}, bf16[192,3072]{1,0:T(8,128)(2,1)}, u32[]{:S(2)}, u32[]{:S(2)}) %collective-permute-start.12) | collective-permute-done | bytes 1179680 | tf_op jit(solution)/shard_map/ppermute | solution.py:458
  105.6 0.6 pad_add_fusion.role_ref
  106.2 0.8 collective-permute-start.18
  107.1 1.5 collective-permute-start.19
  108.6 2.0 collective-permute-start.16
  110.6 2.2 collective-permute-start.17
  112.9 3.2 %pad_maximum_fusion = bf16[384,3072]{1,0:T(8,128)(2,1)} fusion(bf16[192,3072]{1,0:T(8,128)(2,1)S(1)} %collective-permute-done.10.refs_28_.refs_1_.refs_17_, bf16[192,3072]{1,0:T(8,128)(2,1)} %collective-permute-done.4.refs_25_.refs_0_.refs_16_), kind=kLoop, calls=%fused_computation | loop fusion | flops 4718592 | bytes 4718592 | tf_op jit(solution)/shard_map/concatenate | solution.py:533
  116.1 2.5 %broadcast_select_fusion = bf16[1536,384]{1,0:T(8,128)(2,1)} fusion(bf16[1536,384]{1,0:T(8,128)(2,1)S(1)} %copy-done.9, bf16[1536,384]{1,0:T(8,128)(2,1)} %get-tuple-element.206.refs_11_.refs_19_.refs_10_, pred[]{:T(512)S(6)} %or.4), kind=kLoop, calls=%fused_computation.2 | loop fusion | flops 589824 | bytes 3538945 | tf_op jit(solution)/shard_map/jit(_where)/select_n | solution.py:446
  118.6 14.9 %shard_map.39 = (bf16[384,128]{1,0:T(8,128)(2,1)}, bf16[384,128]{1,0:T(8,128)(2,1)}, f32[768,384]{1,0:T(8,128)}, f32[768,384]{1,0:T(8,128)}) custom-call(s32[2]{0:T(128)} %pad_add_fusion.role_ref, bf16[192,3072]{1,0:T(8,128)(2,1)} %get-tuple-element.122.refs_0_.refs_8_, bf16[192,3072]{1,0:T(8,128)(2,1)} %get-tuple-element.128.refs_1_.refs_9_, ...), custom_call_target="tpu_custom_call" | custom-call | flops 6341787648 | tf_op jit(solution)/shard_map/pallas_call | solution.py:359
  133.5 3.5 %collective-permute-done.16.refs_27_.refs_17_ = bf16[1536,384]{1,0:T(8,128)(2,1)} collective-permute-done((bf16[1536,384]{1,0:T(8,128)(2,1)}, bf16[1536,384]{1,0:T(8,128)(2,1)}, u32[]{:S(2)}, u32[]{:S(2)}) %collective-permute-start.16) | collective-permute-done | bytes 1179680 | tf_op jit(solution)/shard_map/ppermute | solution.py:449
  137.1 1.2 collective-permute-start.24
  138.9 3.6 %collective-permute-start.22 = (bf16[1536,384]{1,0:T(8,128)(2,1)}, bf16[1536,384]{1,0:T(8,128)(2,1)}, u32[]{:S(2)}, u32[]{:S(2)}) collective-permute-start(bf16[1536,384]{1,0:T(8,128)(2,1)} %broadcast_select_fusion), channel_id=1, source_target_pairs={{0,4},{4,0},{8,12},{12,8},{1,5},{5,1},{9,13},{13,9},{2,6},{6,2},{1... | collective-permute-start | bytes 3538952 | tf_op jit(solution)/shard_map/ppermute | solution.py:449
  142.5 1.9 collective-permute-start.23
  144.4 22.6 %shard_map.40 = (bf16[384,128]{1,0:T(8,128)(2,1)}, bf16[384,128]{1,0:T(8,128)(2,1)}, f32[768,384]{1,0:T(8,128)}, f32[768,384]{1,0:T(8,128)}, f32[768,384]{1,0:T(8,128)}, /*index=5*/f32[768,384]{1,0:T(8,128)}) custom-call(s32[2]{0:T(128)} %pad_add_fusion.role_ref, bf16[192,3072]{1,0:T(8,128)(2,1)} %collective-permute-done.3.refs_0_.refs_8_, ...), custom_call_target="tpu_custom_call" | custom-call | flops 9965666304 | tf_op jit(solution)/shard_map/pallas_call | solution.py:359
  167.1 1.7 collective-permute-done.22.refs_18_.refs_8_
  168.9 1.6 collective-permute-start.32
  170.5 1.3 collective-permute-start.29
  171.8 1.9 collective-permute-start.30
  173.7 0.9 collective-permute-start.31
  174.6 14.0 %shard_map.41 = (bf16[384,128]{1,0:T(8,128)(2,1)}, bf16[384,128]{1,0:T(8,128)(2,1)}, f32[768,384]{1,0:T(8,128)}, bf16[384,128]{1,0:T(8,128)(2,1)}, bf16[384,128]{1,0:T(8,128)(2,1)}, /*index=5*/f32[768,384]{1,0:T(8,128)}) custom-call(s32[2]{0:T(128)} %pad_add_fusion.role_ref, bf16[192,3072]{1,0:T(8,128)(2,1)} %get-tuple-element.122.refs_0_.refs_8_, ...), custom_call_target="tpu_custom_call" | custom-call | flops 3623878656 | tf_op jit(solution)/shard_map/pallas_call | solution.py:359
  188.6 8.0 %shard_map.42.refs_28_ = f32[768,384]{1,0:T(8,128)} custom-call(s32[2]{0:T(128)} %pad_add_fusion.role_ref, bf16[192,3072]{1,0:T(8,128)(2,1)} %collective-permute-done.4.refs_25_.refs_0_.refs_16_, bf16[192,3072]{1,0:T(8,128)(2,1)} %copy-done.2, bf16[384,3072]{1,0:T(8,128)(2,1)} %collective-permute-done.26.refs_2_.refs_3_.refs_18_.refs_19_, ...), custom_call_target="tpu_custom_call" | custom-call | flops 2717908992 | tf_op jit(solution)/shard_map/pallas_call | solution.py:359
  196.6 5.4 %collective-permute-done.29.refs_25_ = bf16[1536,384]{1,0:T(8,128)(2,1)} collective-permute-done((bf16[1536,384]{1,0:T(8,128)(2,1)}, bf16[1536,384]{1,0:T(8,128)(2,1)}, u32[]{:S(2)}, u32[]{:S(2)}) %collective-permute-start.29) | collective-permute-done | bytes 1179680 | tf_op jit(solution)/shard_map/ppermute | solution.py:452
  202.7 13.7 %shard_map.43 = (bf16[384,384]{1,0:T(8,128)(2,1)}, bf16[384,384]{1,0:T(8,128)(2,1)}, bf16[384,384]{1,0:T(8,128)(2,1)}, bf16[384,384]{1,0:T(8,128)(2,1)}, bf16[38...) custom-call(s32[2]{0:T(128)} %pad_add_fusion.role_ref, bf16[192,3072]{1,0:T(8,128)(2,1)} %get-tuple-element.122.refs_0_.refs_8_, ...), custom_call_target="tpu_custom_call" | custom-call | flops 2717908992 | tf_op jit(solution)/shard_map/pallas_call | solution.py:359
  216.4 0.9 collective-permute-start.34
  217.3 0.5 collective-permute-start.35
  217.8 2.1 collective-permute-start.36
  219.9 1.3 collective-permute-start.37
  221.2 1.3 collective-permute-start.38
  222.5 10.2 %shard_map.44 = (bf16[384,128]{1,0:T(8,128)(2,1)}, bf16[384,128]{1,0:T(8,128)(2,1)}) custom-call(s32[2]{0:T(128)} %pad_add_fusion.role_ref, bf16[192,3072]{1,0:T(8,128)(2,1)} %collective-permute-done.19.refs_0_, bf16[192,3072]{1,0:T(8,128)(2,1)} %collective-permute-done.25.refs_1_, bf16[192,3072]{1,0:T(8,128)(2,1)} %collective-permute-done.33.refs_2_, ...), custom_call_target="tpu_custom_call" | custom-call | flops 3623878656 | tf_op jit(solution)/shard_map/pallas_call | solution.py:359
  232.8 1.3 collective-permute-start.42
  234.1 1.3 collective-permute-start.43
  235.4 0.6 stack.78.place_ref
  236.1 6.8 %collective-permute-done.42.refs_6_ = bf16[384,128]{1,0:T(8,128)(2,1)S(1)} collective-permute-done((bf16[384,128]{1,0:T(8,128)(2,1)}, bf16[384,128]{1,0:T(8,128)(2,1)S(1)}, u32[]{:S(2)}, u32[]{:S(2)}) %collective-permute-start.42) | collective-permute-done | bytes 98336 | tf_op jit(solution)/shard_map/ppermute | solution.py:615
  242.9 1.6 collective-permute-done.43.refs_7_
  244.5 0.6 copy-done.16
  245.1 3.1 %shard_map.45 = bf16[384,1536]{1,0:T(8,128)(2,1)} custom-call(s32[5]{0:T(128)} %stack.78.place_ref, bf16[384,384]{1,0:T(8,128)(2,1)} %get-tuple-element.221.refs_0_, bf16[384,384]{1,0:T(8,128)(2,1)} %copy-done.11, bf16[384,384]{1,0:T(8,128)(2,1)} %copy-done.12, bf16[384,384]{1,0:T(8,128)(2,1)} %collective-permute-done.36.refs_3_, ...), custom_call_target="tpu_custom_call" | custom-call | bytes 2359296 | tf_op jit(solution)/shard_map/pallas_call | solution.py:420
  (79 shorter events, 2.0 us)
Async XLA Ops:
  6.4 29.4 %collective-permute-start = (bf16[1536,384]{1,0:T(8,128)(2,1)}, bf16[1536,384]{1,0:T(8,128)(2,1)}, u32[]{:S(2)}, u32[]{:S(2)}) collective-permute-start(bf16[1536,384]{1,0:T(8,128)(2,1)} %get-tuple-element.124.refs_8_.refs_10_.refs_16_.refs_18_), channel_id=1, source_target_pairs={{0,4},{4,0},{8,12},{12,8},{1,5},{5,1},{9,13},{13,9},{2,6},{6,2},{1... | collective-permute-start | bytes 3538952 | tf_op jit(solution)/shard_map/ppermute | solution.py:449
  9.4 26.3 %collective-permute-start.1 = (bf16[1536,384]{1,0:T(8,128)(2,1)}, bf16[1536,384]{1,0:T(8,128)(2,1)}, u32[]{:S(2)}, u32[]{:S(2)}) collective-permute-start(bf16[1536,384]{1,0:T(8,128)(2,1)} %get-tuple-element.124.refs_8_.refs_10_.refs_16_.refs_18_), channel_id=1, source_target_pairs={{4,8},{8,4},{5,9},{9,5},{6,10},{10,6},{7,11},{11,7},{20,24},{24,20... | collective-permute-start | bytes 3538952 | tf_op jit(solution)/shard_map/ppermute | solution.py:455
  11.1 27.6 %collective-permute-start.2 = (bf16[192,3072]{1,0:T(8,128)(2,1)}, bf16[192,3072]{1,0:T(8,128)(2,1)S(1)}, u32[]{:S(2)}, u32[]{:S(2)}) collective-permute-start(bf16[192,3072]{1,0:T(8,128)(2,1)} %get-tuple-element.122.refs_0_.refs_8_), channel_id=1, source_target_pairs={{0,2},{2,0},{1,3},{3,1},{4,6},{6,4},{5,7},{7,5},{8,10},{10,8},{9,1... | collective-permute-start | bytes 3538952 | tf_op jit(solution)/shard_map/ppermute | solution.py:458
  12.6 27.5 %collective-permute-start.3 = (bf16[192,3072]{1,0:T(8,128)(2,1)}, bf16[192,3072]{1,0:T(8,128)(2,1)}, u32[]{:S(2)}, u32[]{:S(2)}) collective-permute-start(bf16[192,3072]{1,0:T(8,128)(2,1)} %get-tuple-element.122.refs_0_.refs_8_), channel_id=1, source_target_pairs={{0,16},{16,0},{1,17},{17,1},{2,18},{18,2},{3,19},{19,3},{4,20},{20... | collective-permute-start | bytes 3538952 | tf_op jit(solution)/shard_map/ppermute | solution.py:459
  17.0 61.2 %copy-start = (bf16[1,1536,384]{2,1,0:T(8,128)(2,1)}, bf16[1,1536,384]{2,1,0:T(8,128)(2,1)S(1)}, u32[]{:S(2)}) copy-start(bf16[1,1536,384]{2,1,0:T(8,128)(2,1)S(1)} %get-tuple-element.234) | copy-start | bytes 3538948
  17.1 1.7 copy-start.1
  38.8 1.3 copy-start.4
  40.1 7.6 %collective-permute-start.8 = (bf16[192,3072]{1,0:T(8,128)(2,1)S(1)}, bf16[192,3072]{1,0:T(8,128)(2,1)S(1)}, u32[]{:S(2)}, u32[]{:S(2)}) collective-permute-start(bf16[192,3072]{1,0:T(8,128)(2,1)S(1)} %collective-permute-done.2.refs_4_.refs_12_), channel_id=1, source_target_pairs={{0,1},{1,0},{2,3},{3,2},{4,5},{5,4},{6,7},{7,6},{8,9},{9,8},{10,11... | collective-permute-start | bytes 3538952 | tf_op jit(solution)/shard_map/ppermute | solution.py:466
  40.1 32.3 %collective-permute-start.6 = (bf16[192,3072]{1,0:T(8,128)(2,1)}, bf16[192,3072]{1,0:T(8,128)(2,1)}, u32[]{:S(2)}, u32[]{:S(2)}) collective-permute-start(bf16[192,3072]{1,0:T(8,128)(2,1)} %get-tuple-element.128.refs_1_.refs_9_), channel_id=1, source_target_pairs={{0,2},{2,0},{1,3},{3,1},{4,6},{6,4},{5,7},{7,5},{8,10},{10,8},{9,1... | collective-permute-start | bytes 3538952 | tf_op jit(solution)/shard_map/ppermute | solution.py:458
  41.3 31.1 %collective-permute-start.7 = (bf16[192,3072]{1,0:T(8,128)(2,1)}, bf16[192,3072]{1,0:T(8,128)(2,1)}, u32[]{:S(2)}, u32[]{:S(2)}) collective-permute-start(bf16[192,3072]{1,0:T(8,128)(2,1)} %get-tuple-element.128.refs_1_.refs_9_), channel_id=1, source_target_pairs={{0,16},{16,0},{1,17},{17,1},{2,18},{18,2},{3,19},{19,3},{4,20},{20... | collective-permute-start | bytes 3538952 | tf_op jit(solution)/shard_map/ppermute | solution.py:459
  42.8 29.6 %collective-permute-start.4 = (bf16[192,3072]{1,0:T(8,128)(2,1)}, bf16[192,3072]{1,0:T(8,128)(2,1)}, u32[]{:S(2)}, u32[]{:S(2)}) collective-permute-start(bf16[192,3072]{1,0:T(8,128)(2,1)} %broadcast_select_fusion.3), channel_id=1, source_target_pairs={{0,4},{4,0},{8,12},{12,8},{1,5},{5,1},{9,13},{13,9},{2,6},{6,2},{1... | collective-permute-start | bytes 3538952 | tf_op jit(solution)/shard_map/ppermute | solution.py:449
  45.9 26.4 %collective-permute-start.5 = (bf16[1536,384]{1,0:T(8,128)(2,1)}, bf16[1536,384]{1,0:T(8,128)(2,1)}, u32[]{:S(2)}, u32[]{:S(2)}) collective-permute-start(bf16[1536,384]{1,0:T(8,128)(2,1)} %collective-permute-done.refs_15_.refs_16_.refs_23_.refs_26_), channel_id=1, source_target_pairs={{4,8},{8,4},{5,9},{9,5},{6,10},{10,6},{7,11},{11,7},{20,24},{24,20... | collective-permute-start | bytes 3538952 | tf_op jit(solution)/shard_map/ppermute | solution.py:455
  47.6 1.0 copy-start.5
  48.7 23.7 %collective-permute-start.9 = (bf16[192,3072]{1,0:T(8,128)(2,1)}, bf16[192,3072]{1,0:T(8,128)(2,1)}, u32[]{:S(2)}, u32[]{:S(2)}) collective-permute-start(bf16[192,3072]{1,0:T(8,128)(2,1)} %collective-permute-done.3.refs_0_.refs_8_), channel_id=1, source_target_pairs={{0,1},{1,0},{2,3},{3,2},{4,5},{5,4},{6,7},{7,6},{8,9},{9,8},{10,11... | collective-permute-start | bytes 3538952 | tf_op jit(solution)/shard_map/ppermute | solution.py:466
  72.4 5.9 %collective-permute-start.14 = (bf16[192,3072]{1,0:T(8,128)(2,1)}, bf16[192,3072]{1,0:T(8,128)(2,1)}, u32[]{:S(2)}, u32[]{:S(2)}) collective-permute-start(bf16[192,3072]{1,0:T(8,128)(2,1)} %collective-permute-done.6.refs_5_.refs_13_), channel_id=1, source_target_pairs={{0,1},{1,0},{2,3},{3,2},{4,5},{5,4},{6,7},{7,6},{8,9},{9,8},{10,11... | collective-permute-start | bytes 3538952 | tf_op jit(solution)/shard_map/ppermute | solution.py:466
  72.4 33.1 %collective-permute-start.13 = (bf16[192,3072]{1,0:T(8,128)(2,1)}, bf16[192,3072]{1,0:T(8,128)(2,1)}, u32[]{:S(2)}, u32[]{:S(2)}) collective-permute-start(bf16[192,3072]{1,0:T(8,128)(2,1)} %collective-permute-done.6.refs_5_.refs_13_), channel_id=1, source_target_pairs={{0,16},{16,0},{1,17},{17,1},{2,18},{18,2},{3,19},{19,3},{4,20},{20... | collective-permute-start | bytes 3538952 | tf_op jit(solution)/shard_map/ppermute | solution.py:459
  73.0 29.9 %collective-permute-start.10 = (bf16[192,3072]{1,0:T(8,128)(2,1)S(1)}, bf16[192,3072]{1,0:T(8,128)(2,1)S(1)}, u32[]{:S(2)}, u32[]{:S(2)}) collective-permute-start(bf16[192,3072]{1,0:T(8,128)(2,1)S(1)} %broadcast_select_fusion.2), channel_id=1, source_target_pairs={{0,4},{4,0},{8,12},{12,8},{1,5},{5,1},{9,13},{13,9},{2,6},{6,2},{1... | collective-permute-start | bytes 3538952 | tf_op jit(solution)/shard_map/ppermute | solution.py:449
  76.6 26.3 %collective-permute-start.11 = (bf16[1536,384]{1,0:T(8,128)(2,1)S(1)}, bf16[1536,384]{1,0:T(8,128)(2,1)S(1)}, u32[]{:S(2)}, u32[]{:S(2)}) collective-permute-start(bf16[1536,384]{1,0:T(8,128)(2,1)S(1)} %bitcast.33), channel_id=1, source_target_pairs={{4,8},{8,4},{5,9},{9,5},{6,10},{10,6},{7,11},{11,7},{20,24},{24,20... | collective-permute-start | bytes 3538952 | tf_op jit(solution)/shard_map/ppermute | solution.py:455
  77.4 28.1 %collective-permute-start.12 = (bf16[192,3072]{1,0:T(8,128)(2,1)}, bf16[192,3072]{1,0:T(8,128)(2,1)}, u32[]{:S(2)}, u32[]{:S(2)}) collective-permute-start(bf16[192,3072]{1,0:T(8,128)(2,1)} %collective-permute-done.3.refs_0_.refs_8_), channel_id=1, source_target_pairs={{0,2},{2,0},{1,3},{3,1},{4,6},{6,4},{5,7},{7,5},{8,10},{10,8},{9,1... | collective-permute-start | bytes 3538952 | tf_op jit(solution)/shard_map/ppermute | solution.py:458
  78.3 27.2 %collective-permute-start.15 = (bf16[192,3072]{1,0:T(8,128)(2,1)}, bf16[192,3072]{1,0:T(8,128)(2,1)}, u32[]{:S(2)}, u32[]{:S(2)}) collective-permute-start(bf16[192,3072]{1,0:T(8,128)(2,1)} %collective-permute-done.7.refs_1_.refs_9_), channel_id=1, source_target_pairs={{0,1},{1,0},{2,3},{3,2},{4,5},{5,4},{6,7},{7,6},{8,9},{9,8},{10,11... | collective-permute-start | bytes 3538952 | tf_op jit(solution)/shard_map/ppermute | solution.py:466
  102.9 13.2 %copy-start.2 = (bf16[192,3072]{1,0:T(8,128)(2,1)}, bf16[192,3072]{1,0:T(8,128)(2,1)S(1)}, u32[]{:S(2)}) copy-start(bf16[192,3072]{1,0:T(8,128)(2,1)S(1)} %collective-permute-done.10.refs_28_.refs_1_.refs_17_) | copy-start | bytes 3538948
  102.9 2.6 %copy-start.8 = (bf16[1536,384]{1,0:T(8,128)(2,1)}, bf16[1536,384]{1,0:T(8,128)(2,1)S(1)}, u32[]{:S(2)}) copy-start(bf16[1536,384]{1,0:T(8,128)(2,1)S(1)} %collective-permute-done.11.refs_14_.refs_22_) | copy-start | bytes 3538948
  105.5 7.3 %collective-permute-start.20 = (bf16[192,3072]{1,0:T(8,128)(2,1)}, bf16[192,3072]{1,0:T(8,128)(2,1)S(1)}, u32[]{:S(2)}, u32[]{:S(2)}) collective-permute-start(bf16[192,3072]{1,0:T(8,128)(2,1)} %collective-permute-done.12.refs_4_.refs_12_), channel_id=1, source_target_pairs={{0,1},{1,0},{2,3},{3,2},{4,5},{5,4},{6,7},{7,6},{8,9},{9,8},{10,11... | collective-permute-start | bytes 3538952 | tf_op jit(solution)/shard_map/ppermute | solution.py:466
  106.2 9.9 %copy-start.9 = (bf16[1536,384]{1,0:T(8,128)(2,1)S(1)}, bf16[1536,384]{1,0:T(8,128)(2,1)}, u32[]{:S(2)}) copy-start(bf16[1536,384]{1,0:T(8,128)(2,1)} %copy-done.8) | copy-start | bytes 3538948
  106.2 30.8 %collective-permute-start.18 = (bf16[192,3072]{1,0:T(8,128)(2,1)}, bf16[192,3072]{1,0:T(8,128)(2,1)}, u32[]{:S(2)}, u32[]{:S(2)}) collective-permute-start(bf16[192,3072]{1,0:T(8,128)(2,1)} %collective-permute-done.4.refs_25_.refs_0_.refs_16_), channel_id=1, source_target_pairs={{0,2},{2,0},{1,3},{3,1},{4,6},{6,4},{5,7},{7,5},{8,10},{10,8},{9,1... | collective-permute-start | bytes 3538952 | tf_op jit(solution)/shard_map/ppermute | solution.py:458
  107.1 29.9 %collective-permute-start.19 = (bf16[192,3072]{1,0:T(8,128)(2,1)}, bf16[192,3072]{1,0:T(8,128)(2,1)}, u32[]{:S(2)}, u32[]{:S(2)}) collective-permute-start(bf16[192,3072]{1,0:T(8,128)(2,1)} %collective-permute-done.4.refs_25_.refs_0_.refs_16_), channel_id=1, source_target_pairs={{0,16},{16,0},{1,17},{17,1},{2,18},{18,2},{3,19},{19,3},{4,20},{20... | collective-permute-start | bytes 3538952 | tf_op jit(solution)/shard_map/ppermute | solution.py:459
  108.6 28.4 %collective-permute-start.16 = (bf16[1536,384]{1,0:T(8,128)(2,1)}, bf16[1536,384]{1,0:T(8,128)(2,1)}, u32[]{:S(2)}, u32[]{:S(2)}) collective-permute-start(bf16[1536,384]{1,0:T(8,128)(2,1)} %broadcast_select_fusion.1), channel_id=1, source_target_pairs={{0,4},{4,0},{8,12},{12,8},{1,5},{5,1},{9,13},{13,9},{2,6},{6,2},{1... | collective-permute-start | bytes 3538952 | tf_op jit(solution)/shard_map/ppermute | solution.py:449
  110.6 26.4 %collective-permute-start.17 = (bf16[1536,384]{1,0:T(8,128)(2,1)}, bf16[1536,384]{1,0:T(8,128)(2,1)}, u32[]{:S(2)}, u32[]{:S(2)}) collective-permute-start(bf16[1536,384]{1,0:T(8,128)(2,1)} %get-tuple-element.206.refs_11_.refs_19_.refs_10_), channel_id=1, source_target_pairs={{4,8},{8,4},{5,9},{9,5},{6,10},{10,6},{7,11},{11,7},{20,24},{24,20... | collective-permute-start | bytes 3538952 | tf_op jit(solution)/shard_map/ppermute | solution.py:455
  112.8 3.2 %copy-start.6 = (bf16[192,3072]{1,0:T(8,128)(2,1)}, bf16[192,3072]{1,0:T(8,128)(2,1)S(1)}, u32[]{:S(2)}) copy-start(bf16[192,3072]{1,0:T(8,128)(2,1)S(1)} %collective-permute-done.20.refs_6_.refs_14_) | copy-start | bytes 3538948
  112.9 24.2 %collective-permute-start.21 = (bf16[192,3072]{1,0:T(8,128)(2,1)}, bf16[192,3072]{1,0:T(8,128)(2,1)}, u32[]{:S(2)}, u32[]{:S(2)}) collective-permute-start(bf16[192,3072]{1,0:T(8,128)(2,1)} %collective-permute-done.13.refs_5_.refs_13_), channel_id=1, source_target_pairs={{0,1},{1,0},{2,3},{3,2},{4,5},{5,4},{6,7},{7,6},{8,9},{9,8},{10,11... | collective-permute-start | bytes 3538952 | tf_op jit(solution)/shard_map/ppermute | solution.py:466
  118.6 18.5 %copy-start.3 = (bf16[192,3072]{1,0:T(8,128)(2,1)S(1)}, bf16[192,3072]{1,0:T(8,128)(2,1)}, u32[]{:S(2)}) copy-start(bf16[192,3072]{1,0:T(8,128)(2,1)} %copy-done.2) | copy-start | bytes 3538948
  137.0 7.3 %collective-permute-start.26 = (bf16[384,3072]{1,0:T(8,128)(2,1)}, bf16[384,3072]{1,0:T(8,128)(2,1)}, u32[]{:S(2)}, u32[]{:S(2)}) collective-permute-start(bf16[384,3072]{1,0:T(8,128)(2,1)} %pad_maximum_fusion), channel_id=1, source_target_pairs={{0,1},{1,0},{2,3},{3,2},{4,5},{5,4},{6,7},{7,6},{8,9},{9,8},{10,11... | collective-permute-start | bytes 7077896 | tf_op jit(solution)/shard_map/ppermute | solution.py:466
  137.1 31.7 %collective-permute-start.24 = (bf16[192,3072]{1,0:T(8,128)(2,1)S(1)}, bf16[192,3072]{1,0:T(8,128)(2,1)}, u32[]{:S(2)}, u32[]{:S(2)}) collective-permute-start(bf16[192,3072]{1,0:T(8,128)(2,1)S(1)} %copy-done.3), channel_id=1, source_target_pairs={{0,2},{2,0},{1,3},{3,1},{4,6},{6,4},{5,7},{7,5},{8,10},{10,8},{9,1... | collective-permute-start | bytes 3538952 | tf_op jit(solution)/shard_map/ppermute | solution.py:458
  138.4 30.5 %collective-permute-start.25 = (bf16[192,3072]{1,0:T(8,128)(2,1)S(1)}, bf16[192,3072]{1,0:T(8,128)(2,1)}, u32[]{:S(2)}, u32[]{:S(2)}) collective-permute-start(bf16[192,3072]{1,0:T(8,128)(2,1)S(1)} %copy-done.3), channel_id=1, source_target_pairs={{0,16},{16,0},{1,17},{17,1},{2,18},{18,2},{3,19},{19,3},{4,20},{20... | collective-permute-start | bytes 3538952 | tf_op jit(solution)/shard_map/ppermute | solution.py:459
  138.9 29.9 %collective-permute-start.22 = (bf16[1536,384]{1,0:T(8,128)(2,1)}, bf16[1536,384]{1,0:T(8,128)(2,1)}, u32[]{:S(2)}, u32[]{:S(2)}) collective-permute-start(bf16[1536,384]{1,0:T(8,128)(2,1)} %broadcast_select_fusion), channel_id=1, source_target_pairs={{0,4},{4,0},{8,12},{12,8},{1,5},{5,1},{9,13},{13,9},{2,6},{6,2},{1... | collective-permute-start | bytes 3538952 | tf_op jit(solution)/shard_map/ppermute | solution.py:449
  142.5 26.3 %collective-permute-start.23 = (bf16[1536,384]{1,0:T(8,128)(2,1)}, bf16[1536,384]{1,0:T(8,128)(2,1)}, u32[]{:S(2)}, u32[]{:S(2)}) collective-permute-start(bf16[1536,384]{1,0:T(8,128)(2,1)} %collective-permute-done.16.refs_27_.refs_17_), channel_id=1, source_target_pairs={{4,8},{8,4},{5,9},{9,5},{6,10},{10,6},{7,11},{11,7},{20,24},{24,20... | collective-permute-start | bytes 3538952 | tf_op jit(solution)/shard_map/ppermute | solution.py:455
  144.4 24.5 %collective-permute-start.27 = (bf16[192,3072]{1,0:T(8,128)(2,1)}, bf16[192,3072]{1,0:T(8,128)(2,1)}, u32[]{:S(2)}, u32[]{:S(2)}) collective-permute-start(bf16[192,3072]{1,0:T(8,128)(2,1)} %collective-permute-done.18.refs_4_.refs_20_), channel_id=1, source_target_pairs={{0,1},{1,0},{2,3},{3,2},{4,5},{5,4},{6,7},{7,6},{8,9},{9,8},{10,11... | collective-permute-start | bytes 3538952 | tf_op jit(solution)/shard_map/ppermute | solution.py:466
  168.8 5.8 %collective-permute-start.28 = (bf16[192,3072]{1,0:T(8,128)(2,1)}, bf16[192,3072]{1,0:T(8,128)(2,1)S(1)}, u32[]{:S(2)}, u32[]{:S(2)}) collective-permute-start(bf16[192,3072]{1,0:T(8,128)(2,1)} %collective-permute-done.24.refs_5_.refs_21_), channel_id=1, source_target_pairs={{0,1},{1,0},{2,3},{3,2},{4,5},{5,4},{6,7},{7,6},{8,9},{9,8},{10,11... | collective-permute-start | bytes 3538952 | tf_op jit(solution)/shard_map/ppermute | solution.py:466
  168.9 33.2 %collective-permute-start.32 = (bf16[192,3072]{1,0:T(8,128)(2,1)}, bf16[192,3072]{1,0:T(8,128)(2,1)}, u32[]{:S(2)}, u32[]{:S(2)}) collective-permute-start(bf16[192,3072]{1,0:T(8,128)(2,1)} %collective-permute-done.24.refs_5_.refs_21_), channel_id=1, source_target_pairs={{0,16},{16,0},{1,17},{17,1},{2,18},{18,2},{3,19},{19,3},{4,20},{20... | collective-permute-start | bytes 3538952 | tf_op jit(solution)/shard_map/ppermute | solution.py:459
  170.5 31.5 %collective-permute-start.29 = (bf16[1536,384]{1,0:T(8,128)(2,1)}, bf16[1536,384]{1,0:T(8,128)(2,1)}, u32[]{:S(2)}, u32[]{:S(2)}) collective-permute-start(bf16[1536,384]{1,0:T(8,128)(2,1)} %collective-permute-done.23.refs_16_), channel_id=1, source_target_pairs={{4,0},{8,12},{5,1},{9,13},{6,2},{10,14},{7,3},{11,15},{20,16},{24,... | collective-permute-start | bytes 3538952 | tf_op jit(solution)/shard_map/ppermute | solution.py:452
  171.8 30.2 %collective-permute-start.30 = (bf16[1536,384]{1,0:T(8,128)(2,1)}, bf16[1536,384]{1,0:T(8,128)(2,1)}, u32[]{:S(2)}, u32[]{:S(2)}) collective-permute-start(bf16[1536,384]{1,0:T(8,128)(2,1)} %collective-permute-done.22.refs_18_.refs_8_), channel_id=1, source_target_pairs={{4,8},{8,4},{5,9},{9,5},{6,10},{10,6},{7,11},{11,7},{20,24},{24,20... | collective-permute-start | bytes 3538952 | tf_op jit(solution)/shard_map/ppermute | solution.py:455
  173.7 28.4 %collective-permute-start.31 = (bf16[192,3072]{1,0:T(8,128)(2,1)}, bf16[192,3072]{1,0:T(8,128)(2,1)}, u32[]{:S(2)}, u32[]{:S(2)}) collective-permute-start(bf16[192,3072]{1,0:T(8,128)(2,1)} %collective-permute-done.19.refs_0_), channel_id=1, source_target_pairs={{0,2},{2,0},{1,3},{3,1},{4,6},{6,4},{5,7},{7,5},{8,10},{10,8},{9,1... | collective-permute-start | bytes 3538952 | tf_op jit(solution)/shard_map/ppermute | solution.py:458
  174.6 14.0 %copy-start.7 = (bf16[192,3072]{1,0:T(8,128)(2,1)}, bf16[192,3072]{1,0:T(8,128)(2,1)S(1)}, u32[]{:S(2)}) copy-start(bf16[192,3072]{1,0:T(8,128)(2,1)S(1)} %collective-permute-done.28.refs_7_.refs_23_) | copy-start | bytes 3538948
  174.6 27.5 %collective-permute-start.33 = (bf16[192,3072]{1,0:T(8,128)(2,1)}, bf16[192,3072]{1,0:T(8,128)(2,1)}, u32[]{:S(2)}, u32[]{:S(2)}) collective-permute-start(bf16[192,3072]{1,0:T(8,128)(2,1)} %collective-permute-done.19.refs_0_), channel_id=1, source_target_pairs={{0,1},{1,0},{2,3},{3,2},{4,5},{5,4},{6,7},{7,6},{8,9},{9,8},{10,11... | collective-permute-start | bytes 3538952 | tf_op jit(solution)/shard_map/ppermute | solution.py:466
  202.1 15.7 %collective-permute-start.39 = (bf16[192,3072]{1,0:T(8,128)(2,1)}, bf16[192,3072]{1,0:T(8,128)(2,1)S(1)}, u32[]{:S(2)}, u32[]{:S(2)}) collective-permute-start(bf16[192,3072]{1,0:T(8,128)(2,1)} %collective-permute-done.25.refs_1_), channel_id=1, source_target_pairs={{0,1},{1,0},{2,3},{3,2},{4,5},{5,4},{6,7},{7,6},{8,9},{9,8},{10,11... | collective-permute-start | bytes 3538952 | tf_op jit(solution)/shard_map/ppermute | solution.py:586
  202.1 17.8 %collective-permute-start.40 = (bf16[192,3072]{1,0:T(8,128)(2,1)}, bf16[192,3072]{1,0:T(8,128)(2,1)}, u32[]{:S(2)}, u32[]{:S(2)}) collective-permute-start(bf16[192,3072]{1,0:T(8,128)(2,1)} %collective-permute-done.31.refs_4_), channel_id=1, source_target_pairs={{0,1},{1,0},{2,3},{3,2},{4,5},{5,4},{6,7},{7,6},{8,9},{9,8},{10,11... | collective-permute-start | bytes 3538952 | tf_op jit(solution)/shard_map/ppermute | solution.py:586
  202.6 18.6 %collective-permute-start.41 = (bf16[192,3072]{1,0:T(8,128)(2,1)}, bf16[192,3072]{1,0:T(8,128)(2,1)}, u32[]{:S(2)}, u32[]{:S(2)}) collective-permute-start(bf16[192,3072]{1,0:T(8,128)(2,1)} %collective-permute-done.32.refs_5_), channel_id=1, source_target_pairs={{0,1},{1,0},{2,3},{3,2},{4,5},{5,4},{6,7},{7,6},{8,9},{9,8},{10,11... | collective-permute-start | bytes 3538952 | tf_op jit(solution)/shard_map/ppermute | solution.py:586
  216.4 19.7 %collective-permute-start.34 = (bf16[384,384]{1,0:T(8,128)(2,1)}, bf16[384,384]{1,0:T(8,128)(2,1)S(1)}, u32[]{:S(2)}, u32[]{:S(2)}) collective-permute-start(bf16[384,384]{1,0:T(8,128)(2,1)} %get-tuple-element.222), channel_id=1, source_target_pairs={{0,2},{2,0},{16,18},{18,16},{1,3},{3,1},{17,19},{19,17},{4,6},{6,4... | collective-permute-start | bytes 884744 | tf_op jit(solution)/shard_map/ppermute | solution.py:482
  217.3 18.8 %collective-permute-start.35 = (bf16[384,384]{1,0:T(8,128)(2,1)}, bf16[384,384]{1,0:T(8,128)(2,1)S(1)}, u32[]{:S(2)}, u32[]{:S(2)}) collective-permute-start(bf16[384,384]{1,0:T(8,128)(2,1)} %get-tuple-element.223), channel_id=1, source_target_pairs={{0,16},{2,18},{16,0},{18,2},{1,17},{3,19},{17,1},{19,3},{4,20},{6,... | collective-permute-start | bytes 884744 | tf_op jit(solution)/shard_map/ppermute | solution.py:482
  217.8 4.7 %copy-start.10 = (bf16[192,3072]{1,0:T(8,128)(2,1)}, bf16[192,3072]{1,0:T(8,128)(2,1)S(1)}, u32[]{:S(2)}) copy-start(bf16[192,3072]{1,0:T(8,128)(2,1)S(1)} %collective-permute-done.39.refs_3_) | copy-start | bytes 3538948
  217.8 18.3 %collective-permute-start.36 = (bf16[384,384]{1,0:T(8,128)(2,1)}, bf16[384,384]{1,0:T(8,128)(2,1)}, u32[]{:S(2)}, u32[]{:S(2)}) collective-permute-start(bf16[384,384]{1,0:T(8,128)(2,1)} %get-tuple-element.224), channel_id=1, source_target_pairs={{0,18},{2,16},{16,2},{18,0},{1,19},{3,17},{17,3},{19,1},{4,22},{6,... | collective-permute-start | bytes 884744 | tf_op jit(solution)/shard_map/ppermute | solution.py:482
  219.9 12.8 %collective-permute-start.37 = (bf16[384,128]{1,0:T(8,128)(2,1)}, bf16[384,128]{1,0:T(8,128)(2,1)S(1)}, u32[]{:S(2)}, u32[]{:S(2)}) collective-permute-start(bf16[384,128]{1,0:T(8,128)(2,1)} %get-tuple-element.225), channel_id=1, source_target_pairs={{4,0},{6,2},{8,12},{10,14},{20,16},{22,18},{24,28},{26,30},{5,1},{... | collective-permute-start | bytes 294920 | tf_op jit(solution)/shard_map/ppermute | solution.py:615
  221.2 12.8 %collective-permute-start.38 = (bf16[384,128]{1,0:T(8,128)(2,1)}, bf16[384,128]{1,0:T(8,128)(2,1)S(1)}, u32[]{:S(2)}, u32[]{:S(2)}) collective-permute-start(bf16[384,128]{1,0:T(8,128)(2,1)} %get-tuple-element.226), channel_id=1, source_target_pairs={{4,2},{6,0},{8,14},{10,12},{20,18},{22,16},{24,30},{26,28},{5,3},{... | collective-permute-start | bytes 294920 | tf_op jit(solution)/shard_map/ppermute | solution.py:615
  232.7 11.7 %copy-start.13 = (bf16[384,128]{1,0:T(8,128)(2,1)}, bf16[384,128]{1,0:T(8,128)(2,1)S(1)}, u32[]{:S(2)}) copy-start(bf16[384,128]{1,0:T(8,128)(2,1)S(1)} %collective-permute-done.37.refs_4_) | copy-start | bytes 294916
  232.8 10.1 %collective-permute-start.42 = (bf16[384,128]{1,0:T(8,128)(2,1)}, bf16[384,128]{1,0:T(8,128)(2,1)S(1)}, u32[]{:S(2)}, u32[]{:S(2)}) collective-permute-start(bf16[384,128]{1,0:T(8,128)(2,1)} %get-tuple-element.231), channel_id=1, source_target_pairs={{4,16},{6,18},{8,28},{10,30},{20,0},{22,2},{24,12},{26,14},{5,17},... | collective-permute-start | bytes 294920 | tf_op jit(solution)/shard_map/ppermute | solution.py:615
  234.1 10.4 %copy-start.14 = (bf16[384,128]{1,0:T(8,128)(2,1)}, bf16[384,128]{1,0:T(8,128)(2,1)S(1)}, u32[]{:S(2)}) copy-start(bf16[384,128]{1,0:T(8,128)(2,1)S(1)} %collective-permute-done.38.refs_5_) | copy-start | bytes 294916
  234.1 10.4 %collective-permute-start.43 = (bf16[384,128]{1,0:T(8,128)(2,1)}, bf16[384,128]{1,0:T(8,128)(2,1)S(1)}, u32[]{:S(2)}, u32[]{:S(2)}) collective-permute-start(bf16[384,128]{1,0:T(8,128)(2,1)} %get-tuple-element.232), channel_id=1, source_target_pairs={{4,18},{6,16},{8,30},{10,28},{20,2},{22,0},{24,14},{26,12},{5,19},... | collective-permute-start | bytes 294920 | tf_op jit(solution)/shard_map/ppermute | solution.py:615
  236.1 8.4 %copy-start.11 = (bf16[384,384]{1,0:T(8,128)(2,1)}, bf16[384,384]{1,0:T(8,128)(2,1)S(1)}, u32[]{:S(2)}) copy-start(bf16[384,384]{1,0:T(8,128)(2,1)S(1)} %collective-permute-done.34.refs_1_) | copy-start | bytes 884740
  236.1 8.4 %copy-start.12 = (bf16[384,384]{1,0:T(8,128)(2,1)}, bf16[384,384]{1,0:T(8,128)(2,1)S(1)}, u32[]{:S(2)}) copy-start(bf16[384,384]{1,0:T(8,128)(2,1)S(1)} %collective-permute-done.35.refs_2_) | copy-start | bytes 884740
  242.9 1.6 copy-start.15
  244.5 0.6 copy-start.16

commit v2 on v1

--- a/solution.py
+++ b/solution.py
@@ -185,7 +185,7 @@
     token_sems, weight_sems, sum_sems, out_sems, carry_sems = take(5)
     core, inner = role_ref[0], role_ref[1]
     slab = pieces[0][0][0][0].shape[1] // 2
-    tokens, wide = projected_ref.shape
+    tokens, wide = projected_ref.shape[1:]
     part = tokens // 4
 
     def features(i, n):
@@ -273,7 +273,7 @@
         start_stage(*stage)
     for copy in carry_copies():
         copy.start()
-    ready = set()
+    ready, waiting = set(), []
     for index, (i, n) in enumerate(stages):
         low, high = plan.uses[i][n]
         pltpu.make_async_copy(features(i, n), features(i, n), token_sems.at[i, n]).wait()
@@ -296,12 +296,17 @@
             if n != mine[0] or j in plan.added[i]:
                 value += total(i, j)[...]
             if n == mine[-1] and j in plan.finished[i]:
-                projected_ref[...] = value.astype(jnp.bfloat16)
-                attend_rows(projected_ref, outs[i][j], plan.carried[i] * wide // 3)
+                projected_ref[i % 2] = value.astype(jnp.bfloat16)
+                if waiting:
+                    attend_rows(*waiting.pop())
+                column = plan.carried[i] * wide // 3
+                waiting.append((projected_ref.at[i % 2], outs[i][j], column))
                 continue
             total(i, j)[...] = value
             if n == mine[-1]:
                 out_copy(i, j).start()
+    if waiting:
+        attend_rows(*waiting.pop())
     for copy in carry_copies():
         copy.wait()
     for i in images:
@@ -310,7 +315,7 @@
                 out_copy(i, j).wait()
 
 
-def run_jobs(core, inner, tokens, wide, images, weights):
+def run_jobs(role, tokens, wide, images, weights):
     images = [
         dict(
             image,
@@ -365,7 +370,7 @@
             pltpu.VMEM((total, depth), jnp.bfloat16),
             pltpu.VMEM((depth, jobs * wide), jnp.bfloat16),
             pltpu.VMEM((total, jobs * wide), jnp.float32),
-            pltpu.VMEM((tokens, wide), jnp.bfloat16),
+            pltpu.VMEM((2, tokens, wide), jnp.bfloat16),
             pltpu.SemaphoreType.DMA((count, len(weights))),
             pltpu.SemaphoreType.DMA((len(weights), jobs)),
             pltpu.SemaphoreType.DMA((count, jobs)),
@@ -376,7 +381,7 @@
         cost_estimate=pl.CostEstimate(
             flops=2 * tokens * slab * wide * added, bytes_accessed=0, transcendentals=0
         ),
-    )(jnp.stack([core, inner]).astype(jnp.int32), *operands)
+    )(role, *operands)
     got = list(got)
     return [
         {
@@ -466,7 +471,6 @@
             got.append(lax.ppermute(value, "head", swap))
         return got
 
-    run = functools.partial(run_jobs, core, inner, seqs * rows, columns)
 
     def exchange(mixed):
         got = []
@@ -496,9 +500,12 @@
         lax.dynamic_index_in_dim(later_weight, group * heads + j, 0, keepdims=False) for j in (1, 2)
     ]
     give = pick(fold(own1), cut0)
-    pair1, middle1, beside1, across1, own1, own2, cut0, cut1, tokens, give = wait(
-        (pair1, middle1, beside1, across1, own1, own2, cut0, cut1, tokens, give)
-    )
+    role = jnp.stack([core, inner]).astype(jnp.int32)
+    beside1, across1, own1, own2, cut1, tokens, give, role = wait(
+        (beside1, across1, own1, own2, cut1, tokens, give, role)
+    )
+    pair1, middle1, give = wait((pair1, middle1, give))
+    run = functools.partial(run_jobs, role, seqs * rows, columns)
 
     pair2, middle2 = pair(give), middle(pair1)
     beside2, across2 = beside(cut1), across(cut1)

time: 253 us -> 249 us (0.984)
  waiting for transfers between devices: 79 us -> 74.8 us
  Pallas kernels: 97.6 us -> 94.9 us
    ppermute x5, waiting for transfers between devices: 58.2 us -> 41.4 us  [pair(): return lax.ppermute(value, 'dp', [(0, 1), (1, 0), (2, 3), (3, 2)])]
    ppermute x6, waiting for transfers between devices: 5.69 us -> 17.6 us  [shared(): beside = lambda value: lax.ppermute(value, 'seq', swap)]
    pallas_call x6, Pallas kernels: 83.4 us -> 80.7 us  [run_jobs(): pl.pallas_call(functools.partial(job_kernel, plan), out_shape=shapes, in_...]
    unnamed x35 -> x37, local copies, waits for them, and re-layouts: 5.67 us -> 7.73 us
  transfers between devices with their start and end apart: 44 -> 44, of which waited for: 12 -> 11; matrix products, arithmetic and copies ran while one was open for 7% -> 7% of each run, Pallas kernels for 36% -> 35%
where the time goes in v2:
time: 249 us; the launch traced here: 245 us
  Pallas kernels  94.9 us (38%)
  waiting for transfers between devices  74.8 us (30%)
  starting transfers between devices  52 us (21%)
  local copies, waits for them, and re-layouts  12.8 us (5%)
  other arithmetic  9.68 us (4%)
    pallas_call x6, Pallas kernels, run_jobs(): pl.pallas_call(functools.partial(job_kernel, plan), out_shape=shapes, in_...  80.7 us
    ppermute x5, waiting for transfers between devices, pair(): return lax.ppermute(value, 'dp', [(0, 1), (1, 0), (2, 3), (3, 2)])  41.4 us
    ppermute x6, waiting for transfers between devices, shared(): beside = lambda value: lax.ppermute(value, 'seq', swap)  17.6 us
    ppermute x5, starting transfers between devices, pair(): return lax.ppermute(value, 'dp', [(0, 1), (1, 0), (2, 3), (3, 2)])  15.8 us
    pallas_call x2, Pallas kernels, normalize_part(): pl.pallas_call(normalize_kernel, out_shape=[half] * 2 + [jax.ShapeDtypeSt...  11.1 us
    ppermute x6, starting transfers between devices, middle(): return lax.ppermute(value, 'dp', [(1, 2), (2, 1)])  9.99 us
    ppermute x6, starting transfers between devices, shared(): beside = lambda value: lax.ppermute(value, 'seq', swap)  8.09 us
    ppermute x4, waiting for transfers between devices, hand_back(): got.append(lax.ppermute(sent, ('groups', 'dp', 'seq'), steps))  7.8 us
  transfers between devices with their start and end apart: 44, of which 11 were waited for; matrix products, arithmetic and copies ran while one was open for 7% of the time, Pallas kernels for 35%

profile of v2, /device:TPU:0, one launch (start us, length us, event | category | flops | bytes accessed | tf_op | source)
XLA Modules:
  0.0 244.9 jit_solution(4653325134079027355)
XLA Ops:
  0.0 0.7 stack.70.place_ref
  0.7 5.7 %shard_map.37 = (bf16[192,3072]{1,0:T(8,128)(2,1)}, bf16[192,3072]{1,0:T(8,128)(2,1)}, bf16[1536,384]{1,0:T(8,128)(2,1)}) custom-call(s32[6]{0:T(128)} %stack.70.place_ref, bf16[1,384,6144]{2,1,0:T(8,128)(2,1)} %tokens_ref.2, f32[1,6144]{1,0:T(1,128)} %bitcast.41, bf16[6,1536,384]{2,1,0:T(8,128)(2,1)} %bitcast.29), custom_call_target="tpu_custom_call" | custom-call | flops 9437184 | bytes 4718592 | tf_op jit(solution)/shard_map/pallas_call | solution.py:120
  6.4 3.0 %collective-permute-start = (bf16[192,3072]{1,0:T(8,128)(2,1)}, bf16[192,3072]{1,0:T(8,128)(2,1)S(1)}, u32[]{:S(2)}, u32[]{:S(2)}) collective-permute-start(bf16[192,3072]{1,0:T(8,128)(2,1)} %get-tuple-element.124.refs_0_.refs_8_), channel_id=1, source_target_pairs={{0,2},{2,0},{1,3},{3,1},{4,6},{6,4},{5,7},{7,5},{8,10},{10,8},{9,1... | collective-permute-start | bytes 3538952 | tf_op jit(solution)/shard_map/ppermute | solution.py:463
  9.4 1.5 collective-permute-start.1
  10.9 1.6 collective-permute-start.2
  12.5 1.7 collective-permute-start.3
  14.1 2.9 %dynamic-slice_bitcast_fusion = (bf16[1536,384]{1,0:T(8,128)(2,1)}, bf16[1,1536,384]{2,1,0:T(8,128)(2,1)S(1)}) fusion(bf16[6,1536,384]{2,1,0:T(8,128)(2,1)} %bitcast.30, s32[]{:T(128)S(6)} %select_n.77, s32[]{:T(128)S(6)} %select_n.76), kind=kLoop, calls=%fused_computation.1 | loop fusion | bytes 4718600 | tf_op jit(solution)/shard_map/jit(dynamic_index_in_dim)/squeeze | solution.py:500
  17.2 1.5 copy-done.1
  18.7 1.2 broadcast_select_fusion.3
  19.9 0.6 pad_add_fusion.role_ref
  20.5 15.0 %collective-permute-done.refs_4_.refs_12_ = bf16[192,3072]{1,0:T(8,128)(2,1)S(1)} collective-permute-done((bf16[192,3072]{1,0:T(8,128)(2,1)}, bf16[192,3072]{1,0:T(8,128)(2,1)S(1)}, u32[]{:S(2)}, u32[]{:S(2)}) %collective-permute-start) | collective-permute-done | bytes 1179680 | tf_op jit(solution)/shard_map/ppermute | solution.py:463
  35.5 1.6 collective-permute-done.1.refs_0_.refs_8_
  37.1 1.2 collective-permute-start.6
  38.3 1.5 collective-permute-start.7
  39.8 3.1 %collective-permute-start.4 = (bf16[192,3072]{1,0:T(8,128)(2,1)}, bf16[192,3072]{1,0:T(8,128)(2,1)}, u32[]{:S(2)}, u32[]{:S(2)}) collective-permute-start(bf16[192,3072]{1,0:T(8,128)(2,1)} %broadcast_select_fusion.3), channel_id=1, source_target_pairs={{0,4},{4,0},{8,12},{12,8},{1,5},{5,1},{9,13},{13,9},{2,6},{6,2},{1... | collective-permute-start | bytes 3538952 | tf_op jit(solution)/shard_map/ppermute | solution.py:454
  42.9 1.7 collective-permute-start.5
  44.6 1.1 copy-done.5
  45.7 0.7 stack.73.place_ref
  46.3 2.5 %copy.8 = bf16[24,8,8,384]{3,1,2,0:T(8,128)(2,1)} copy(bf16[24,8,8,384]{3,1,0,2:T(8,128)(2,1)} %bitcast.27) | data formatting | bytes 2359296
  48.9 5.4 %shard_map.38 = (bf16[192,3072]{1,0:T(8,128)(2,1)}, bf16[192,3072]{1,0:T(8,128)(2,1)}) custom-call(s32[5]{0:T(128)} %stack.73.place_ref, bf16[1,384,6144]{2,1,0:T(8,128)(2,1)} %tokens_ref.2, f32[1,6144]{1,0:T(1,128)} %bitcast.42, bf16[6,1536,384]{2,1,0:T(8,128)(2,1)} %bitcast.31), custom_call_target="tpu_custom_call" | custom-call | flops 9437184 | bytes 4718592 | tf_op jit(solution)/shard_map/pallas_call | solution.py:120
  54.2 1.4 broadcast_select_fusion.2
  55.6 12.3 %collective-permute-done.4.refs_25_.refs_0_.refs_16_ = bf16[192,3072]{1,0:T(8,128)(2,1)} collective-permute-done((bf16[192,3072]{1,0:T(8,128)(2,1)}, bf16[192,3072]{1,0:T(8,128)(2,1)}, u32[]{:S(2)}, u32[]{:S(2)}) %collective-permute-start.4) | collective-permute-done | bytes 1179680 | tf_op jit(solution)/shard_map/ppermute | solution.py:454
  68.1 0.6 collective-permute-start.13
  68.6 4.6 %collective-permute-start.10 = (bf16[192,3072]{1,0:T(8,128)(2,1)S(1)}, bf16[192,3072]{1,0:T(8,128)(2,1)S(1)}, u32[]{:S(2)}, u32[]{:S(2)}) collective-permute-start(bf16[192,3072]{1,0:T(8,128)(2,1)S(1)} %broadcast_select_fusion.2), channel_id=1, source_target_pairs={{0,4},{4,0},{8,12},{12,8},{1,5},{5,1},{9,13},{13,9},{2,6},{6,2},{1... | collective-permute-start | bytes 3538952 | tf_op jit(solution)/shard_map/ppermute | solution.py:454
  73.2 0.7 collective-permute-start.11
  74.0 0.9 collective-permute-start.12
  74.9 1.2 broadcast_select_fusion.1
  76.1 23.4 %collective-permute-done.10.refs_28_.refs_1_.refs_17_ = bf16[192,3072]{1,0:T(8,128)(2,1)S(1)} collective-permute-done((bf16[192,3072]{1,0:T(8,128)(2,1)S(1)}, bf16[192,3072]{1,0:T(8,128)(2,1)S(1)}, u32[]{:S(2)}, u32[]{:S(2)}) %collective-permute-start.10) | collective-permute-done | bytes 1179680 | tf_op jit(solution)/shard_map/ppermute | solution.py:454
  99.5 2.5 %collective-permute-done.12.refs_4_.refs_12_ = bf16[192,3072]{1,0:T(8,128)(2,1)S(1)} collective-permute-done((bf16[192,3072]{1,0:T(8,128)(2,1)}, bf16[192,3072]{1,0:T(8,128)(2,1)S(1)}, u32[]{:S(2)}, u32[]{:S(2)}) %collective-permute-start.12) | collective-permute-done | bytes 1179680 | tf_op jit(solution)/shard_map/ppermute | solution.py:463
  102.0 1.0 copy-done.6
  103.0 0.8 collective-permute-start.18
  103.8 1.5 collective-permute-start.19
  105.4 2.9 %collective-permute-start.16 = (bf16[1536,384]{1,0:T(8,128)(2,1)}, bf16[1536,384]{1,0:T(8,128)(2,1)}, u32[]{:S(2)}, u32[]{:S(2)}) collective-permute-start(bf16[1536,384]{1,0:T(8,128)(2,1)} %broadcast_select_fusion.1), channel_id=1, source_target_pairs={{0,4},{4,0},{8,12},{12,8},{1,5},{5,1},{9,13},{13,9},{2,6},{6,2},{1... | collective-permute-start | bytes 3538952 | tf_op jit(solution)/shard_map/ppermute | solution.py:454
  108.3 2.2 collective-permute-start.17
  110.5 1.0 copy-done.8
  111.5 2.8 %pad_maximum_fusion = bf16[384,3072]{1,0:T(8,128)(2,1)} fusion(bf16[192,3072]{1,0:T(8,128)(2,1)S(1)} %collective-permute-done.10.refs_28_.refs_1_.refs_17_, bf16[192,3072]{1,0:T(8,128)(2,1)} %collective-permute-done.4.refs_25_.refs_0_.refs_16_), kind=kLoop, calls=%fused_computation | loop fusion | flops 4718592 | bytes 4718592 | tf_op jit(solution)/shard_map/concatenate | solution.py:540
  114.3 2.5 %broadcast_select_fusion = bf16[1536,384]{1,0:T(8,128)(2,1)} fusion(bf16[1536,384]{1,0:T(8,128)(2,1)S(1)} %collective-permute-done.11.refs_14_.refs_22_, bf16[1536,384]{1,0:T(8,128)(2,1)} %get-tuple-element.210.refs_11_.refs_19_.refs_10_, pred[]{:T(512)S(6)} %or.4), kind=kLoop, calls=%fused_computation.2 | loop fusion | flops 589824 | bytes 3538945 | tf_op jit(solution)/shard_map/jit(_where)/select_n | solution.py:451
  116.8 15.0 %shard_map.39 = (bf16[384,128]{1,0:T(8,128)(2,1)}, bf16[384,128]{1,0:T(8,128)(2,1)}, f32[768,384]{1,0:T(8,128)}, f32[768,384]{1,0:T(8,128)}) custom-call(s32[2]{0:T(128)} %pad_add_fusion.role_ref, bf16[192,3072]{1,0:T(8,128)(2,1)} %get-tuple-element.124.refs_0_.refs_8_, bf16[192,3072]{1,0:T(8,128)(2,1)} %get-tuple-element.132.refs_1_.refs_9_, ...), custom_call_target="tpu_custom_call" | custom-call | flops 6341787648 | tf_op jit(solution)/shard_map/pallas_call | solution.py:364
  131.8 2.9 %collective-permute-done.16.refs_27_.refs_17_ = bf16[1536,384]{1,0:T(8,128)(2,1)} collective-permute-done((bf16[1536,384]{1,0:T(8,128)(2,1)}, bf16[1536,384]{1,0:T(8,128)(2,1)}, u32[]{:S(2)}, u32[]{:S(2)}) %collective-permute-start.16) | collective-permute-done | bytes 1179680 | tf_op jit(solution)/shard_map/ppermute | solution.py:454
  134.8 1.2 collective-permute-start.24
  136.5 3.6 %collective-permute-start.22 = (bf16[1536,384]{1,0:T(8,128)(2,1)}, bf16[1536,384]{1,0:T(8,128)(2,1)}, u32[]{:S(2)}, u32[]{:S(2)}) collective-permute-start(bf16[1536,384]{1,0:T(8,128)(2,1)} %broadcast_select_fusion), channel_id=1, source_target_pairs={{0,4},{4,0},{8,12},{12,8},{1,5},{5,1},{9,13},{13,9},{2,6},{6,2},{1... | collective-permute-start | bytes 3538952 | tf_op jit(solution)/shard_map/ppermute | solution.py:454
  140.2 1.9 collective-permute-start.23
  142.1 21.6 %shard_map.40 = (bf16[384,128]{1,0:T(8,128)(2,1)}, bf16[384,128]{1,0:T(8,128)(2,1)}, f32[768,384]{1,0:T(8,128)}, f32[768,384]{1,0:T(8,128)}, f32[768,384]{1,0:T(8,128)}, /*index=5*/f32[768,384]{1,0:T(8,128)}) custom-call(s32[2]{0:T(128)} %pad_add_fusion.role_ref, bf16[192,3072]{1,0:T(8,128)(2,1)} %collective-permute-done.1.refs_0_.refs_8_, ...), custom_call_target="tpu_custom_call" | custom-call | flops 9965666304 | tf_op jit(solution)/shard_map/pallas_call | solution.py:364
  163.7 2.8 %collective-permute-done.22.refs_18_.refs_8_ = bf16[1536,384]{1,0:T(8,128)(2,1)} collective-permute-done((bf16[1536,384]{1,0:T(8,128)(2,1)}, bf16[1536,384]{1,0:T(8,128)(2,1)}, u32[]{:S(2)}, u32[]{:S(2)}) %collective-permute-start.22) | collective-permute-done | bytes 1179680 | tf_op jit(solution)/shard_map/ppermute | solution.py:454
  166.6 1.6 collective-permute-start.32
  168.2 1.3 collective-permute-start.29
  169.4 1.9 collective-permute-start.30
  171.3 0.9 collective-permute-start.31
  172.2 12.9 %shard_map.41 = (bf16[384,128]{1,0:T(8,128)(2,1)}, bf16[384,128]{1,0:T(8,128)(2,1)}, f32[768,384]{1,0:T(8,128)}, bf16[384,128]{1,0:T(8,128)(2,1)}, bf16[384,128]{1,0:T(8,128)(2,1)}, /*index=5*/f32[768,384]{1,0:T(8,128)}) custom-call(s32[2]{0:T(128)} %pad_add_fusion.role_ref, bf16[192,3072]{1,0:T(8,128)(2,1)} %get-tuple-element.124.refs_0_.refs_8_, ...), custom_call_target="tpu_custom_call" | custom-call | flops 3623878656 | tf_op jit(solution)/shard_map/pallas_call | solution.py:364
  185.2 8.0 %shard_map.42.refs_28_ = f32[768,384]{1,0:T(8,128)} custom-call(s32[2]{0:T(128)} %pad_add_fusion.role_ref, bf16[192,3072]{1,0:T(8,128)(2,1)} %collective-permute-done.4.refs_25_.refs_0_.refs_16_, bf16[192,3072]{1,0:T(8,128)(2,1)} %copy-done.2, bf16[384,3072]{1,0:T(8,128)(2,1)} %collective-permute-done.26.refs_2_.refs_3_.refs_18_.refs_19_, ...), custom_call_target="tpu_custom_call" | custom-call | flops 2717908992 | tf_op jit(solution)/shard_map/pallas_call | solution.py:364
  193.2 6.4 %collective-permute-done.29.refs_25_ = bf16[1536,384]{1,0:T(8,128)(2,1)} collective-permute-done((bf16[1536,384]{1,0:T(8,128)(2,1)}, bf16[1536,384]{1,0:T(8,128)(2,1)}, u32[]{:S(2)}, u32[]{:S(2)}) %collective-permute-start.29) | collective-permute-done | bytes 1179680 | tf_op jit(solution)/shard_map/ppermute | solution.py:457
  200.4 13.0 %shard_map.43 = (bf16[384,384]{1,0:T(8,128)(2,1)}, bf16[384,384]{1,0:T(8,128)(2,1)}, bf16[384,384]{1,0:T(8,128)(2,1)}, bf16[384,384]{1,0:T(8,128)(2,1)}, bf16[38...) custom-call(s32[2]{0:T(128)} %pad_add_fusion.role_ref, bf16[192,3072]{1,0:T(8,128)(2,1)} %get-tuple-element.124.refs_0_.refs_8_, ...), custom_call_target="tpu_custom_call" | custom-call | flops 2717908992 | tf_op jit(solution)/shard_map/pallas_call | solution.py:364
  213.4 0.9 collective-permute-start.34
  214.8 2.1 collective-permute-start.36
  217.0 1.3 collective-permute-start.37
  218.3 1.3 collective-permute-start.38
  219.6 10.2 %shard_map.44 = (bf16[384,128]{1,0:T(8,128)(2,1)}, bf16[384,128]{1,0:T(8,128)(2,1)}) custom-call(s32[2]{0:T(128)} %pad_add_fusion.role_ref, bf16[192,3072]{1,0:T(8,128)(2,1)} %collective-permute-done.19.refs_0_, bf16[192,3072]{1,0:T(8,128)(2,1)} %collective-permute-done.25.refs_1_, bf16[192,3072]{1,0:T(8,128)(2,1)} %collective-permute-done.33.refs_2_, ...), custom_call_target="tpu_custom_call" | custom-call | flops 3623878656 | tf_op jit(solution)/shard_map/pallas_call | solution.py:364
  229.8 1.3 collective-permute-start.42
  231.1 1.3 collective-permute-start.43
  232.5 0.6 stack.63.place_ref
  233.1 6.2 %collective-permute-done.42.refs_6_ = bf16[384,128]{1,0:T(8,128)(2,1)S(1)} collective-permute-done((bf16[384,128]{1,0:T(8,128)(2,1)}, bf16[384,128]{1,0:T(8,128)(2,1)S(1)}, u32[]{:S(2)}, u32[]{:S(2)}) %collective-permute-start.42) | collective-permute-done | bytes 98336 | tf_op jit(solution)/shard_map/ppermute | solution.py:622
  239.3 1.6 collective-permute-done.43.refs_7_
  240.9 0.6 copy-done.17
  241.5 3.1 %shard_map.45 = bf16[384,1536]{1,0:T(8,128)(2,1)} custom-call(s32[5]{0:T(128)} %stack.63.place_ref, bf16[384,384]{1,0:T(8,128)(2,1)} %get-tuple-element.225.refs_0_, bf16[384,384]{1,0:T(8,128)(2,1)} %copy-done.12, bf16[384,384]{1,0:T(8,128)(2,1)} %copy-done.13, bf16[384,384]{1,0:T(8,128)(2,1)} %collective-permute-done.36.refs_3_, ...), custom_call_target="tpu_custom_call" | custom-call | bytes 2359296 | tf_op jit(solution)/shard_map/pallas_call | solution.py:425
  (81 shorter events, 2.3 us)
Async XLA Ops:
  6.4 29.2 %collective-permute-start = (bf16[192,3072]{1,0:T(8,128)(2,1)}, bf16[192,3072]{1,0:T(8,128)(2,1)S(1)}, u32[]{:S(2)}, u32[]{:S(2)}) collective-permute-start(bf16[192,3072]{1,0:T(8,128)(2,1)} %get-tuple-element.124.refs_0_.refs_8_), channel_id=1, source_target_pairs={{0,2},{2,0},{1,3},{3,1},{4,6},{6,4},{5,7},{7,5},{8,10},{10,8},{9,1... | collective-permute-start | bytes 3538952 | tf_op jit(solution)/shard_map/ppermute | solution.py:463
  9.4 27.7 %collective-permute-start.1 = (bf16[192,3072]{1,0:T(8,128)(2,1)}, bf16[192,3072]{1,0:T(8,128)(2,1)}, u32[]{:S(2)}, u32[]{:S(2)}) collective-permute-start(bf16[192,3072]{1,0:T(8,128)(2,1)} %get-tuple-element.124.refs_0_.refs_8_), channel_id=1, source_target_pairs={{0,16},{16,0},{1,17},{17,1},{2,18},{18,2},{3,19},{19,3},{4,20},{20... | collective-permute-start | bytes 3538952 | tf_op jit(solution)/shard_map/ppermute | solution.py:464
  10.9 28.9 %collective-permute-start.2 = (bf16[1536,384]{1,0:T(8,128)(2,1)}, bf16[1536,384]{1,0:T(8,128)(2,1)}, u32[]{:S(2)}, u32[]{:S(2)}) collective-permute-start(bf16[1536,384]{1,0:T(8,128)(2,1)} %get-tuple-element.128.refs_8_.refs_10_.refs_16_.refs_18_), channel_id=1, source_target_pairs={{0,4},{4,0},{8,12},{12,8},{1,5},{5,1},{9,13},{13,9},{2,6},{6,2},{1... | collective-permute-start | bytes 3538952 | tf_op jit(solution)/shard_map/ppermute | solution.py:454
  12.5 27.4 %collective-permute-start.3 = (bf16[1536,384]{1,0:T(8,128)(2,1)}, bf16[1536,384]{1,0:T(8,128)(2,1)}, u32[]{:S(2)}, u32[]{:S(2)}) collective-permute-start(bf16[1536,384]{1,0:T(8,128)(2,1)} %get-tuple-element.128.refs_8_.refs_10_.refs_16_.refs_18_), channel_id=1, source_target_pairs={{4,8},{8,4},{5,9},{9,5},{6,10},{10,6},{7,11},{11,7},{20,24},{24,20... | collective-permute-start | bytes 3538952 | tf_op jit(solution)/shard_map/ppermute | solution.py:460
  17.0 57.8 %copy-start = (bf16[1,1536,384]{2,1,0:T(8,128)(2,1)}, bf16[1,1536,384]{2,1,0:T(8,128)(2,1)S(1)}, u32[]{:S(2)}) copy-start(bf16[1,1536,384]{2,1,0:T(8,128)(2,1)S(1)} %get-tuple-element.238) | copy-start | bytes 3538948
  17.0 1.7 copy-start.1
  35.5 1.6 copy-start.4
  37.1 7.5 %collective-permute-start.8 = (bf16[192,3072]{1,0:T(8,128)(2,1)S(1)}, bf16[192,3072]{1,0:T(8,128)(2,1)S(1)}, u32[]{:S(2)}, u32[]{:S(2)}) collective-permute-start(bf16[192,3072]{1,0:T(8,128)(2,1)S(1)} %collective-permute-done.refs_4_.refs_12_), channel_id=1, source_target_pairs={{0,1},{1,0},{2,3},{3,2},{4,5},{5,4},{6,7},{7,6},{8,9},{9,8},{10,11... | collective-permute-start | bytes 3538952 | tf_op jit(solution)/shard_map/ppermute | solution.py:471
  37.1 30.9 %collective-permute-start.6 = (bf16[192,3072]{1,0:T(8,128)(2,1)}, bf16[192,3072]{1,0:T(8,128)(2,1)}, u32[]{:S(2)}, u32[]{:S(2)}) collective-permute-start(bf16[192,3072]{1,0:T(8,128)(2,1)} %get-tuple-element.132.refs_1_.refs_9_), channel_id=1, source_target_pairs={{0,2},{2,0},{1,3},{3,1},{4,6},{6,4},{5,7},{7,5},{8,10},{10,8},{9,1... | collective-permute-start | bytes 3538952 | tf_op jit(solution)/shard_map/ppermute | solution.py:463
  38.3 29.7 %collective-permute-start.7 = (bf16[192,3072]{1,0:T(8,128)(2,1)}, bf16[192,3072]{1,0:T(8,128)(2,1)}, u32[]{:S(2)}, u32[]{:S(2)}) collective-permute-start(bf16[192,3072]{1,0:T(8,128)(2,1)} %get-tuple-element.132.refs_1_.refs_9_), channel_id=1, source_target_pairs={{0,16},{16,0},{1,17},{17,1},{2,18},{18,2},{3,19},{19,3},{4,20},{20... | collective-permute-start | bytes 3538952 | tf_op jit(solution)/shard_map/ppermute | solution.py:464
  39.8 28.1 %collective-permute-start.4 = (bf16[192,3072]{1,0:T(8,128)(2,1)}, bf16[192,3072]{1,0:T(8,128)(2,1)}, u32[]{:S(2)}, u32[]{:S(2)}) collective-permute-start(bf16[192,3072]{1,0:T(8,128)(2,1)} %broadcast_select_fusion.3), channel_id=1, source_target_pairs={{0,4},{4,0},{8,12},{12,8},{1,5},{5,1},{9,13},{13,9},{2,6},{6,2},{1... | collective-permute-start | bytes 3538952 | tf_op jit(solution)/shard_map/ppermute | solution.py:454
  42.9 25.0 %collective-permute-start.5 = (bf16[1536,384]{1,0:T(8,128)(2,1)}, bf16[1536,384]{1,0:T(8,128)(2,1)}, u32[]{:S(2)}, u32[]{:S(2)}) collective-permute-start(bf16[1536,384]{1,0:T(8,128)(2,1)} %collective-permute-done.2.refs_15_.refs_16_.refs_23_.refs_26_), channel_id=1, source_target_pairs={{4,8},{8,4},{5,9},{9,5},{6,10},{10,6},{7,11},{11,7},{20,24},{24,20... | collective-permute-start | bytes 3538952 | tf_op jit(solution)/shard_map/ppermute | solution.py:460
  44.6 1.1 copy-start.5
  45.7 22.3 %collective-permute-start.9 = (bf16[192,3072]{1,0:T(8,128)(2,1)}, bf16[192,3072]{1,0:T(8,128)(2,1)}, u32[]{:S(2)}, u32[]{:S(2)}) collective-permute-start(bf16[192,3072]{1,0:T(8,128)(2,1)} %collective-permute-done.1.refs_0_.refs_8_), channel_id=1, source_target_pairs={{0,1},{1,0},{2,3},{3,2},{4,5},{5,4},{6,7},{7,6},{8,9},{9,8},{10,11... | collective-permute-start | bytes 3538952 | tf_op jit(solution)/shard_map/ppermute | solution.py:471
  68.0 6.9 %collective-permute-start.14 = (bf16[192,3072]{1,0:T(8,128)(2,1)}, bf16[192,3072]{1,0:T(8,128)(2,1)}, u32[]{:S(2)}, u32[]{:S(2)}) collective-permute-start(bf16[192,3072]{1,0:T(8,128)(2,1)} %collective-permute-done.6.refs_5_.refs_13_), channel_id=1, source_target_pairs={{0,1},{1,0},{2,3},{3,2},{4,5},{5,4},{6,7},{7,6},{8,9},{9,8},{10,11... | collective-permute-start | bytes 3538952 | tf_op jit(solution)/shard_map/ppermute | solution.py:471
  68.1 33.9 %collective-permute-start.13 = (bf16[192,3072]{1,0:T(8,128)(2,1)}, bf16[192,3072]{1,0:T(8,128)(2,1)}, u32[]{:S(2)}, u32[]{:S(2)}) collective-permute-start(bf16[192,3072]{1,0:T(8,128)(2,1)} %collective-permute-done.6.refs_5_.refs_13_), channel_id=1, source_target_pairs={{0,16},{16,0},{1,17},{17,1},{2,18},{18,2},{3,19},{19,3},{4,20},{20... | collective-permute-start | bytes 3538952 | tf_op jit(solution)/shard_map/ppermute | solution.py:464
  68.6 30.9 %collective-permute-start.10 = (bf16[192,3072]{1,0:T(8,128)(2,1)S(1)}, bf16[192,3072]{1,0:T(8,128)(2,1)S(1)}, u32[]{:S(2)}, u32[]{:S(2)}) collective-permute-start(bf16[192,3072]{1,0:T(8,128)(2,1)S(1)} %broadcast_select_fusion.2), channel_id=1, source_target_pairs={{0,4},{4,0},{8,12},{12,8},{1,5},{5,1},{9,13},{13,9},{2,6},{6,2},{1... | collective-permute-start | bytes 3538952 | tf_op jit(solution)/shard_map/ppermute | solution.py:454
  73.2 26.3 %collective-permute-start.11 = (bf16[1536,384]{1,0:T(8,128)(2,1)S(1)}, bf16[1536,384]{1,0:T(8,128)(2,1)S(1)}, u32[]{:S(2)}, u32[]{:S(2)}) collective-permute-start(bf16[1536,384]{1,0:T(8,128)(2,1)S(1)} %bitcast.33), channel_id=1, source_target_pairs={{4,8},{8,4},{5,9},{9,5},{6,10},{10,6},{7,11},{11,7},{20,24},{24,20... | collective-permute-start | bytes 3538952 | tf_op jit(solution)/shard_map/ppermute | solution.py:460
  74.0 28.0 %collective-permute-start.12 = (bf16[192,3072]{1,0:T(8,128)(2,1)}, bf16[192,3072]{1,0:T(8,128)(2,1)S(1)}, u32[]{:S(2)}, u32[]{:S(2)}) collective-permute-start(bf16[192,3072]{1,0:T(8,128)(2,1)} %collective-permute-done.1.refs_0_.refs_8_), channel_id=1, source_target_pairs={{0,2},{2,0},{1,3},{3,1},{4,6},{6,4},{5,7},{7,5},{8,10},{10,8},{9,1... | collective-permute-start | bytes 3538952 | tf_op jit(solution)/shard_map/ppermute | solution.py:463
  74.9 27.1 %collective-permute-start.15 = (bf16[192,3072]{1,0:T(8,128)(2,1)}, bf16[192,3072]{1,0:T(8,128)(2,1)S(1)}, u32[]{:S(2)}, u32[]{:S(2)}) collective-permute-start(bf16[192,3072]{1,0:T(8,128)(2,1)} %collective-permute-done.7.refs_1_.refs_9_), channel_id=1, source_target_pairs={{0,1},{1,0},{2,3},{3,2},{4,5},{5,4},{6,7},{7,6},{8,9},{9,8},{10,11... | collective-permute-start | bytes 3538952 | tf_op jit(solution)/shard_map/ppermute | solution.py:471
  99.5 14.8 %copy-start.2 = (bf16[192,3072]{1,0:T(8,128)(2,1)}, bf16[192,3072]{1,0:T(8,128)(2,1)S(1)}, u32[]{:S(2)}) copy-start(bf16[192,3072]{1,0:T(8,128)(2,1)S(1)} %collective-permute-done.10.refs_28_.refs_1_.refs_17_) | copy-start | bytes 3538948
  99.5 14.8 %copy-start.10 = (bf16[1536,384]{1,0:T(8,128)(2,1)}, bf16[1536,384]{1,0:T(8,128)(2,1)S(1)}, u32[]{:S(2)}) copy-start(bf16[1536,384]{1,0:T(8,128)(2,1)S(1)} %collective-permute-done.11.refs_14_.refs_22_) | copy-start | bytes 3538948
  102.0 1.0 copy-start.6
  103.0 7.5 %copy-start.7 = (bf16[192,3072]{1,0:T(8,128)(2,1)}, bf16[192,3072]{1,0:T(8,128)(2,1)S(1)}, u32[]{:S(2)}) copy-start(bf16[192,3072]{1,0:T(8,128)(2,1)S(1)} %collective-permute-done.15.refs_3_.refs_11_) | copy-start | bytes 3538948
  103.0 7.5 %collective-permute-start.20 = (bf16[192,3072]{1,0:T(8,128)(2,1)S(1)}, bf16[192,3072]{1,0:T(8,128)(2,1)S(1)}, u32[]{:S(2)}, u32[]{:S(2)}) collective-permute-start(bf16[192,3072]{1,0:T(8,128)(2,1)S(1)} %collective-permute-done.12.refs_4_.refs_12_), channel_id=1, source_target_pairs={{0,1},{1,0},{2,3},{3,2},{4,5},{5,4},{6,7},{7,6},{8,9},{9,8},{10,11... | collective-permute-start | bytes 3538952 | tf_op jit(solution)/shard_map/ppermute | solution.py:471
  103.0 31.7 %collective-permute-start.18 = (bf16[192,3072]{1,0:T(8,128)(2,1)}, bf16[192,3072]{1,0:T(8,128)(2,1)}, u32[]{:S(2)}, u32[]{:S(2)}) collective-permute-start(bf16[192,3072]{1,0:T(8,128)(2,1)} %collective-permute-done.4.refs_25_.refs_0_.refs_16_), channel_id=1, source_target_pairs={{0,2},{2,0},{1,3},{3,1},{4,6},{6,4},{5,7},{7,5},{8,10},{10,8},{9,1... | collective-permute-start | bytes 3538952 | tf_op jit(solution)/shard_map/ppermute | solution.py:463
  103.8 30.8 %collective-permute-start.19 = (bf16[192,3072]{1,0:T(8,128)(2,1)}, bf16[192,3072]{1,0:T(8,128)(2,1)}, u32[]{:S(2)}, u32[]{:S(2)}) collective-permute-start(bf16[192,3072]{1,0:T(8,128)(2,1)} %collective-permute-done.4.refs_25_.refs_0_.refs_16_), channel_id=1, source_target_pairs={{0,16},{16,0},{1,17},{17,1},{2,18},{18,2},{3,19},{19,3},{4,20},{20... | collective-permute-start | bytes 3538952 | tf_op jit(solution)/shard_map/ppermute | solution.py:464
  105.4 29.3 %collective-permute-start.16 = (bf16[1536,384]{1,0:T(8,128)(2,1)}, bf16[1536,384]{1,0:T(8,128)(2,1)}, u32[]{:S(2)}, u32[]{:S(2)}) collective-permute-start(bf16[1536,384]{1,0:T(8,128)(2,1)} %broadcast_select_fusion.1), channel_id=1, source_target_pairs={{0,4},{4,0},{8,12},{12,8},{1,5},{5,1},{9,13},{13,9},{2,6},{6,2},{1... | collective-permute-start | bytes 3538952 | tf_op jit(solution)/shard_map/ppermute | solution.py:454
  108.3 26.4 %collective-permute-start.17 = (bf16[1536,384]{1,0:T(8,128)(2,1)}, bf16[1536,384]{1,0:T(8,128)(2,1)}, u32[]{:S(2)}, u32[]{:S(2)}) collective-permute-start(bf16[1536,384]{1,0:T(8,128)(2,1)} %get-tuple-element.210.refs_11_.refs_19_.refs_10_), channel_id=1, source_target_pairs={{4,8},{8,4},{5,9},{9,5},{6,10},{10,6},{7,11},{11,7},{20,24},{24,20... | collective-permute-start | bytes 3538952 | tf_op jit(solution)/shard_map/ppermute | solution.py:460
  110.5 1.0 copy-start.8
  111.5 23.2 %collective-permute-start.21 = (bf16[192,3072]{1,0:T(8,128)(2,1)}, bf16[192,3072]{1,0:T(8,128)(2,1)}, u32[]{:S(2)}, u32[]{:S(2)}) collective-permute-start(bf16[192,3072]{1,0:T(8,128)(2,1)} %collective-permute-done.13.refs_5_.refs_13_), channel_id=1, source_target_pairs={{0,1},{1,0},{2,3},{3,2},{4,5},{5,4},{6,7},{7,6},{8,9},{9,8},{10,11... | collective-permute-start | bytes 3538952 | tf_op jit(solution)/shard_map/ppermute | solution.py:471
  116.8 18.0 %copy-start.3 = (bf16[192,3072]{1,0:T(8,128)(2,1)S(1)}, bf16[192,3072]{1,0:T(8,128)(2,1)}, u32[]{:S(2)}) copy-start(bf16[192,3072]{1,0:T(8,128)(2,1)} %copy-done.2) | copy-start | bytes 3538948
  134.7 7.3 %collective-permute-start.26 = (bf16[384,3072]{1,0:T(8,128)(2,1)}, bf16[384,3072]{1,0:T(8,128)(2,1)}, u32[]{:S(2)}, u32[]{:S(2)}) collective-permute-start(bf16[384,3072]{1,0:T(8,128)(2,1)} %pad_maximum_fusion), channel_id=1, source_target_pairs={{0,1},{1,0},{2,3},{3,2},{4,5},{5,4},{6,7},{7,6},{8,9},{9,8},{10,11... | collective-permute-start | bytes 7077896 | tf_op jit(solution)/shard_map/ppermute | solution.py:471
  134.8 31.7 %collective-permute-start.24 = (bf16[192,3072]{1,0:T(8,128)(2,1)S(1)}, bf16[192,3072]{1,0:T(8,128)(2,1)}, u32[]{:S(2)}, u32[]{:S(2)}) collective-permute-start(bf16[192,3072]{1,0:T(8,128)(2,1)S(1)} %copy-done.3), channel_id=1, source_target_pairs={{0,2},{2,0},{1,3},{3,1},{4,6},{6,4},{5,7},{7,5},{8,10},{10,8},{9,1... | collective-permute-start | bytes 3538952 | tf_op jit(solution)/shard_map/ppermute | solution.py:463
  136.0 30.5 %collective-permute-start.25 = (bf16[192,3072]{1,0:T(8,128)(2,1)S(1)}, bf16[192,3072]{1,0:T(8,128)(2,1)}, u32[]{:S(2)}, u32[]{:S(2)}) collective-permute-start(bf16[192,3072]{1,0:T(8,128)(2,1)S(1)} %copy-done.3), channel_id=1, source_target_pairs={{0,16},{16,0},{1,17},{17,1},{2,18},{18,2},{3,19},{19,3},{4,20},{20... | collective-permute-start | bytes 3538952 | tf_op jit(solution)/shard_map/ppermute | solution.py:464
  136.5 29.9 %collective-permute-start.22 = (bf16[1536,384]{1,0:T(8,128)(2,1)}, bf16[1536,384]{1,0:T(8,128)(2,1)}, u32[]{:S(2)}, u32[]{:S(2)}) collective-permute-start(bf16[1536,384]{1,0:T(8,128)(2,1)} %broadcast_select_fusion), channel_id=1, source_target_pairs={{0,4},{4,0},{8,12},{12,8},{1,5},{5,1},{9,13},{13,9},{2,6},{6,2},{1... | collective-permute-start | bytes 3538952 | tf_op jit(solution)/shard_map/ppermute | solution.py:454
  140.2 26.3 %collective-permute-start.23 = (bf16[1536,384]{1,0:T(8,128)(2,1)}, bf16[1536,384]{1,0:T(8,128)(2,1)}, u32[]{:S(2)}, u32[]{:S(2)}) collective-permute-start(bf16[1536,384]{1,0:T(8,128)(2,1)} %collective-permute-done.16.refs_27_.refs_17_), channel_id=1, source_target_pairs={{4,8},{8,4},{5,9},{9,5},{6,10},{10,6},{7,11},{11,7},{20,24},{24,20... | collective-permute-start | bytes 3538952 | tf_op jit(solution)/shard_map/ppermute | solution.py:460
  142.0 24.5 %collective-permute-start.27 = (bf16[192,3072]{1,0:T(8,128)(2,1)}, bf16[192,3072]{1,0:T(8,128)(2,1)}, u32[]{:S(2)}, u32[]{:S(2)}) collective-permute-start(bf16[192,3072]{1,0:T(8,128)(2,1)} %collective-permute-done.18.refs_4_.refs_20_), channel_id=1, source_target_pairs={{0,1},{1,0},{2,3},{3,2},{4,5},{5,4},{6,7},{7,6},{8,9},{9,8},{10,11... | collective-permute-start | bytes 3538952 | tf_op jit(solution)/shard_map/ppermute | solution.py:471
  166.5 5.7 %collective-permute-start.28 = (bf16[192,3072]{1,0:T(8,128)(2,1)}, bf16[192,3072]{1,0:T(8,128)(2,1)S(1)}, u32[]{:S(2)}, u32[]{:S(2)}) collective-permute-start(bf16[192,3072]{1,0:T(8,128)(2,1)} %collective-permute-done.24.refs_5_.refs_21_), channel_id=1, source_target_pairs={{0,1},{1,0},{2,3},{3,2},{4,5},{5,4},{6,7},{7,6},{8,9},{9,8},{10,11... | collective-permute-start | bytes 3538952 | tf_op jit(solution)/shard_map/ppermute | solution.py:471
  166.6 33.2 %collective-permute-start.32 = (bf16[192,3072]{1,0:T(8,128)(2,1)}, bf16[192,3072]{1,0:T(8,128)(2,1)}, u32[]{:S(2)}, u32[]{:S(2)}) collective-permute-start(bf16[192,3072]{1,0:T(8,128)(2,1)} %collective-permute-done.24.refs_5_.refs_21_), channel_id=1, source_target_pairs={{0,16},{16,0},{1,17},{17,1},{2,18},{18,2},{3,19},{19,3},{4,20},{20... | collective-permute-start | bytes 3538952 | tf_op jit(solution)/shard_map/ppermute | solution.py:464
  168.2 31.5 %collective-permute-start.29 = (bf16[1536,384]{1,0:T(8,128)(2,1)}, bf16[1536,384]{1,0:T(8,128)(2,1)}, u32[]{:S(2)}, u32[]{:S(2)}) collective-permute-start(bf16[1536,384]{1,0:T(8,128)(2,1)} %collective-permute-done.23.refs_16_), channel_id=1, source_target_pairs={{4,0},{8,12},{5,1},{9,13},{6,2},{10,14},{7,3},{11,15},{20,16},{24,... | collective-permute-start | bytes 3538952 | tf_op jit(solution)/shard_map/ppermute | solution.py:457
  169.4 30.2 %collective-permute-start.30 = (bf16[1536,384]{1,0:T(8,128)(2,1)}, bf16[1536,384]{1,0:T(8,128)(2,1)}, u32[]{:S(2)}, u32[]{:S(2)}) collective-permute-start(bf16[1536,384]{1,0:T(8,128)(2,1)} %collective-permute-done.22.refs_18_.refs_8_), channel_id=1, source_target_pairs={{4,8},{8,4},{5,9},{9,5},{6,10},{10,6},{7,11},{11,7},{20,24},{24,20... | collective-permute-start | bytes 3538952 | tf_op jit(solution)/shard_map/ppermute | solution.py:460
  171.3 28.4 %collective-permute-start.31 = (bf16[192,3072]{1,0:T(8,128)(2,1)}, bf16[192,3072]{1,0:T(8,128)(2,1)}, u32[]{:S(2)}, u32[]{:S(2)}) collective-permute-start(bf16[192,3072]{1,0:T(8,128)(2,1)} %collective-permute-done.19.refs_0_), channel_id=1, source_target_pairs={{0,2},{2,0},{1,3},{3,1},{4,6},{6,4},{5,7},{7,5},{8,10},{10,8},{9,1... | collective-permute-start | bytes 3538952 | tf_op jit(solution)/shard_map/ppermute | solution.py:463
  172.2 12.9 %copy-start.9 = (bf16[192,3072]{1,0:T(8,128)(2,1)}, bf16[192,3072]{1,0:T(8,128)(2,1)S(1)}, u32[]{:S(2)}) copy-start(bf16[192,3072]{1,0:T(8,128)(2,1)S(1)} %collective-permute-done.28.refs_7_.refs_23_) | copy-start | bytes 3538948
  172.2 27.5 %collective-permute-start.33 = (bf16[192,3072]{1,0:T(8,128)(2,1)}, bf16[192,3072]{1,0:T(8,128)(2,1)}, u32[]{:S(2)}, u32[]{:S(2)}) collective-permute-start(bf16[192,3072]{1,0:T(8,128)(2,1)} %collective-permute-done.19.refs_0_), channel_id=1, source_target_pairs={{0,1},{1,0},{2,3},{3,2},{4,5},{5,4},{6,7},{7,6},{8,9},{9,8},{10,11... | collective-permute-start | bytes 3538952 | tf_op jit(solution)/shard_map/ppermute | solution.py:471
  199.8 15.1 %collective-permute-start.39 = (bf16[192,3072]{1,0:T(8,128)(2,1)}, bf16[192,3072]{1,0:T(8,128)(2,1)S(1)}, u32[]{:S(2)}, u32[]{:S(2)}) collective-permute-start(bf16[192,3072]{1,0:T(8,128)(2,1)} %collective-permute-done.25.refs_1_), channel_id=1, source_target_pairs={{0,1},{1,0},{2,3},{3,2},{4,5},{5,4},{6,7},{7,6},{8,9},{9,8},{10,11... | collective-permute-start | bytes 3538952 | tf_op jit(solution)/shard_map/ppermute | solution.py:593
  199.8 17.2 %collective-permute-start.40 = (bf16[192,3072]{1,0:T(8,128)(2,1)}, bf16[192,3072]{1,0:T(8,128)(2,1)}, u32[]{:S(2)}, u32[]{:S(2)}) collective-permute-start(bf16[192,3072]{1,0:T(8,128)(2,1)} %collective-permute-done.31.refs_4_), channel_id=1, source_target_pairs={{0,1},{1,0},{2,3},{3,2},{4,5},{5,4},{6,7},{7,6},{8,9},{9,8},{10,11... | collective-permute-start | bytes 3538952 | tf_op jit(solution)/shard_map/ppermute | solution.py:593
  200.3 18.0 %collective-permute-start.41 = (bf16[192,3072]{1,0:T(8,128)(2,1)}, bf16[192,3072]{1,0:T(8,128)(2,1)}, u32[]{:S(2)}, u32[]{:S(2)}) collective-permute-start(bf16[192,3072]{1,0:T(8,128)(2,1)} %collective-permute-done.32.refs_5_), channel_id=1, source_target_pairs={{0,1},{1,0},{2,3},{3,2},{4,5},{5,4},{6,7},{7,6},{8,9},{9,8},{10,11... | collective-permute-start | bytes 3538952 | tf_op jit(solution)/shard_map/ppermute | solution.py:593
  213.4 19.6 %collective-permute-start.34 = (bf16[384,384]{1,0:T(8,128)(2,1)}, bf16[384,384]{1,0:T(8,128)(2,1)S(1)}, u32[]{:S(2)}, u32[]{:S(2)}) collective-permute-start(bf16[384,384]{1,0:T(8,128)(2,1)} %get-tuple-element.226), channel_id=1, source_target_pairs={{0,2},{2,0},{16,18},{18,16},{1,3},{3,1},{17,19},{19,17},{4,6},{6,4... | collective-permute-start | bytes 884744 | tf_op jit(solution)/shard_map/ppermute | solution.py:486
  214.3 18.7 %collective-permute-start.35 = (bf16[384,384]{1,0:T(8,128)(2,1)}, bf16[384,384]{1,0:T(8,128)(2,1)S(1)}, u32[]{:S(2)}, u32[]{:S(2)}) collective-permute-start(bf16[384,384]{1,0:T(8,128)(2,1)} %get-tuple-element.227), channel_id=1, source_target_pairs={{0,16},{2,18},{16,0},{18,2},{1,17},{3,19},{17,1},{19,3},{4,20},{6,... | collective-permute-start | bytes 884744 | tf_op jit(solution)/shard_map/ppermute | solution.py:486
  214.8 4.7 %copy-start.11 = (bf16[192,3072]{1,0:T(8,128)(2,1)}, bf16[192,3072]{1,0:T(8,128)(2,1)S(1)}, u32[]{:S(2)}) copy-start(bf16[192,3072]{1,0:T(8,128)(2,1)S(1)} %collective-permute-done.39.refs_3_) | copy-start | bytes 3538948
  214.8 18.2 %collective-permute-start.36 = (bf16[384,384]{1,0:T(8,128)(2,1)}, bf16[384,384]{1,0:T(8,128)(2,1)}, u32[]{:S(2)}, u32[]{:S(2)}) collective-permute-start(bf16[384,384]{1,0:T(8,128)(2,1)} %get-tuple-element.228), channel_id=1, source_target_pairs={{0,18},{2,16},{16,2},{18,0},{1,19},{3,17},{17,3},{19,1},{4,22},{6,... | collective-permute-start | bytes 884744 | tf_op jit(solution)/shard_map/ppermute | solution.py:486
  217.0 12.8 %collective-permute-start.37 = (bf16[384,128]{1,0:T(8,128)(2,1)}, bf16[384,128]{1,0:T(8,128)(2,1)S(1)}, u32[]{:S(2)}, u32[]{:S(2)}) collective-permute-start(bf16[384,128]{1,0:T(8,128)(2,1)} %get-tuple-element.229), channel_id=1, source_target_pairs={{4,0},{6,2},{8,12},{10,14},{20,16},{22,18},{24,28},{26,30},{5,1},{... | collective-permute-start | bytes 294920 | tf_op jit(solution)/shard_map/ppermute | solution.py:622
  218.3 12.8 %collective-permute-start.38 = (bf16[384,128]{1,0:T(8,128)(2,1)}, bf16[384,128]{1,0:T(8,128)(2,1)S(1)}, u32[]{:S(2)}, u32[]{:S(2)}) collective-permute-start(bf16[384,128]{1,0:T(8,128)(2,1)} %get-tuple-element.230), channel_id=1, source_target_pairs={{4,2},{6,0},{8,14},{10,12},{20,18},{22,16},{24,30},{26,28},{5,3},{... | collective-permute-start | bytes 294920 | tf_op jit(solution)/shard_map/ppermute | solution.py:622
  229.8 11.1 %copy-start.14 = (bf16[384,128]{1,0:T(8,128)(2,1)}, bf16[384,128]{1,0:T(8,128)(2,1)S(1)}, u32[]{:S(2)}) copy-start(bf16[384,128]{1,0:T(8,128)(2,1)S(1)} %collective-permute-done.37.refs_4_) | copy-start | bytes 294916
  229.8 9.5 %collective-permute-start.42 = (bf16[384,128]{1,0:T(8,128)(2,1)}, bf16[384,128]{1,0:T(8,128)(2,1)S(1)}, u32[]{:S(2)}, u32[]{:S(2)}) collective-permute-start(bf16[384,128]{1,0:T(8,128)(2,1)} %get-tuple-element.235), channel_id=1, source_target_pairs={{4,16},{6,18},{8,28},{10,30},{20,0},{22,2},{24,12},{26,14},{5,17},... | collective-permute-start | bytes 294920 | tf_op jit(solution)/shard_map/ppermute | solution.py:622
  231.1 9.8 %copy-start.15 = (bf16[384,128]{1,0:T(8,128)(2,1)}, bf16[384,128]{1,0:T(8,128)(2,1)S(1)}, u32[]{:S(2)}) copy-start(bf16[384,128]{1,0:T(8,128)(2,1)S(1)} %collective-permute-done.38.refs_5_) | copy-start | bytes 294916
  231.1 9.8 %collective-permute-start.43 = (bf16[384,128]{1,0:T(8,128)(2,1)}, bf16[384,128]{1,0:T(8,128)(2,1)S(1)}, u32[]{:S(2)}, u32[]{:S(2)}) collective-permute-start(bf16[384,128]{1,0:T(8,128)(2,1)} %get-tuple-element.236), channel_id=1, source_target_pairs={{4,18},{6,16},{8,30},{10,28},{20,2},{22,0},{24,14},{26,12},{5,19},... | collective-permute-start | bytes 294920 | tf_op jit(solution)/shard_map/ppermute | solution.py:622
  233.1 7.8 %copy-start.12 = (bf16[384,384]{1,0:T(8,128)(2,1)}, bf16[384,384]{1,0:T(8,128)(2,1)S(1)}, u32[]{:S(2)}) copy-start(bf16[384,384]{1,0:T(8,128)(2,1)S(1)} %collective-permute-done.34.refs_1_) | copy-start | bytes 884740
  233.1 7.8 %copy-start.13 = (bf16[384,384]{1,0:T(8,128)(2,1)}, bf16[384,384]{1,0:T(8,128)(2,1)S(1)}, u32[]{:S(2)}) copy-start(bf16[384,384]{1,0:T(8,128)(2,1)S(1)} %collective-permute-done.35.refs_2_) | copy-start | bytes 884740
  239.3 1.6 copy-start.16
  240.9 0.6 copy-start.17

commit v3 on v2

--- a/solution.py
+++ b/solution.py
@@ -273,7 +273,7 @@
         start_stage(*stage)
     for copy in carry_copies():
         copy.start()
-    ready, waiting = set(), []
+    ready, waiting, step = set(), [], 384
     for index, (i, n) in enumerate(stages):
         low, high = plan.uses[i][n]
         pltpu.make_async_copy(features(i, n), features(i, n), token_sems.at[i, n]).wait()
@@ -283,27 +283,41 @@
                 pltpu.make_async_copy(weight(n, j), weight(n, j), weight_sems.at[n, j]).wait()
         if index + ahead < len(stages):
             start_stage(*stages[index + ahead])
-        term = jnp.dot(
-            features(i, n)[...],
-            weight_ref[n * slab : (n + 1) * slab, low * wide : high * wide],
-            preferred_element_type=jnp.float32,
-        )
+        mine = {
+            j: [m for m in ns if plan.uses[i][m] and j in range(*plan.uses[i][m])]
+            for j in range(low, high)
+        }
         for j in range(low, high):
-            value = term[:, (j - low) * wide : (j - low + 1) * wide]
-            mine = [m for m in ns if plan.uses[i][m] and j in range(*plan.uses[i][m])]
-            if n == mine[0] and j in plan.added[i]:
+            if n == mine[j][0] and j in plan.added[i]:
                 partial_copy(i, j).wait()
-            if n != mine[0] or j in plan.added[i]:
-                value += total(i, j)[...]
-            if n == mine[-1] and j in plan.finished[i]:
-                projected_ref[i % 2] = value.astype(jnp.bfloat16)
+
+        @pl.loop(0, tokens // step)
+        def _(r):
+            local = pl.ds(pl.multiple_of(r * step, step), step)
+            rows = pl.ds(pl.multiple_of(i * tokens + r * step, step), step)
+            term = jnp.dot(
+                features_ref[rows, n * slab : (n + 1) * slab],
+                weight_ref[n * slab : (n + 1) * slab, low * wide : high * wide],
+                preferred_element_type=jnp.float32,
+            )
+            for j in range(low, high):
+                value = term[:, (j - low) * wide : (j - low + 1) * wide]
+                if n != mine[j][0] or j in plan.added[i]:
+                    value += total_ref[rows, j * wide : (j + 1) * wide]
+                if n == mine[j][-1] and j in plan.finished[i]:
+                    projected_ref[i % 2, local, :] = value.astype(jnp.bfloat16)
+                else:
+                    total_ref[rows, j * wide : (j + 1) * wide] = value
+
+        for j in range(low, high):
+            if n != mine[j][-1]:
+                continue
+            if j in plan.finished[i]:
                 if waiting:
                     attend_rows(*waiting.pop())
                 column = plan.carried[i] * wide // 3
                 waiting.append((projected_ref.at[i % 2], outs[i][j], column))
-                continue
-            total(i, j)[...] = value
-            if n == mine[-1]:
+            else:
                 out_copy(i, j).start()
     if waiting:
         attend_rows(*waiting.pop())

time: 249 us -> 247 us (level); the launches traced: 245 us -> 246 us
    ppermute x5, waiting for transfers between devices: 41.4 us -> 44.1 us  [pair(): return lax.ppermute(value, 'dp', [(0, 1), (1, 0), (2, 3), (3, 2)])]
  transfers between devices with their start and end apart: 44 -> 44, of which waited for: 11 -> 10; matrix products, arithmetic and copies ran while one was open for 7% -> 7% of each run, Pallas kernels for 35% -> 35%
where the time goes in v3:
time: 247 us; the launch traced here: 246 us
  Pallas kernels  94.5 us (38%)
  waiting for transfers between devices  77.2 us (31%)
  starting transfers between devices  51.4 us (21%)
  local copies, waits for them, and re-layouts  12.8 us (5%)
  other arithmetic  9.68 us (4%)
    pallas_call x6, Pallas kernels, run_jobs(): pl.pallas_call(functools.partial(job_kernel, plan), out_shape=shapes, in_...  80.4 us
    ppermute x5, waiting for transfers between devices, pair(): return lax.ppermute(value, 'dp', [(0, 1), (1, 0), (2, 3), (3, 2)])  44.1 us
    ppermute x6, waiting for transfers between devices, shared(): beside = lambda value: lax.ppermute(value, 'seq', swap)  17.5 us
    ppermute x5, starting transfers between devices, pair(): return lax.ppermute(value, 'dp', [(0, 1), (1, 0), (2, 3), (3, 2)])  15.8 us
    pallas_call x2, Pallas kernels, normalize_part(): pl.pallas_call(normalize_kernel, out_shape=[half] * 2 + [jax.ShapeDtypeSt...  11.1 us
    ppermute x6, starting transfers between devices, middle(): return lax.ppermute(value, 'dp', [(1, 2), (2, 1)])  9.16 us
    ppermute x4, waiting for transfers between devices, hand_back(): got.append(lax.ppermute(sent, ('groups', 'dp', 'seq'), steps))  8.09 us
    ppermute x6, starting transfers between devices, shared(): beside = lambda value: lax.ppermute(value, 'seq', swap)  8.03 us
  transfers between devices with their start and end apart: 44, of which 10 were waited for; matrix products, arithmetic and copies ran while one was open for 7% of the time, Pallas kernels for 35%

profile of v3, /device:TPU:0, one launch (start us, length us, event | category | flops | bytes accessed | tf_op | source)
XLA Modules:
  0.0 246.1 jit_solution(807870905109842560)
XLA Ops:
  0.0 0.7 stack.70.place_ref
  0.7 5.7 %shard_map.37 = (bf16[192,3072]{1,0:T(8,128)(2,1)}, bf16[192,3072]{1,0:T(8,128)(2,1)}, bf16[1536,384]{1,0:T(8,128)(2,1)}) custom-call(s32[6]{0:T(128)} %stack.70.place_ref, bf16[1,384,6144]{2,1,0:T(8,128)(2,1)} %tokens_ref.2, f32[1,6144]{1,0:T(1,128)} %bitcast.41, bf16[6,1536,384]{2,1,0:T(8,128)(2,1)} %bitcast.29), custom_call_target="tpu_custom_call" | custom-call | flops 9437184 | bytes 4718592 | tf_op jit(solution)/shard_map/pallas_call | solution.py:120
  6.4 3.0 %collective-permute-start = (bf16[192,3072]{1,0:T(8,128)(2,1)}, bf16[192,3072]{1,0:T(8,128)(2,1)S(1)}, u32[]{:S(2)}, u32[]{:S(2)}) collective-permute-start(bf16[192,3072]{1,0:T(8,128)(2,1)} %get-tuple-element.124.refs_0_.refs_8_), channel_id=1, source_target_pairs={{0,2},{2,0},{1,3},{3,1},{4,6},{6,4},{5,7},{7,5},{8,10},{10,8},{9,1... | collective-permute-start | bytes 3538952 | tf_op jit(solution)/shard_map/ppermute | solution.py:477
  9.4 1.5 collective-permute-start.1
  10.9 1.6 collective-permute-start.2
  12.5 1.7 collective-permute-start.3
  14.1 2.9 %dynamic-slice_bitcast_fusion = (bf16[1536,384]{1,0:T(8,128)(2,1)}, bf16[1,1536,384]{2,1,0:T(8,128)(2,1)S(1)}) fusion(bf16[6,1536,384]{2,1,0:T(8,128)(2,1)} %bitcast.30, s32[]{:T(128)S(6)} %select_n.77, s32[]{:T(128)S(6)} %select_n.76), kind=kLoop, calls=%fused_computation.1 | loop fusion | bytes 4718600 | tf_op jit(solution)/shard_map/jit(dynamic_index_in_dim)/squeeze | solution.py:514
  17.2 1.5 copy-done.1
  18.7 1.2 broadcast_select_fusion.3
  19.9 0.6 pad_add_fusion.role_ref
  20.5 15.0 %collective-permute-done.refs_4_.refs_12_ = bf16[192,3072]{1,0:T(8,128)(2,1)S(1)} collective-permute-done((bf16[192,3072]{1,0:T(8,128)(2,1)}, bf16[192,3072]{1,0:T(8,128)(2,1)S(1)}, u32[]{:S(2)}, u32[]{:S(2)}) %collective-permute-start) | collective-permute-done | bytes 1179680 | tf_op jit(solution)/shard_map/ppermute | solution.py:477
  35.5 1.6 collective-permute-done.1.refs_0_.refs_8_
  37.1 1.2 collective-permute-start.6
  38.3 1.5 collective-permute-start.7
  39.8 3.1 %collective-permute-start.4 = (bf16[192,3072]{1,0:T(8,128)(2,1)}, bf16[192,3072]{1,0:T(8,128)(2,1)}, u32[]{:S(2)}, u32[]{:S(2)}) collective-permute-start(bf16[192,3072]{1,0:T(8,128)(2,1)} %broadcast_select_fusion.3), channel_id=1, source_target_pairs={{0,4},{4,0},{8,12},{12,8},{1,5},{5,1},{9,13},{13,9},{2,6},{6,2},{1... | collective-permute-start | bytes 3538952 | tf_op jit(solution)/shard_map/ppermute | solution.py:468
  42.9 1.7 collective-permute-start.5
  44.6 1.1 copy-done.5
  45.7 0.7 stack.73.place_ref
  46.3 2.5 %copy.8 = bf16[24,8,8,384]{3,1,2,0:T(8,128)(2,1)} copy(bf16[24,8,8,384]{3,1,0,2:T(8,128)(2,1)} %bitcast.27) | data formatting | bytes 2359296
  48.9 5.4 %shard_map.38 = (bf16[192,3072]{1,0:T(8,128)(2,1)}, bf16[192,3072]{1,0:T(8,128)(2,1)}) custom-call(s32[5]{0:T(128)} %stack.73.place_ref, bf16[1,384,6144]{2,1,0:T(8,128)(2,1)} %tokens_ref.2, f32[1,6144]{1,0:T(1,128)} %bitcast.42, bf16[6,1536,384]{2,1,0:T(8,128)(2,1)} %bitcast.31), custom_call_target="tpu_custom_call" | custom-call | flops 9437184 | bytes 4718592 | tf_op jit(solution)/shard_map/pallas_call | solution.py:120
  54.2 1.4 broadcast_select_fusion.2
  55.6 12.3 %collective-permute-done.4.refs_25_.refs_0_.refs_16_ = bf16[192,3072]{1,0:T(8,128)(2,1)} collective-permute-done((bf16[192,3072]{1,0:T(8,128)(2,1)}, bf16[192,3072]{1,0:T(8,128)(2,1)}, u32[]{:S(2)}, u32[]{:S(2)}) %collective-permute-start.4) | collective-permute-done | bytes 1179680 | tf_op jit(solution)/shard_map/ppermute | solution.py:468
  68.1 0.6 collective-permute-start.13
  68.6 4.6 %collective-permute-start.10 = (bf16[192,3072]{1,0:T(8,128)(2,1)S(1)}, bf16[192,3072]{1,0:T(8,128)(2,1)S(1)}, u32[]{:S(2)}, u32[]{:S(2)}) collective-permute-start(bf16[192,3072]{1,0:T(8,128)(2,1)S(1)} %broadcast_select_fusion.2), channel_id=1, source_target_pairs={{0,4},{4,0},{8,12},{12,8},{1,5},{5,1},{9,13},{13,9},{2,6},{6,2},{1... | collective-permute-start | bytes 3538952 | tf_op jit(solution)/shard_map/ppermute | solution.py:468
  73.2 0.7 collective-permute-start.11
  74.0 0.9 collective-permute-start.12
  74.9 1.2 broadcast_select_fusion.1
  76.1 23.4 %collective-permute-done.10.refs_28_.refs_1_.refs_17_ = bf16[192,3072]{1,0:T(8,128)(2,1)S(1)} collective-permute-done((bf16[192,3072]{1,0:T(8,128)(2,1)S(1)}, bf16[192,3072]{1,0:T(8,128)(2,1)S(1)}, u32[]{:S(2)}, u32[]{:S(2)}) %collective-permute-start.10) | collective-permute-done | bytes 1179680 | tf_op jit(solution)/shard_map/ppermute | solution.py:468
  99.5 2.5 %collective-permute-done.12.refs_4_.refs_12_ = bf16[192,3072]{1,0:T(8,128)(2,1)S(1)} collective-permute-done((bf16[192,3072]{1,0:T(8,128)(2,1)}, bf16[192,3072]{1,0:T(8,128)(2,1)S(1)}, u32[]{:S(2)}, u32[]{:S(2)}) %collective-permute-start.12) | collective-permute-done | bytes 1179680 | tf_op jit(solution)/shard_map/ppermute | solution.py:477
  102.0 1.0 copy-done.6
  103.0 0.8 collective-permute-start.18
  103.8 1.5 collective-permute-start.19
  105.4 2.9 %collective-permute-start.16 = (bf16[1536,384]{1,0:T(8,128)(2,1)}, bf16[1536,384]{1,0:T(8,128)(2,1)}, u32[]{:S(2)}, u32[]{:S(2)}) collective-permute-start(bf16[1536,384]{1,0:T(8,128)(2,1)} %broadcast_select_fusion.1), channel_id=1, source_target_pairs={{0,4},{4,0},{8,12},{12,8},{1,5},{5,1},{9,13},{13,9},{2,6},{6,2},{1... | collective-permute-start | bytes 3538952 | tf_op jit(solution)/shard_map/ppermute | solution.py:468
  108.3 1.7 collective-permute-start.17
  110.0 1.0 copy-done.8
  111.0 2.8 %pad_maximum_fusion = bf16[384,3072]{1,0:T(8,128)(2,1)} fusion(bf16[192,3072]{1,0:T(8,128)(2,1)S(1)} %collective-permute-done.10.refs_28_.refs_1_.refs_17_, bf16[192,3072]{1,0:T(8,128)(2,1)} %collective-permute-done.4.refs_25_.refs_0_.refs_16_), kind=kLoop, calls=%fused_computation | loop fusion | flops 4718592 | bytes 4718592 | tf_op jit(solution)/shard_map/concatenate | solution.py:554
  113.8 2.5 %broadcast_select_fusion = bf16[1536,384]{1,0:T(8,128)(2,1)} fusion(bf16[1536,384]{1,0:T(8,128)(2,1)S(1)} %collective-permute-done.11.refs_14_.refs_22_, bf16[1536,384]{1,0:T(8,128)(2,1)} %get-tuple-element.210.refs_11_.refs_19_.refs_10_, pred[]{:T(512)S(6)} %or.4), kind=kLoop, calls=%fused_computation.2 | loop fusion | flops 589824 | bytes 3538945 | tf_op jit(solution)/shard_map/jit(_where)/select_n | solution.py:465
  116.3 14.6 %shard_map.39 = (bf16[384,128]{1,0:T(8,128)(2,1)}, bf16[384,128]{1,0:T(8,128)(2,1)}, f32[768,384]{1,0:T(8,128)}, f32[768,384]{1,0:T(8,128)}) custom-call(s32[2]{0:T(128)} %pad_add_fusion.role_ref, bf16[192,3072]{1,0:T(8,128)(2,1)} %get-tuple-element.124.refs_0_.refs_8_, bf16[192,3072]{1,0:T(8,128)(2,1)} %get-tuple-element.132.refs_1_.refs_9_, ...), custom_call_target="tpu_custom_call" | custom-call | flops 6341787648 | tf_op jit(solution)/shard_map/pallas_call | solution.py:378
  130.9 3.8 %collective-permute-done.16.refs_27_.refs_17_ = bf16[1536,384]{1,0:T(8,128)(2,1)} collective-permute-done((bf16[1536,384]{1,0:T(8,128)(2,1)}, bf16[1536,384]{1,0:T(8,128)(2,1)}, u32[]{:S(2)}, u32[]{:S(2)}) %collective-permute-start.16) | collective-permute-done | bytes 1179680 | tf_op jit(solution)/shard_map/ppermute | solution.py:468
  134.8 1.2 collective-permute-start.24
  136.5 3.6 %collective-permute-start.22 = (bf16[1536,384]{1,0:T(8,128)(2,1)}, bf16[1536,384]{1,0:T(8,128)(2,1)}, u32[]{:S(2)}, u32[]{:S(2)}) collective-permute-start(bf16[1536,384]{1,0:T(8,128)(2,1)} %broadcast_select_fusion), channel_id=1, source_target_pairs={{0,4},{4,0},{8,12},{12,8},{1,5},{5,1},{9,13},{13,9},{2,6},{6,2},{1... | collective-permute-start | bytes 3538952 | tf_op jit(solution)/shard_map/ppermute | solution.py:468
  140.2 1.7 collective-permute-start.23
  141.9 20.0 %shard_map.40 = (bf16[384,128]{1,0:T(8,128)(2,1)}, bf16[384,128]{1,0:T(8,128)(2,1)}, f32[768,384]{1,0:T(8,128)}, f32[768,384]{1,0:T(8,128)}, f32[768,384]{1,0:T(8,128)}, /*index=5*/f32[768,384]{1,0:T(8,128)}) custom-call(s32[2]{0:T(128)} %pad_add_fusion.role_ref, bf16[192,3072]{1,0:T(8,128)(2,1)} %collective-permute-done.1.refs_0_.refs_8_, ...), custom_call_target="tpu_custom_call" | custom-call | flops 9965666304 | tf_op jit(solution)/shard_map/pallas_call | solution.py:378
  161.9 4.6 %collective-permute-done.22.refs_18_.refs_8_ = bf16[1536,384]{1,0:T(8,128)(2,1)} collective-permute-done((bf16[1536,384]{1,0:T(8,128)(2,1)}, bf16[1536,384]{1,0:T(8,128)(2,1)}, u32[]{:S(2)}, u32[]{:S(2)}) %collective-permute-start.22) | collective-permute-done | bytes 1179680 | tf_op jit(solution)/shard_map/ppermute | solution.py:468
  166.6 1.6 collective-permute-start.32
  168.2 1.3 collective-permute-start.29
  169.4 1.7 collective-permute-start.30
  171.1 0.8 collective-permute-start.31
  172.0 13.1 %shard_map.41 = (bf16[384,128]{1,0:T(8,128)(2,1)}, bf16[384,128]{1,0:T(8,128)(2,1)}, f32[768,384]{1,0:T(8,128)}, bf16[384,128]{1,0:T(8,128)(2,1)}, bf16[384,128]{1,0:T(8,128)(2,1)}, /*index=5*/f32[768,384]{1,0:T(8,128)}) custom-call(s32[2]{0:T(128)} %pad_add_fusion.role_ref, bf16[192,3072]{1,0:T(8,128)(2,1)} %get-tuple-element.124.refs_0_.refs_8_, ...), custom_call_target="tpu_custom_call" | custom-call | flops 3623878656 | tf_op jit(solution)/shard_map/pallas_call | solution.py:378
  185.1 8.8 %shard_map.42.refs_28_ = f32[768,384]{1,0:T(8,128)} custom-call(s32[2]{0:T(128)} %pad_add_fusion.role_ref, bf16[192,3072]{1,0:T(8,128)(2,1)} %collective-permute-done.4.refs_25_.refs_0_.refs_16_, bf16[192,3072]{1,0:T(8,128)(2,1)} %copy-done.2, bf16[384,3072]{1,0:T(8,128)(2,1)} %collective-permute-done.26.refs_2_.refs_3_.refs_18_.refs_19_, ...), custom_call_target="tpu_custom_call" | custom-call | flops 2717908992 | tf_op jit(solution)/shard_map/pallas_call | solution.py:378
  193.8 5.8 %collective-permute-done.29.refs_25_ = bf16[1536,384]{1,0:T(8,128)(2,1)} collective-permute-done((bf16[1536,384]{1,0:T(8,128)(2,1)}, bf16[1536,384]{1,0:T(8,128)(2,1)}, u32[]{:S(2)}, u32[]{:S(2)}) %collective-permute-start.29) | collective-permute-done | bytes 1179680 | tf_op jit(solution)/shard_map/ppermute | solution.py:471
  200.3 12.8 %shard_map.43 = (bf16[384,384]{1,0:T(8,128)(2,1)}, bf16[384,384]{1,0:T(8,128)(2,1)}, bf16[384,384]{1,0:T(8,128)(2,1)}, bf16[384,384]{1,0:T(8,128)(2,1)}, bf16[38...) custom-call(s32[2]{0:T(128)} %pad_add_fusion.role_ref, bf16[192,3072]{1,0:T(8,128)(2,1)} %get-tuple-element.124.refs_0_.refs_8_, ...), custom_call_target="tpu_custom_call" | custom-call | flops 2717908992 | tf_op jit(solution)/shard_map/pallas_call | solution.py:378
  213.2 0.9 collective-permute-start.34
  214.6 2.1 collective-permute-start.36
  216.7 1.3 collective-permute-start.37
  218.0 1.6 collective-permute-start.38
  219.6 11.2 %shard_map.44 = (bf16[384,128]{1,0:T(8,128)(2,1)}, bf16[384,128]{1,0:T(8,128)(2,1)}) custom-call(s32[2]{0:T(128)} %pad_add_fusion.role_ref, bf16[192,3072]{1,0:T(8,128)(2,1)} %collective-permute-done.19.refs_0_, bf16[192,3072]{1,0:T(8,128)(2,1)} %collective-permute-done.25.refs_1_, bf16[192,3072]{1,0:T(8,128)(2,1)} %collective-permute-done.33.refs_2_, ...), custom_call_target="tpu_custom_call" | custom-call | flops 3623878656 | tf_op jit(solution)/shard_map/pallas_call | solution.py:378
  230.8 1.3 collective-permute-start.42
  232.1 1.3 collective-permute-start.43
  233.5 0.6 stack.63.place_ref
  234.1 6.5 %collective-permute-done.42.refs_6_ = bf16[384,128]{1,0:T(8,128)(2,1)S(1)} collective-permute-done((bf16[384,128]{1,0:T(8,128)(2,1)}, bf16[384,128]{1,0:T(8,128)(2,1)S(1)}, u32[]{:S(2)}, u32[]{:S(2)}) %collective-permute-start.42) | collective-permute-done | bytes 98336 | tf_op jit(solution)/shard_map/ppermute | solution.py:636
  240.6 1.6 collective-permute-done.43.refs_7_
  242.2 0.6 copy-done.17
  242.8 3.1 %shard_map.45 = bf16[384,1536]{1,0:T(8,128)(2,1)} custom-call(s32[5]{0:T(128)} %stack.63.place_ref, bf16[384,384]{1,0:T(8,128)(2,1)} %get-tuple-element.225.refs_0_, bf16[384,384]{1,0:T(8,128)(2,1)} %copy-done.12, bf16[384,384]{1,0:T(8,128)(2,1)} %copy-done.13, bf16[384,384]{1,0:T(8,128)(2,1)} %collective-permute-done.36.refs_3_, ...), custom_call_target="tpu_custom_call" | custom-call | bytes 2359296 | tf_op jit(solution)/shard_map/pallas_call | solution.py:439
  (81 shorter events, 2.2 us)
Async XLA Ops:
  6.4 29.2 %collective-permute-start = (bf16[192,3072]{1,0:T(8,128)(2,1)}, bf16[192,3072]{1,0:T(8,128)(2,1)S(1)}, u32[]{:S(2)}, u32[]{:S(2)}) collective-permute-start(bf16[192,3072]{1,0:T(8,128)(2,1)} %get-tuple-element.124.refs_0_.refs_8_), channel_id=1, source_target_pairs={{0,2},{2,0},{1,3},{3,1},{4,6},{6,4},{5,7},{7,5},{8,10},{10,8},{9,1... | collective-permute-start | bytes 3538952 | tf_op jit(solution)/shard_map/ppermute | solution.py:477
  9.4 27.7 %collective-permute-start.1 = (bf16[192,3072]{1,0:T(8,128)(2,1)}, bf16[192,3072]{1,0:T(8,128)(2,1)}, u32[]{:S(2)}, u32[]{:S(2)}) collective-permute-start(bf16[192,3072]{1,0:T(8,128)(2,1)} %get-tuple-element.124.refs_0_.refs_8_), channel_id=1, source_target_pairs={{0,16},{16,0},{1,17},{17,1},{2,18},{18,2},{3,19},{19,3},{4,20},{20... | collective-permute-start | bytes 3538952 | tf_op jit(solution)/shard_map/ppermute | solution.py:478
  10.9 28.9 %collective-permute-start.2 = (bf16[1536,384]{1,0:T(8,128)(2,1)}, bf16[1536,384]{1,0:T(8,128)(2,1)}, u32[]{:S(2)}, u32[]{:S(2)}) collective-permute-start(bf16[1536,384]{1,0:T(8,128)(2,1)} %get-tuple-element.128.refs_8_.refs_10_.refs_16_.refs_18_), channel_id=1, source_target_pairs={{0,4},{4,0},{8,12},{12,8},{1,5},{5,1},{9,13},{13,9},{2,6},{6,2},{1... | collective-permute-start | bytes 3538952 | tf_op jit(solution)/shard_map/ppermute | solution.py:468
  12.5 27.4 %collective-permute-start.3 = (bf16[1536,384]{1,0:T(8,128)(2,1)}, bf16[1536,384]{1,0:T(8,128)(2,1)}, u32[]{:S(2)}, u32[]{:S(2)}) collective-permute-start(bf16[1536,384]{1,0:T(8,128)(2,1)} %get-tuple-element.128.refs_8_.refs_10_.refs_16_.refs_18_), channel_id=1, source_target_pairs={{4,8},{8,4},{5,9},{9,5},{6,10},{10,6},{7,11},{11,7},{20,24},{24,20... | collective-permute-start | bytes 3538952 | tf_op jit(solution)/shard_map/ppermute | solution.py:474
  17.0 57.8 %copy-start = (bf16[1,1536,384]{2,1,0:T(8,128)(2,1)}, bf16[1,1536,384]{2,1,0:T(8,128)(2,1)S(1)}, u32[]{:S(2)}) copy-start(bf16[1,1536,384]{2,1,0:T(8,128)(2,1)S(1)} %get-tuple-element.238) | copy-start | bytes 3538948
  17.0 1.7 copy-start.1
  35.5 1.6 copy-start.4
  37.1 7.5 %collective-permute-start.8 = (bf16[192,3072]{1,0:T(8,128)(2,1)S(1)}, bf16[192,3072]{1,0:T(8,128)(2,1)S(1)}, u32[]{:S(2)}, u32[]{:S(2)}) collective-permute-start(bf16[192,3072]{1,0:T(8,128)(2,1)S(1)} %collective-permute-done.refs_4_.refs_12_), channel_id=1, source_target_pairs={{0,1},{1,0},{2,3},{3,2},{4,5},{5,4},{6,7},{7,6},{8,9},{9,8},{10,11... | collective-permute-start | bytes 3538952 | tf_op jit(solution)/shard_map/ppermute | solution.py:485
  37.1 30.9 %collective-permute-start.6 = (bf16[192,3072]{1,0:T(8,128)(2,1)}, bf16[192,3072]{1,0:T(8,128)(2,1)}, u32[]{:S(2)}, u32[]{:S(2)}) collective-permute-start(bf16[192,3072]{1,0:T(8,128)(2,1)} %get-tuple-element.132.refs_1_.refs_9_), channel_id=1, source_target_pairs={{0,2},{2,0},{1,3},{3,1},{4,6},{6,4},{5,7},{7,5},{8,10},{10,8},{9,1... | collective-permute-start | bytes 3538952 | tf_op jit(solution)/shard_map/ppermute | solution.py:477
  38.3 29.7 %collective-permute-start.7 = (bf16[192,3072]{1,0:T(8,128)(2,1)}, bf16[192,3072]{1,0:T(8,128)(2,1)}, u32[]{:S(2)}, u32[]{:S(2)}) collective-permute-start(bf16[192,3072]{1,0:T(8,128)(2,1)} %get-tuple-element.132.refs_1_.refs_9_), channel_id=1, source_target_pairs={{0,16},{16,0},{1,17},{17,1},{2,18},{18,2},{3,19},{19,3},{4,20},{20... | collective-permute-start | bytes 3538952 | tf_op jit(solution)/shard_map/ppermute | solution.py:478
  39.8 28.1 %collective-permute-start.4 = (bf16[192,3072]{1,0:T(8,128)(2,1)}, bf16[192,3072]{1,0:T(8,128)(2,1)}, u32[]{:S(2)}, u32[]{:S(2)}) collective-permute-start(bf16[192,3072]{1,0:T(8,128)(2,1)} %broadcast_select_fusion.3), channel_id=1, source_target_pairs={{0,4},{4,0},{8,12},{12,8},{1,5},{5,1},{9,13},{13,9},{2,6},{6,2},{1... | collective-permute-start | bytes 3538952 | tf_op jit(solution)/shard_map/ppermute | solution.py:468
  42.9 25.0 %collective-permute-start.5 = (bf16[1536,384]{1,0:T(8,128)(2,1)}, bf16[1536,384]{1,0:T(8,128)(2,1)}, u32[]{:S(2)}, u32[]{:S(2)}) collective-permute-start(bf16[1536,384]{1,0:T(8,128)(2,1)} %collective-permute-done.2.refs_15_.refs_16_.refs_23_.refs_26_), channel_id=1, source_target_pairs={{4,8},{8,4},{5,9},{9,5},{6,10},{10,6},{7,11},{11,7},{20,24},{24,20... | collective-permute-start | bytes 3538952 | tf_op jit(solution)/shard_map/ppermute | solution.py:474
  44.6 1.1 copy-start.5
  45.7 22.3 %collective-permute-start.9 = (bf16[192,3072]{1,0:T(8,128)(2,1)}, bf16[192,3072]{1,0:T(8,128)(2,1)}, u32[]{:S(2)}, u32[]{:S(2)}) collective-permute-start(bf16[192,3072]{1,0:T(8,128)(2,1)} %collective-permute-done.1.refs_0_.refs_8_), channel_id=1, source_target_pairs={{0,1},{1,0},{2,3},{3,2},{4,5},{5,4},{6,7},{7,6},{8,9},{9,8},{10,11... | collective-permute-start | bytes 3538952 | tf_op jit(solution)/shard_map/ppermute | solution.py:485
  68.0 6.9 %collective-permute-start.14 = (bf16[192,3072]{1,0:T(8,128)(2,1)}, bf16[192,3072]{1,0:T(8,128)(2,1)}, u32[]{:S(2)}, u32[]{:S(2)}) collective-permute-start(bf16[192,3072]{1,0:T(8,128)(2,1)} %collective-permute-done.6.refs_5_.refs_13_), channel_id=1, source_target_pairs={{0,1},{1,0},{2,3},{3,2},{4,5},{5,4},{6,7},{7,6},{8,9},{9,8},{10,11... | collective-permute-start | bytes 3538952 | tf_op jit(solution)/shard_map/ppermute | solution.py:485
  68.1 33.9 %collective-permute-start.13 = (bf16[192,3072]{1,0:T(8,128)(2,1)}, bf16[192,3072]{1,0:T(8,128)(2,1)}, u32[]{:S(2)}, u32[]{:S(2)}) collective-permute-start(bf16[192,3072]{1,0:T(8,128)(2,1)} %collective-permute-done.6.refs_5_.refs_13_), channel_id=1, source_target_pairs={{0,16},{16,0},{1,17},{17,1},{2,18},{18,2},{3,19},{19,3},{4,20},{20... | collective-permute-start | bytes 3538952 | tf_op jit(solution)/shard_map/ppermute | solution.py:478
  68.6 30.9 %collective-permute-start.10 = (bf16[192,3072]{1,0:T(8,128)(2,1)S(1)}, bf16[192,3072]{1,0:T(8,128)(2,1)S(1)}, u32[]{:S(2)}, u32[]{:S(2)}) collective-permute-start(bf16[192,3072]{1,0:T(8,128)(2,1)S(1)} %broadcast_select_fusion.2), channel_id=1, source_target_pairs={{0,4},{4,0},{8,12},{12,8},{1,5},{5,1},{9,13},{13,9},{2,6},{6,2},{1... | collective-permute-start | bytes 3538952 | tf_op jit(solution)/shard_map/ppermute | solution.py:468
  73.2 26.3 %collective-permute-start.11 = (bf16[1536,384]{1,0:T(8,128)(2,1)S(1)}, bf16[1536,384]{1,0:T(8,128)(2,1)S(1)}, u32[]{:S(2)}, u32[]{:S(2)}) collective-permute-start(bf16[1536,384]{1,0:T(8,128)(2,1)S(1)} %bitcast.33), channel_id=1, source_target_pairs={{4,8},{8,4},{5,9},{9,5},{6,10},{10,6},{7,11},{11,7},{20,24},{24,20... | collective-permute-start | bytes 3538952 | tf_op jit(solution)/shard_map/ppermute | solution.py:474
  74.0 28.0 %collective-permute-start.12 = (bf16[192,3072]{1,0:T(8,128)(2,1)}, bf16[192,3072]{1,0:T(8,128)(2,1)S(1)}, u32[]{:S(2)}, u32[]{:S(2)}) collective-permute-start(bf16[192,3072]{1,0:T(8,128)(2,1)} %collective-permute-done.1.refs_0_.refs_8_), channel_id=1, source_target_pairs={{0,2},{2,0},{1,3},{3,1},{4,6},{6,4},{5,7},{7,5},{8,10},{10,8},{9,1... | collective-permute-start | bytes 3538952 | tf_op jit(solution)/shard_map/ppermute | solution.py:477
  74.9 27.1 %collective-permute-start.15 = (bf16[192,3072]{1,0:T(8,128)(2,1)}, bf16[192,3072]{1,0:T(8,128)(2,1)S(1)}, u32[]{:S(2)}, u32[]{:S(2)}) collective-permute-start(bf16[192,3072]{1,0:T(8,128)(2,1)} %collective-permute-done.7.refs_1_.refs_9_), channel_id=1, source_target_pairs={{0,1},{1,0},{2,3},{3,2},{4,5},{5,4},{6,7},{7,6},{8,9},{9,8},{10,11... | collective-permute-start | bytes 3538952 | tf_op jit(solution)/shard_map/ppermute | solution.py:485
  99.5 14.3 %copy-start.2 = (bf16[192,3072]{1,0:T(8,128)(2,1)}, bf16[192,3072]{1,0:T(8,128)(2,1)S(1)}, u32[]{:S(2)}) copy-start(bf16[192,3072]{1,0:T(8,128)(2,1)S(1)} %collective-permute-done.10.refs_28_.refs_1_.refs_17_) | copy-start | bytes 3538948
  99.5 14.3 %copy-start.10 = (bf16[1536,384]{1,0:T(8,128)(2,1)}, bf16[1536,384]{1,0:T(8,128)(2,1)S(1)}, u32[]{:S(2)}) copy-start(bf16[1536,384]{1,0:T(8,128)(2,1)S(1)} %collective-permute-done.11.refs_14_.refs_22_) | copy-start | bytes 3538948
  102.0 1.0 copy-start.6
  103.0 7.0 %copy-start.7 = (bf16[192,3072]{1,0:T(8,128)(2,1)}, bf16[192,3072]{1,0:T(8,128)(2,1)S(1)}, u32[]{:S(2)}) copy-start(bf16[192,3072]{1,0:T(8,128)(2,1)S(1)} %collective-permute-done.15.refs_3_.refs_11_) | copy-start | bytes 3538948
  103.0 7.0 %collective-permute-start.20 = (bf16[192,3072]{1,0:T(8,128)(2,1)S(1)}, bf16[192,3072]{1,0:T(8,128)(2,1)S(1)}, u32[]{:S(2)}, u32[]{:S(2)}) collective-permute-start(bf16[192,3072]{1,0:T(8,128)(2,1)S(1)} %collective-permute-done.12.refs_4_.refs_12_), channel_id=1, source_target_pairs={{0,1},{1,0},{2,3},{3,2},{4,5},{5,4},{6,7},{7,6},{8,9},{9,8},{10,11... | collective-permute-start | bytes 3538952 | tf_op jit(solution)/shard_map/ppermute | solution.py:485
  103.0 31.7 %collective-permute-start.18 = (bf16[192,3072]{1,0:T(8,128)(2,1)}, bf16[192,3072]{1,0:T(8,128)(2,1)}, u32[]{:S(2)}, u32[]{:S(2)}) collective-permute-start(bf16[192,3072]{1,0:T(8,128)(2,1)} %collective-permute-done.4.refs_25_.refs_0_.refs_16_), channel_id=1, source_target_pairs={{0,2},{2,0},{1,3},{3,1},{4,6},{6,4},{5,7},{7,5},{8,10},{10,8},{9,1... | collective-permute-start | bytes 3538952 | tf_op jit(solution)/shard_map/ppermute | solution.py:477
  103.8 30.8 %collective-permute-start.19 = (bf16[192,3072]{1,0:T(8,128)(2,1)}, bf16[192,3072]{1,0:T(8,128)(2,1)}, u32[]{:S(2)}, u32[]{:S(2)}) collective-permute-start(bf16[192,3072]{1,0:T(8,128)(2,1)} %collective-permute-done.4.refs_25_.refs_0_.refs_16_), channel_id=1, source_target_pairs={{0,16},{16,0},{1,17},{17,1},{2,18},{18,2},{3,19},{19,3},{4,20},{20... | collective-permute-start | bytes 3538952 | tf_op jit(solution)/shard_map/ppermute | solution.py:478
  105.4 29.3 %collective-permute-start.16 = (bf16[1536,384]{1,0:T(8,128)(2,1)}, bf16[1536,384]{1,0:T(8,128)(2,1)}, u32[]{:S(2)}, u32[]{:S(2)}) collective-permute-start(bf16[1536,384]{1,0:T(8,128)(2,1)} %broadcast_select_fusion.1), channel_id=1, source_target_pairs={{0,4},{4,0},{8,12},{12,8},{1,5},{5,1},{9,13},{13,9},{2,6},{6,2},{1... | collective-permute-start | bytes 3538952 | tf_op jit(solution)/shard_map/ppermute | solution.py:468
  108.3 26.4 %collective-permute-start.17 = (bf16[1536,384]{1,0:T(8,128)(2,1)}, bf16[1536,384]{1,0:T(8,128)(2,1)}, u32[]{:S(2)}, u32[]{:S(2)}) collective-permute-start(bf16[1536,384]{1,0:T(8,128)(2,1)} %get-tuple-element.210.refs_11_.refs_19_.refs_10_), channel_id=1, source_target_pairs={{4,8},{8,4},{5,9},{9,5},{6,10},{10,6},{7,11},{11,7},{20,24},{24,20... | collective-permute-start | bytes 3538952 | tf_op jit(solution)/shard_map/ppermute | solution.py:474
  110.0 1.0 copy-start.8
  111.0 23.7 %collective-permute-start.21 = (bf16[192,3072]{1,0:T(8,128)(2,1)}, bf16[192,3072]{1,0:T(8,128)(2,1)}, u32[]{:S(2)}, u32[]{:S(2)}) collective-permute-start(bf16[192,3072]{1,0:T(8,128)(2,1)} %collective-permute-done.13.refs_5_.refs_13_), channel_id=1, source_target_pairs={{0,1},{1,0},{2,3},{3,2},{4,5},{5,4},{6,7},{7,6},{8,9},{9,8},{10,11... | collective-permute-start | bytes 3538952 | tf_op jit(solution)/shard_map/ppermute | solution.py:485
  116.3 18.5 %copy-start.3 = (bf16[192,3072]{1,0:T(8,128)(2,1)S(1)}, bf16[192,3072]{1,0:T(8,128)(2,1)}, u32[]{:S(2)}) copy-start(bf16[192,3072]{1,0:T(8,128)(2,1)} %copy-done.2) | copy-start | bytes 3538948
  134.7 7.2 %collective-permute-start.26 = (bf16[384,3072]{1,0:T(8,128)(2,1)}, bf16[384,3072]{1,0:T(8,128)(2,1)}, u32[]{:S(2)}, u32[]{:S(2)}) collective-permute-start(bf16[384,3072]{1,0:T(8,128)(2,1)} %pad_maximum_fusion), channel_id=1, source_target_pairs={{0,1},{1,0},{2,3},{3,2},{4,5},{5,4},{6,7},{7,6},{8,9},{9,8},{10,11... | collective-permute-start | bytes 7077896 | tf_op jit(solution)/shard_map/ppermute | solution.py:485
  134.8 31.7 %collective-permute-start.24 = (bf16[192,3072]{1,0:T(8,128)(2,1)S(1)}, bf16[192,3072]{1,0:T(8,128)(2,1)}, u32[]{:S(2)}, u32[]{:S(2)}) collective-permute-start(bf16[192,3072]{1,0:T(8,128)(2,1)S(1)} %copy-done.3), channel_id=1, source_target_pairs={{0,2},{2,0},{1,3},{3,1},{4,6},{6,4},{5,7},{7,5},{8,10},{10,8},{9,1... | collective-permute-start | bytes 3538952 | tf_op jit(solution)/shard_map/ppermute | solution.py:477
  136.0 30.5 %collective-permute-start.25 = (bf16[192,3072]{1,0:T(8,128)(2,1)S(1)}, bf16[192,3072]{1,0:T(8,128)(2,1)}, u32[]{:S(2)}, u32[]{:S(2)}) collective-permute-start(bf16[192,3072]{1,0:T(8,128)(2,1)S(1)} %copy-done.3), channel_id=1, source_target_pairs={{0,16},{16,0},{1,17},{17,1},{2,18},{18,2},{3,19},{19,3},{4,20},{20... | collective-permute-start | bytes 3538952 | tf_op jit(solution)/shard_map/ppermute | solution.py:478
  136.5 29.9 %collective-permute-start.22 = (bf16[1536,384]{1,0:T(8,128)(2,1)}, bf16[1536,384]{1,0:T(8,128)(2,1)}, u32[]{:S(2)}, u32[]{:S(2)}) collective-permute-start(bf16[1536,384]{1,0:T(8,128)(2,1)} %broadcast_select_fusion), channel_id=1, source_target_pairs={{0,4},{4,0},{8,12},{12,8},{1,5},{5,1},{9,13},{13,9},{2,6},{6,2},{1... | collective-permute-start | bytes 3538952 | tf_op jit(solution)/shard_map/ppermute | solution.py:468
  140.2 26.3 %collective-permute-start.23 = (bf16[1536,384]{1,0:T(8,128)(2,1)}, bf16[1536,384]{1,0:T(8,128)(2,1)}, u32[]{:S(2)}, u32[]{:S(2)}) collective-permute-start(bf16[1536,384]{1,0:T(8,128)(2,1)} %collective-permute-done.16.refs_27_.refs_17_), channel_id=1, source_target_pairs={{4,8},{8,4},{5,9},{9,5},{6,10},{10,6},{7,11},{11,7},{20,24},{24,20... | collective-permute-start | bytes 3538952 | tf_op jit(solution)/shard_map/ppermute | solution.py:474
  141.9 24.6 %collective-permute-start.27 = (bf16[192,3072]{1,0:T(8,128)(2,1)}, bf16[192,3072]{1,0:T(8,128)(2,1)}, u32[]{:S(2)}, u32[]{:S(2)}) collective-permute-start(bf16[192,3072]{1,0:T(8,128)(2,1)} %collective-permute-done.18.refs_4_.refs_20_), channel_id=1, source_target_pairs={{0,1},{1,0},{2,3},{3,2},{4,5},{5,4},{6,7},{7,6},{8,9},{9,8},{10,11... | collective-permute-start | bytes 3538952 | tf_op jit(solution)/shard_map/ppermute | solution.py:485
  166.5 5.5 %collective-permute-start.28 = (bf16[192,3072]{1,0:T(8,128)(2,1)}, bf16[192,3072]{1,0:T(8,128)(2,1)S(1)}, u32[]{:S(2)}, u32[]{:S(2)}) collective-permute-start(bf16[192,3072]{1,0:T(8,128)(2,1)} %collective-permute-done.24.refs_5_.refs_21_), channel_id=1, source_target_pairs={{0,1},{1,0},{2,3},{3,2},{4,5},{5,4},{6,7},{7,6},{8,9},{9,8},{10,11... | collective-permute-start | bytes 3538952 | tf_op jit(solution)/shard_map/ppermute | solution.py:485
  166.6 33.1 %collective-permute-start.32 = (bf16[192,3072]{1,0:T(8,128)(2,1)}, bf16[192,3072]{1,0:T(8,128)(2,1)}, u32[]{:S(2)}, u32[]{:S(2)}) collective-permute-start(bf16[192,3072]{1,0:T(8,128)(2,1)} %collective-permute-done.24.refs_5_.refs_21_), channel_id=1, source_target_pairs={{0,16},{16,0},{1,17},{17,1},{2,18},{18,2},{3,19},{19,3},{4,20},{20... | collective-permute-start | bytes 3538952 | tf_op jit(solution)/shard_map/ppermute | solution.py:478
  168.2 31.5 %collective-permute-start.29 = (bf16[1536,384]{1,0:T(8,128)(2,1)}, bf16[1536,384]{1,0:T(8,128)(2,1)}, u32[]{:S(2)}, u32[]{:S(2)}) collective-permute-start(bf16[1536,384]{1,0:T(8,128)(2,1)} %collective-permute-done.23.refs_16_), channel_id=1, source_target_pairs={{4,0},{8,12},{5,1},{9,13},{6,2},{10,14},{7,3},{11,15},{20,16},{24,... | collective-permute-start | bytes 3538952 | tf_op jit(solution)/shard_map/ppermute | solution.py:471
  169.4 30.2 %collective-permute-start.30 = (bf16[1536,384]{1,0:T(8,128)(2,1)}, bf16[1536,384]{1,0:T(8,128)(2,1)}, u32[]{:S(2)}, u32[]{:S(2)}) collective-permute-start(bf16[1536,384]{1,0:T(8,128)(2,1)} %collective-permute-done.22.refs_18_.refs_8_), channel_id=1, source_target_pairs={{4,8},{8,4},{5,9},{9,5},{6,10},{10,6},{7,11},{11,7},{20,24},{24,20... | collective-permute-start | bytes 3538952 | tf_op jit(solution)/shard_map/ppermute | solution.py:474
  171.1 28.5 %collective-permute-start.31 = (bf16[192,3072]{1,0:T(8,128)(2,1)}, bf16[192,3072]{1,0:T(8,128)(2,1)}, u32[]{:S(2)}, u32[]{:S(2)}) collective-permute-start(bf16[192,3072]{1,0:T(8,128)(2,1)} %collective-permute-done.19.refs_0_), channel_id=1, source_target_pairs={{0,2},{2,0},{1,3},{3,1},{4,6},{6,4},{5,7},{7,5},{8,10},{10,8},{9,1... | collective-permute-start | bytes 3538952 | tf_op jit(solution)/shard_map/ppermute | solution.py:477
  172.0 13.1 %copy-start.9 = (bf16[192,3072]{1,0:T(8,128)(2,1)}, bf16[192,3072]{1,0:T(8,128)(2,1)S(1)}, u32[]{:S(2)}) copy-start(bf16[192,3072]{1,0:T(8,128)(2,1)S(1)} %collective-permute-done.28.refs_7_.refs_23_) | copy-start | bytes 3538948
  172.0 27.7 %collective-permute-start.33 = (bf16[192,3072]{1,0:T(8,128)(2,1)}, bf16[192,3072]{1,0:T(8,128)(2,1)}, u32[]{:S(2)}, u32[]{:S(2)}) collective-permute-start(bf16[192,3072]{1,0:T(8,128)(2,1)} %collective-permute-done.19.refs_0_), channel_id=1, source_target_pairs={{0,1},{1,0},{2,3},{3,2},{4,5},{5,4},{6,7},{7,6},{8,9},{9,8},{10,11... | collective-permute-start | bytes 3538952 | tf_op jit(solution)/shard_map/ppermute | solution.py:485
  199.7 14.9 %collective-permute-start.39 = (bf16[192,3072]{1,0:T(8,128)(2,1)}, bf16[192,3072]{1,0:T(8,128)(2,1)S(1)}, u32[]{:S(2)}, u32[]{:S(2)}) collective-permute-start(bf16[192,3072]{1,0:T(8,128)(2,1)} %collective-permute-done.25.refs_1_), channel_id=1, source_target_pairs={{0,1},{1,0},{2,3},{3,2},{4,5},{5,4},{6,7},{7,6},{8,9},{9,8},{10,11... | collective-permute-start | bytes 3538952 | tf_op jit(solution)/shard_map/ppermute | solution.py:607
  199.8 17.0 %collective-permute-start.40 = (bf16[192,3072]{1,0:T(8,128)(2,1)}, bf16[192,3072]{1,0:T(8,128)(2,1)}, u32[]{:S(2)}, u32[]{:S(2)}) collective-permute-start(bf16[192,3072]{1,0:T(8,128)(2,1)} %collective-permute-done.31.refs_4_), channel_id=1, source_target_pairs={{0,1},{1,0},{2,3},{3,2},{4,5},{5,4},{6,7},{7,6},{8,9},{9,8},{10,11... | collective-permute-start | bytes 3538952 | tf_op jit(solution)/shard_map/ppermute | solution.py:607
  200.3 17.8 %collective-permute-start.41 = (bf16[192,3072]{1,0:T(8,128)(2,1)}, bf16[192,3072]{1,0:T(8,128)(2,1)}, u32[]{:S(2)}, u32[]{:S(2)}) collective-permute-start(bf16[192,3072]{1,0:T(8,128)(2,1)} %collective-permute-done.32.refs_5_), channel_id=1, source_target_pairs={{0,1},{1,0},{2,3},{3,2},{4,5},{5,4},{6,7},{7,6},{8,9},{9,8},{10,11... | collective-permute-start | bytes 3538952 | tf_op jit(solution)/shard_map/ppermute | solution.py:607
  213.2 20.9 %collective-permute-start.34 = (bf16[384,384]{1,0:T(8,128)(2,1)}, bf16[384,384]{1,0:T(8,128)(2,1)S(1)}, u32[]{:S(2)}, u32[]{:S(2)}) collective-permute-start(bf16[384,384]{1,0:T(8,128)(2,1)} %get-tuple-element.226), channel_id=1, source_target_pairs={{0,2},{2,0},{16,18},{18,16},{1,3},{3,1},{17,19},{19,17},{4,6},{6,4... | collective-permute-start | bytes 884744 | tf_op jit(solution)/shard_map/ppermute | solution.py:500
  214.1 20.0 %collective-permute-start.35 = (bf16[384,384]{1,0:T(8,128)(2,1)}, bf16[384,384]{1,0:T(8,128)(2,1)S(1)}, u32[]{:S(2)}, u32[]{:S(2)}) collective-permute-start(bf16[384,384]{1,0:T(8,128)(2,1)} %get-tuple-element.227), channel_id=1, source_target_pairs={{0,16},{2,18},{16,0},{18,2},{1,17},{3,19},{17,1},{19,3},{4,20},{6,... | collective-permute-start | bytes 884744 | tf_op jit(solution)/shard_map/ppermute | solution.py:500
  214.6 5.0 %copy-start.11 = (bf16[192,3072]{1,0:T(8,128)(2,1)}, bf16[192,3072]{1,0:T(8,128)(2,1)S(1)}, u32[]{:S(2)}) copy-start(bf16[192,3072]{1,0:T(8,128)(2,1)S(1)} %collective-permute-done.39.refs_3_) | copy-start | bytes 3538948
  214.6 19.5 %collective-permute-start.36 = (bf16[384,384]{1,0:T(8,128)(2,1)}, bf16[384,384]{1,0:T(8,128)(2,1)}, u32[]{:S(2)}, u32[]{:S(2)}) collective-permute-start(bf16[384,384]{1,0:T(8,128)(2,1)} %get-tuple-element.228), channel_id=1, source_target_pairs={{0,18},{2,16},{16,2},{18,0},{1,19},{3,17},{17,3},{19,1},{4,22},{6,... | collective-permute-start | bytes 884744 | tf_op jit(solution)/shard_map/ppermute | solution.py:500
  216.7 14.1 %collective-permute-start.37 = (bf16[384,128]{1,0:T(8,128)(2,1)}, bf16[384,128]{1,0:T(8,128)(2,1)S(1)}, u32[]{:S(2)}, u32[]{:S(2)}) collective-permute-start(bf16[384,128]{1,0:T(8,128)(2,1)} %get-tuple-element.229), channel_id=1, source_target_pairs={{4,0},{6,2},{8,12},{10,14},{20,16},{22,18},{24,28},{26,30},{5,1},{... | collective-permute-start | bytes 294920 | tf_op jit(solution)/shard_map/ppermute | solution.py:636
  218.0 14.1 %collective-permute-start.38 = (bf16[384,128]{1,0:T(8,128)(2,1)}, bf16[384,128]{1,0:T(8,128)(2,1)S(1)}, u32[]{:S(2)}, u32[]{:S(2)}) collective-permute-start(bf16[384,128]{1,0:T(8,128)(2,1)} %get-tuple-element.230), channel_id=1, source_target_pairs={{4,2},{6,0},{8,14},{10,12},{20,18},{22,16},{24,30},{26,28},{5,3},{... | collective-permute-start | bytes 294920 | tf_op jit(solution)/shard_map/ppermute | solution.py:636
  230.8 11.4 %copy-start.14 = (bf16[384,128]{1,0:T(8,128)(2,1)}, bf16[384,128]{1,0:T(8,128)(2,1)S(1)}, u32[]{:S(2)}) copy-start(bf16[384,128]{1,0:T(8,128)(2,1)S(1)} %collective-permute-done.37.refs_4_) | copy-start | bytes 294916
  230.8 9.8 %collective-permute-start.42 = (bf16[384,128]{1,0:T(8,128)(2,1)}, bf16[384,128]{1,0:T(8,128)(2,1)S(1)}, u32[]{:S(2)}, u32[]{:S(2)}) collective-permute-start(bf16[384,128]{1,0:T(8,128)(2,1)} %get-tuple-element.235), channel_id=1, source_target_pairs={{4,16},{6,18},{8,28},{10,30},{20,0},{22,2},{24,12},{26,14},{5,17},... | collective-permute-start | bytes 294920 | tf_op jit(solution)/shard_map/ppermute | solution.py:636
  232.1 10.1 %copy-start.15 = (bf16[384,128]{1,0:T(8,128)(2,1)}, bf16[384,128]{1,0:T(8,128)(2,1)S(1)}, u32[]{:S(2)}) copy-start(bf16[384,128]{1,0:T(8,128)(2,1)S(1)} %collective-permute-done.38.refs_5_) | copy-start | bytes 294916
  232.1 10.1 %collective-permute-start.43 = (bf16[384,128]{1,0:T(8,128)(2,1)}, bf16[384,128]{1,0:T(8,128)(2,1)S(1)}, u32[]{:S(2)}, u32[]{:S(2)}) collective-permute-start(bf16[384,128]{1,0:T(8,128)(2,1)} %get-tuple-element.236), channel_id=1, source_target_pairs={{4,18},{6,16},{8,30},{10,28},{20,2},{22,0},{24,14},{26,12},{5,19},... | collective-permute-start | bytes 294920 | tf_op jit(solution)/shard_map/ppermute | solution.py:636
  234.1 8.1 %copy-start.12 = (bf16[384,384]{1,0:T(8,128)(2,1)}, bf16[384,384]{1,0:T(8,128)(2,1)S(1)}, u32[]{:S(2)}) copy-start(bf16[384,384]{1,0:T(8,128)(2,1)S(1)} %collective-permute-done.34.refs_1_) | copy-start | bytes 884740
  234.1 8.1 %copy-start.13 = (bf16[384,384]{1,0:T(8,128)(2,1)}, bf16[384,384]{1,0:T(8,128)(2,1)S(1)}, u32[]{:S(2)}) copy-start(bf16[384,384]{1,0:T(8,128)(2,1)S(1)} %collective-permute-done.35.refs_2_) | copy-start | bytes 884740
  240.6 1.6 copy-start.16
  242.2 0.6 copy-start.17

commit v4 on v3

--- a/solution.py
+++ b/solution.py
@@ -65,7 +65,7 @@
     normed_refs, rest = refs[:2], refs[2:]
     rows, width = tokens_ref.shape[1:]
     lanes = 128
-    slab, span = width // 4, width // 2
+    slab = width // 4
     step, steps = pl.program_id(0), pl.num_programs(0)
     if rest:
         own_ref, own_buf, own_sems = rest
@@ -84,22 +84,31 @@
     def widened(begin):
         return tokens_ref[0, :, pl.ds(begin, lanes)].astype(jnp.float32)
 
-    total = jnp.zeros((rows, lanes), jnp.float32)
-    for begin in range(0, width, lanes):
-        total += widened(begin)
-    mean = jnp.sum(total, axis=-1, keepdims=True) / width
-    total = jnp.zeros((rows, lanes), jnp.float32)
-    for begin in range(0, width, lanes):
-        centered = widened(begin) - mean
-        total += centered * centered
+    def sums(block, total):
+        for begin in range(0, slab, lanes):
+            total += widened(pl.multiple_of(block * slab + begin, lanes))
+        return total
+
+    zero = jnp.zeros((rows, lanes), jnp.float32)
+    mean = jnp.sum(lax.fori_loop(0, 4, sums, zero), axis=-1, keepdims=True) / width
+
+    def squares(block, total):
+        for begin in range(0, slab, lanes):
+            centered = widened(pl.multiple_of(block * slab + begin, lanes)) - mean
+            total += centered * centered
+        return total
+
+    total = lax.fori_loop(0, 4, squares, zero)
     scale = lax.rsqrt(jnp.sum(total, axis=-1, keepdims=True) / width + 1e-06)
-    for i in range(4):
-        source = place_ref[i + 1] * slab
-        for begin in range(0, slab, lanes):
-            column = pl.multiple_of(source + begin, lanes)
-            part = (widened(column) - mean) * scale * gain_ref[:, pl.ds(column, lanes)]
-            target = i * slab % span + begin
-            normed_refs[i * slab // span][:, target : target + lanes] = part.astype(jnp.bfloat16)
+    for cut, normed_ref in enumerate(normed_refs):
+
+        @pl.loop(0, 2)
+        def _(half):
+            for begin in range(0, slab, lanes):
+                column = pl.multiple_of(place_ref[1 + 2 * cut + half] * slab + begin, lanes)
+                part = (widened(column) - mean) * scale * gain_ref[:, pl.ds(column, lanes)]
+                target = pl.multiple_of(half * slab + begin, lanes)
+                normed_ref[:, pl.ds(target, lanes)] = part.astype(jnp.bfloat16)
 
     if rest:
 
@@ -273,7 +282,7 @@
         start_stage(*stage)
     for copy in carry_copies():
         copy.start()
-    ready, waiting, step = set(), [], 384
+    ready, waiting, step = set(), [], plan.step
     for index, (i, n) in enumerate(stages):
         low, high = plan.uses[i][n]
         pltpu.make_async_copy(features(i, n), features(i, n), token_sems.at[i, n]).wait()
@@ -291,8 +300,7 @@
             if n == mine[j][0] and j in plan.added[i]:
                 partial_copy(i, j).wait()
 
-        @pl.loop(0, tokens // step)
-        def _(r):
+        def project(r):
             local = pl.ds(pl.multiple_of(r * step, step), step)
             rows = pl.ds(pl.multiple_of(i * tokens + r * step, step), step)
             term = jnp.dot(
@@ -308,6 +316,11 @@
                     projected_ref[i % 2, local, :] = value.astype(jnp.bfloat16)
                 else:
                     total_ref[rows, j * wide : (j + 1) * wide] = value
+
+        if step == tokens:
+            project(0)
+        else:
+            pl.loop(0, tokens // step)(project)
 
         for j in range(low, high):
             if n != mine[j][-1]:
@@ -329,7 +342,7 @@
                 out_copy(i, j).wait()
 
 
-def run_jobs(role, tokens, wide, images, weights):
+def run_jobs(role, tokens, wide, images, weights, step=384):
     images = [
         dict(
             image,
@@ -352,6 +365,7 @@
         added=[tuple(image["sums"]) for image in images],
         finished=[image["finish"] for image in images],
         carried=[len(image["carry"][0]) for image in images],
+        step=step,
     )
     operands = [x for i in images for place in i["pieces"] for owner in place for x, _ in owner]
     slab = operands[0].shape[1] // 2
@@ -616,7 +630,9 @@
     )
     lent1 = (((across4, across5), (far_across4, far_across5)), ((beside6, across6), far6))
     (lent1,) = run(
-        [dict(pieces=lent1, uses=[(0, 1)] * 4, finish=(0,))], [*lent_weights, (3, 0, [middle6])]
+        [dict(pieces=lent1, uses=[(0, 1)] * 4, finish=(0,))],
+        [*lent_weights, (3, 0, [middle6])],
+        step=seqs * rows,
     )
 
     def hand_back(mixed):

time: 247 us -> 247 us (level)
  no operation moved by 1% of the time
where the time goes in v4:
time: 247 us; the launch traced here: 246 us
  Pallas kernels  95.1 us (39%)
  waiting for transfers between devices  76.5 us (31%)
  starting transfers between devices  51.4 us (21%)
  local copies, waits for them, and re-layouts  12.8 us (5%)
  other arithmetic  9.68 us (4%)
    pallas_call x6, Pallas kernels, run_jobs(): pl.pallas_call(functools.partial(job_kernel, plan), out_shape=shapes, in_...  79.4 us
    ppermute x5, waiting for transfers between devices, pair(): return lax.ppermute(value, 'dp', [(0, 1), (1, 0), (2, 3), (3, 2)])  43.4 us
    ppermute x6, waiting for transfers between devices, shared(): beside = lambda value: lax.ppermute(value, 'seq', swap)  17.5 us
    ppermute x5, starting transfers between devices, pair(): return lax.ppermute(value, 'dp', [(0, 1), (1, 0), (2, 3), (3, 2)])  15.8 us
    pallas_call x2, Pallas kernels, normalize_part(): pl.pallas_call(normalize_kernel, out_shape=[half] * 2 + [jax.ShapeDtypeSt...  12.6 us
    ppermute x6, starting transfers between devices, middle(): return lax.ppermute(value, 'dp', [(1, 2), (2, 1)])  9.16 us
    ppermute x4, waiting for transfers between devices, hand_back(): got.append(lax.ppermute(sent, ('groups', 'dp', 'seq'), steps))  8.1 us
    ppermute x6, starting transfers between devices, shared(): beside = lambda value: lax.ppermute(value, 'seq', swap)  8.03 us
  transfers between devices with their start and end apart: 44, of which 10 were waited for; matrix products, arithmetic and copies ran while one was open for 7% of the time, Pallas kernels for 35%

profile of v4, /device:TPU:0, one launch (start us, length us, event | category | flops | bytes accessed | tf_op | source)
XLA Modules:
  0.0 246.0 jit_solution(18331528061116392116)
XLA Ops:
  0.0 0.7 stack.70.place_ref
  0.7 6.5 %shard_map.37 = (bf16[192,3072]{1,0:T(8,128)(2,1)}, bf16[192,3072]{1,0:T(8,128)(2,1)}, bf16[1536,384]{1,0:T(8,128)(2,1)}) custom-call(s32[6]{0:T(128)} %stack.70.place_ref, bf16[1,384,6144]{2,1,0:T(8,128)(2,1)} %tokens_ref.2, f32[1,6144]{1,0:T(1,128)} %bitcast.41, bf16[6,1536,384]{2,1,0:T(8,128)(2,1)} %bitcast.29), custom_call_target="tpu_custom_call" | custom-call | flops 9437184 | bytes 4718592 | tf_op jit(solution)/shard_map/pallas_call | solution.py:129
  7.2 3.0 %collective-permute-start = (bf16[192,3072]{1,0:T(8,128)(2,1)}, bf16[192,3072]{1,0:T(8,128)(2,1)S(1)}, u32[]{:S(2)}, u32[]{:S(2)}) collective-permute-start(bf16[192,3072]{1,0:T(8,128)(2,1)} %get-tuple-element.124.refs_0_.refs_8_), channel_id=1, source_target_pairs={{0,2},{2,0},{1,3},{3,1},{4,6},{6,4},{5,7},{7,5},{8,10},{10,8},{9,1... | collective-permute-start | bytes 3538952 | tf_op jit(solution)/shard_map/ppermute | solution.py:491
  10.2 1.5 collective-permute-start.1
  11.7 1.6 collective-permute-start.2
  13.3 1.7 collective-permute-start.3
  15.0 2.9 %dynamic-slice_bitcast_fusion = (bf16[1536,384]{1,0:T(8,128)(2,1)}, bf16[1,1536,384]{2,1,0:T(8,128)(2,1)S(1)}) fusion(bf16[6,1536,384]{2,1,0:T(8,128)(2,1)} %bitcast.30, s32[]{:T(128)S(6)} %select_n.77, s32[]{:T(128)S(6)} %select_n.76), kind=kLoop, calls=%fused_computation.1 | loop fusion | bytes 4718600 | tf_op jit(solution)/shard_map/jit(dynamic_index_in_dim)/squeeze | solution.py:528
  18.1 1.5 copy-done.1
  19.6 1.2 broadcast_select_fusion.3
  20.7 0.6 pad_add_fusion.role_ref
  21.4 15.0 %collective-permute-done.refs_4_.refs_12_ = bf16[192,3072]{1,0:T(8,128)(2,1)S(1)} collective-permute-done((bf16[192,3072]{1,0:T(8,128)(2,1)}, bf16[192,3072]{1,0:T(8,128)(2,1)S(1)}, u32[]{:S(2)}, u32[]{:S(2)}) %collective-permute-start) | collective-permute-done | bytes 1179680 | tf_op jit(solution)/shard_map/ppermute | solution.py:491
  36.4 1.6 collective-permute-done.1.refs_0_.refs_8_
  37.9 1.2 collective-permute-start.6
  39.1 1.5 collective-permute-start.7
  40.7 3.1 %collective-permute-start.4 = (bf16[192,3072]{1,0:T(8,128)(2,1)}, bf16[192,3072]{1,0:T(8,128)(2,1)}, u32[]{:S(2)}, u32[]{:S(2)}) collective-permute-start(bf16[192,3072]{1,0:T(8,128)(2,1)} %broadcast_select_fusion.3), channel_id=1, source_target_pairs={{0,4},{4,0},{8,12},{12,8},{1,5},{5,1},{9,13},{13,9},{2,6},{6,2},{1... | collective-permute-start | bytes 3538952 | tf_op jit(solution)/shard_map/ppermute | solution.py:482
  43.8 1.7 collective-permute-start.5
  45.5 1.1 copy-done.5
  46.5 0.7 stack.73.place_ref
  47.2 2.5 %copy.8 = bf16[24,8,8,384]{3,1,2,0:T(8,128)(2,1)} copy(bf16[24,8,8,384]{3,1,0,2:T(8,128)(2,1)} %bitcast.27) | data formatting | bytes 2359296
  49.7 6.1 %shard_map.38 = (bf16[192,3072]{1,0:T(8,128)(2,1)}, bf16[192,3072]{1,0:T(8,128)(2,1)}) custom-call(s32[5]{0:T(128)} %stack.73.place_ref, bf16[1,384,6144]{2,1,0:T(8,128)(2,1)} %tokens_ref.2, f32[1,6144]{1,0:T(1,128)} %bitcast.42, bf16[6,1536,384]{2,1,0:T(8,128)(2,1)} %bitcast.31), custom_call_target="tpu_custom_call" | custom-call | flops 9437184 | bytes 4718592 | tf_op jit(solution)/shard_map/pallas_call | solution.py:129
  55.8 1.4 broadcast_select_fusion.2
  57.2 11.6 %collective-permute-done.4.refs_25_.refs_0_.refs_16_ = bf16[192,3072]{1,0:T(8,128)(2,1)} collective-permute-done((bf16[192,3072]{1,0:T(8,128)(2,1)}, bf16[192,3072]{1,0:T(8,128)(2,1)}, u32[]{:S(2)}, u32[]{:S(2)}) %collective-permute-start.4) | collective-permute-done | bytes 1179680 | tf_op jit(solution)/shard_map/ppermute | solution.py:482
  68.9 0.6 collective-permute-start.13
  69.5 4.6 %collective-permute-start.10 = (bf16[192,3072]{1,0:T(8,128)(2,1)S(1)}, bf16[192,3072]{1,0:T(8,128)(2,1)S(1)}, u32[]{:S(2)}, u32[]{:S(2)}) collective-permute-start(bf16[192,3072]{1,0:T(8,128)(2,1)S(1)} %broadcast_select_fusion.2), channel_id=1, source_target_pairs={{0,4},{4,0},{8,12},{12,8},{1,5},{5,1},{9,13},{13,9},{2,6},{6,2},{1... | collective-permute-start | bytes 3538952 | tf_op jit(solution)/shard_map/ppermute | solution.py:482
  74.1 0.7 collective-permute-start.11
  74.8 0.9 collective-permute-start.12
  75.7 1.2 broadcast_select_fusion.1
  76.9 23.4 %collective-permute-done.10.refs_28_.refs_1_.refs_17_ = bf16[192,3072]{1,0:T(8,128)(2,1)S(1)} collective-permute-done((bf16[192,3072]{1,0:T(8,128)(2,1)S(1)}, bf16[192,3072]{1,0:T(8,128)(2,1)S(1)}, u32[]{:S(2)}, u32[]{:S(2)}) %collective-permute-start.10) | collective-permute-done | bytes 1179680 | tf_op jit(solution)/shard_map/ppermute | solution.py:482
  100.4 2.5 %collective-permute-done.12.refs_4_.refs_12_ = bf16[192,3072]{1,0:T(8,128)(2,1)S(1)} collective-permute-done((bf16[192,3072]{1,0:T(8,128)(2,1)}, bf16[192,3072]{1,0:T(8,128)(2,1)S(1)}, u32[]{:S(2)}, u32[]{:S(2)}) %collective-permute-start.12) | collective-permute-done | bytes 1179680 | tf_op jit(solution)/shard_map/ppermute | solution.py:491
  102.8 1.0 copy-done.6
  103.8 0.8 collective-permute-start.18
  104.7 1.5 collective-permute-start.19
  106.2 2.9 %collective-permute-start.16 = (bf16[1536,384]{1,0:T(8,128)(2,1)}, bf16[1536,384]{1,0:T(8,128)(2,1)}, u32[]{:S(2)}, u32[]{:S(2)}) collective-permute-start(bf16[1536,384]{1,0:T(8,128)(2,1)} %broadcast_select_fusion.1), channel_id=1, source_target_pairs={{0,4},{4,0},{8,12},{12,8},{1,5},{5,1},{9,13},{13,9},{2,6},{6,2},{1... | collective-permute-start | bytes 3538952 | tf_op jit(solution)/shard_map/ppermute | solution.py:482
  109.1 1.7 collective-permute-start.17
  110.8 1.0 copy-done.8
  111.8 2.8 %pad_maximum_fusion = bf16[384,3072]{1,0:T(8,128)(2,1)} fusion(bf16[192,3072]{1,0:T(8,128)(2,1)S(1)} %collective-permute-done.10.refs_28_.refs_1_.refs_17_, bf16[192,3072]{1,0:T(8,128)(2,1)} %collective-permute-done.4.refs_25_.refs_0_.refs_16_), kind=kLoop, calls=%fused_computation | loop fusion | flops 4718592 | bytes 4718592 | tf_op jit(solution)/shard_map/concatenate | solution.py:568
  114.6 2.5 %broadcast_select_fusion = bf16[1536,384]{1,0:T(8,128)(2,1)} fusion(bf16[1536,384]{1,0:T(8,128)(2,1)S(1)} %collective-permute-done.11.refs_14_.refs_22_, bf16[1536,384]{1,0:T(8,128)(2,1)} %get-tuple-element.210.refs_11_.refs_19_.refs_10_, pred[]{:T(512)S(6)} %or.4), kind=kLoop, calls=%fused_computation.2 | loop fusion | flops 589824 | bytes 3538945 | tf_op jit(solution)/shard_map/jit(_where)/select_n | solution.py:479
  117.1 14.6 %shard_map.39 = (bf16[384,128]{1,0:T(8,128)(2,1)}, bf16[384,128]{1,0:T(8,128)(2,1)}, f32[768,384]{1,0:T(8,128)}, f32[768,384]{1,0:T(8,128)}) custom-call(s32[2]{0:T(128)} %pad_add_fusion.role_ref, bf16[192,3072]{1,0:T(8,128)(2,1)} %get-tuple-element.124.refs_0_.refs_8_, bf16[192,3072]{1,0:T(8,128)(2,1)} %get-tuple-element.132.refs_1_.refs_9_, ...), custom_call_target="tpu_custom_call" | custom-call | flops 6341787648 | tf_op jit(solution)/shard_map/pallas_call | solution.py:392
  131.7 3.8 %collective-permute-done.16.refs_27_.refs_17_ = bf16[1536,384]{1,0:T(8,128)(2,1)} collective-permute-done((bf16[1536,384]{1,0:T(8,128)(2,1)}, bf16[1536,384]{1,0:T(8,128)(2,1)}, u32[]{:S(2)}, u32[]{:S(2)}) %collective-permute-start.16) | collective-permute-done | bytes 1179680 | tf_op jit(solution)/shard_map/ppermute | solution.py:482
  135.6 1.2 collective-permute-start.24
  137.4 3.6 %collective-permute-start.22 = (bf16[1536,384]{1,0:T(8,128)(2,1)}, bf16[1536,384]{1,0:T(8,128)(2,1)}, u32[]{:S(2)}, u32[]{:S(2)}) collective-permute-start(bf16[1536,384]{1,0:T(8,128)(2,1)} %broadcast_select_fusion), channel_id=1, source_target_pairs={{0,4},{4,0},{8,12},{12,8},{1,5},{5,1},{9,13},{13,9},{2,6},{6,2},{1... | collective-permute-start | bytes 3538952 | tf_op jit(solution)/shard_map/ppermute | solution.py:482
  141.0 1.7 collective-permute-start.23
  142.7 20.0 %shard_map.40 = (bf16[384,128]{1,0:T(8,128)(2,1)}, bf16[384,128]{1,0:T(8,128)(2,1)}, f32[768,384]{1,0:T(8,128)}, f32[768,384]{1,0:T(8,128)}, f32[768,384]{1,0:T(8,128)}, /*index=5*/f32[768,384]{1,0:T(8,128)}) custom-call(s32[2]{0:T(128)} %pad_add_fusion.role_ref, bf16[192,3072]{1,0:T(8,128)(2,1)} %collective-permute-done.1.refs_0_.refs_8_, ...), custom_call_target="tpu_custom_call" | custom-call | flops 9965666304 | tf_op jit(solution)/shard_map/pallas_call | solution.py:392
  162.7 4.6 %collective-permute-done.22.refs_18_.refs_8_ = bf16[1536,384]{1,0:T(8,128)(2,1)} collective-permute-done((bf16[1536,384]{1,0:T(8,128)(2,1)}, bf16[1536,384]{1,0:T(8,128)(2,1)}, u32[]{:S(2)}, u32[]{:S(2)}) %collective-permute-start.22) | collective-permute-done | bytes 1179680 | tf_op jit(solution)/shard_map/ppermute | solution.py:482
  167.4 1.6 collective-permute-start.32
  169.0 1.3 collective-permute-start.29
  170.3 1.7 collective-permute-start.30
  172.0 0.8 collective-permute-start.31
  172.8 13.0 %shard_map.41 = (bf16[384,128]{1,0:T(8,128)(2,1)}, bf16[384,128]{1,0:T(8,128)(2,1)}, f32[768,384]{1,0:T(8,128)}, bf16[384,128]{1,0:T(8,128)(2,1)}, bf16[384,128]{1,0:T(8,128)(2,1)}, /*index=5*/f32[768,384]{1,0:T(8,128)}) custom-call(s32[2]{0:T(128)} %pad_add_fusion.role_ref, bf16[192,3072]{1,0:T(8,128)(2,1)} %get-tuple-element.124.refs_0_.refs_8_, ...), custom_call_target="tpu_custom_call" | custom-call | flops 3623878656 | tf_op jit(solution)/shard_map/pallas_call | solution.py:392
  185.9 8.8 %shard_map.42.refs_28_ = f32[768,384]{1,0:T(8,128)} custom-call(s32[2]{0:T(128)} %pad_add_fusion.role_ref, bf16[192,3072]{1,0:T(8,128)(2,1)} %collective-permute-done.4.refs_25_.refs_0_.refs_16_, bf16[192,3072]{1,0:T(8,128)(2,1)} %copy-done.2, bf16[384,3072]{1,0:T(8,128)(2,1)} %collective-permute-done.26.refs_2_.refs_3_.refs_18_.refs_19_, ...), custom_call_target="tpu_custom_call" | custom-call | flops 2717908992 | tf_op jit(solution)/shard_map/pallas_call | solution.py:392
  194.7 5.8 %collective-permute-done.29.refs_25_ = bf16[1536,384]{1,0:T(8,128)(2,1)} collective-permute-done((bf16[1536,384]{1,0:T(8,128)(2,1)}, bf16[1536,384]{1,0:T(8,128)(2,1)}, u32[]{:S(2)}, u32[]{:S(2)}) %collective-permute-start.29) | collective-permute-done | bytes 1179680 | tf_op jit(solution)/shard_map/ppermute | solution.py:485
  201.2 12.8 %shard_map.43 = (bf16[384,384]{1,0:T(8,128)(2,1)}, bf16[384,384]{1,0:T(8,128)(2,1)}, bf16[384,384]{1,0:T(8,128)(2,1)}, bf16[384,384]{1,0:T(8,128)(2,1)}, bf16[38...) custom-call(s32[2]{0:T(128)} %pad_add_fusion.role_ref, bf16[192,3072]{1,0:T(8,128)(2,1)} %get-tuple-element.124.refs_0_.refs_8_, ...), custom_call_target="tpu_custom_call" | custom-call | flops 2717908992 | tf_op jit(solution)/shard_map/pallas_call | solution.py:392
  214.0 0.9 collective-permute-start.34
  215.4 2.1 collective-permute-start.36
  217.6 1.3 collective-permute-start.37
  218.9 1.6 collective-permute-start.38
  220.4 10.2 %shard_map.44 = (bf16[384,128]{1,0:T(8,128)(2,1)}, bf16[384,128]{1,0:T(8,128)(2,1)}) custom-call(s32[2]{0:T(128)} %pad_add_fusion.role_ref, bf16[192,3072]{1,0:T(8,128)(2,1)} %collective-permute-done.19.refs_0_, bf16[192,3072]{1,0:T(8,128)(2,1)} %collective-permute-done.25.refs_1_, bf16[192,3072]{1,0:T(8,128)(2,1)} %collective-permute-done.33.refs_2_, ...), custom_call_target="tpu_custom_call" | custom-call | flops 3623878656 | tf_op jit(solution)/shard_map/pallas_call | solution.py:392
  230.6 1.3 collective-permute-start.42
  231.9 1.3 collective-permute-start.43
  233.3 0.6 stack.63.place_ref
  233.9 6.5 %collective-permute-done.42.refs_6_ = bf16[384,128]{1,0:T(8,128)(2,1)S(1)} collective-permute-done((bf16[384,128]{1,0:T(8,128)(2,1)}, bf16[384,128]{1,0:T(8,128)(2,1)S(1)}, u32[]{:S(2)}, u32[]{:S(2)}) %collective-permute-start.42) | collective-permute-done | bytes 98336 | tf_op jit(solution)/shard_map/ppermute | solution.py:652
  240.5 1.6 collective-permute-done.43.refs_7_
  242.1 0.6 copy-done.17
  242.7 3.1 %shard_map.45 = bf16[384,1536]{1,0:T(8,128)(2,1)} custom-call(s32[5]{0:T(128)} %stack.63.place_ref, bf16[384,384]{1,0:T(8,128)(2,1)} %get-tuple-element.225.refs_0_, bf16[384,384]{1,0:T(8,128)(2,1)} %copy-done.12, bf16[384,384]{1,0:T(8,128)(2,1)} %copy-done.13, bf16[384,384]{1,0:T(8,128)(2,1)} %collective-permute-done.36.refs_3_, ...), custom_call_target="tpu_custom_call" | custom-call | bytes 2359296 | tf_op jit(solution)/shard_map/pallas_call | solution.py:453
  (81 shorter events, 2.2 us)
Async XLA Ops:
  7.2 29.2 %collective-permute-start = (bf16[192,3072]{1,0:T(8,128)(2,1)}, bf16[192,3072]{1,0:T(8,128)(2,1)S(1)}, u32[]{:S(2)}, u32[]{:S(2)}) collective-permute-start(bf16[192,3072]{1,0:T(8,128)(2,1)} %get-tuple-element.124.refs_0_.refs_8_), channel_id=1, source_target_pairs={{0,2},{2,0},{1,3},{3,1},{4,6},{6,4},{5,7},{7,5},{8,10},{10,8},{9,1... | collective-permute-start | bytes 3538952 | tf_op jit(solution)/shard_map/ppermute | solution.py:491
  10.2 27.7 %collective-permute-start.1 = (bf16[192,3072]{1,0:T(8,128)(2,1)}, bf16[192,3072]{1,0:T(8,128)(2,1)}, u32[]{:S(2)}, u32[]{:S(2)}) collective-permute-start(bf16[192,3072]{1,0:T(8,128)(2,1)} %get-tuple-element.124.refs_0_.refs_8_), channel_id=1, source_target_pairs={{0,16},{16,0},{1,17},{17,1},{2,18},{18,2},{3,19},{19,3},{4,20},{20... | collective-permute-start | bytes 3538952 | tf_op jit(solution)/shard_map/ppermute | solution.py:492
  11.7 28.9 %collective-permute-start.2 = (bf16[1536,384]{1,0:T(8,128)(2,1)}, bf16[1536,384]{1,0:T(8,128)(2,1)}, u32[]{:S(2)}, u32[]{:S(2)}) collective-permute-start(bf16[1536,384]{1,0:T(8,128)(2,1)} %get-tuple-element.128.refs_8_.refs_10_.refs_16_.refs_18_), channel_id=1, source_target_pairs={{0,4},{4,0},{8,12},{12,8},{1,5},{5,1},{9,13},{13,9},{2,6},{6,2},{1... | collective-permute-start | bytes 3538952 | tf_op jit(solution)/shard_map/ppermute | solution.py:482
  13.3 27.4 %collective-permute-start.3 = (bf16[1536,384]{1,0:T(8,128)(2,1)}, bf16[1536,384]{1,0:T(8,128)(2,1)}, u32[]{:S(2)}, u32[]{:S(2)}) collective-permute-start(bf16[1536,384]{1,0:T(8,128)(2,1)} %get-tuple-element.128.refs_8_.refs_10_.refs_16_.refs_18_), channel_id=1, source_target_pairs={{4,8},{8,4},{5,9},{9,5},{6,10},{10,6},{7,11},{11,7},{20,24},{24,20... | collective-permute-start | bytes 3538952 | tf_op jit(solution)/shard_map/ppermute | solution.py:488
  17.9 57.8 %copy-start = (bf16[1,1536,384]{2,1,0:T(8,128)(2,1)}, bf16[1,1536,384]{2,1,0:T(8,128)(2,1)S(1)}, u32[]{:S(2)}) copy-start(bf16[1,1536,384]{2,1,0:T(8,128)(2,1)S(1)} %get-tuple-element.238) | copy-start | bytes 3538948
  17.9 1.7 copy-start.1
  36.4 1.6 copy-start.4
  37.9 7.5 %collective-permute-start.8 = (bf16[192,3072]{1,0:T(8,128)(2,1)S(1)}, bf16[192,3072]{1,0:T(8,128)(2,1)S(1)}, u32[]{:S(2)}, u32[]{:S(2)}) collective-permute-start(bf16[192,3072]{1,0:T(8,128)(2,1)S(1)} %collective-permute-done.refs_4_.refs_12_), channel_id=1, source_target_pairs={{0,1},{1,0},{2,3},{3,2},{4,5},{5,4},{6,7},{7,6},{8,9},{9,8},{10,11... | collective-permute-start | bytes 3538952 | tf_op jit(solution)/shard_map/ppermute | solution.py:499
  37.9 30.9 %collective-permute-start.6 = (bf16[192,3072]{1,0:T(8,128)(2,1)}, bf16[192,3072]{1,0:T(8,128)(2,1)}, u32[]{:S(2)}, u32[]{:S(2)}) collective-permute-start(bf16[192,3072]{1,0:T(8,128)(2,1)} %get-tuple-element.132.refs_1_.refs_9_), channel_id=1, source_target_pairs={{0,2},{2,0},{1,3},{3,1},{4,6},{6,4},{5,7},{7,5},{8,10},{10,8},{9,1... | collective-permute-start | bytes 3538952 | tf_op jit(solution)/shard_map/ppermute | solution.py:491
  39.1 29.7 %collective-permute-start.7 = (bf16[192,3072]{1,0:T(8,128)(2,1)}, bf16[192,3072]{1,0:T(8,128)(2,1)}, u32[]{:S(2)}, u32[]{:S(2)}) collective-permute-start(bf16[192,3072]{1,0:T(8,128)(2,1)} %get-tuple-element.132.refs_1_.refs_9_), channel_id=1, source_target_pairs={{0,16},{16,0},{1,17},{17,1},{2,18},{18,2},{3,19},{19,3},{4,20},{20... | collective-permute-start | bytes 3538952 | tf_op jit(solution)/shard_map/ppermute | solution.py:492
  40.7 28.1 %collective-permute-start.4 = (bf16[192,3072]{1,0:T(8,128)(2,1)}, bf16[192,3072]{1,0:T(8,128)(2,1)}, u32[]{:S(2)}, u32[]{:S(2)}) collective-permute-start(bf16[192,3072]{1,0:T(8,128)(2,1)} %broadcast_select_fusion.3), channel_id=1, source_target_pairs={{0,4},{4,0},{8,12},{12,8},{1,5},{5,1},{9,13},{13,9},{2,6},{6,2},{1... | collective-permute-start | bytes 3538952 | tf_op jit(solution)/shard_map/ppermute | solution.py:482
  43.8 25.0 %collective-permute-start.5 = (bf16[1536,384]{1,0:T(8,128)(2,1)}, bf16[1536,384]{1,0:T(8,128)(2,1)}, u32[]{:S(2)}, u32[]{:S(2)}) collective-permute-start(bf16[1536,384]{1,0:T(8,128)(2,1)} %collective-permute-done.2.refs_15_.refs_16_.refs_23_.refs_26_), channel_id=1, source_target_pairs={{4,8},{8,4},{5,9},{9,5},{6,10},{10,6},{7,11},{11,7},{20,24},{24,20... | collective-permute-start | bytes 3538952 | tf_op jit(solution)/shard_map/ppermute | solution.py:488
  45.5 1.1 copy-start.5
  46.5 22.3 %collective-permute-start.9 = (bf16[192,3072]{1,0:T(8,128)(2,1)}, bf16[192,3072]{1,0:T(8,128)(2,1)}, u32[]{:S(2)}, u32[]{:S(2)}) collective-permute-start(bf16[192,3072]{1,0:T(8,128)(2,1)} %collective-permute-done.1.refs_0_.refs_8_), channel_id=1, source_target_pairs={{0,1},{1,0},{2,3},{3,2},{4,5},{5,4},{6,7},{7,6},{8,9},{9,8},{10,11... | collective-permute-start | bytes 3538952 | tf_op jit(solution)/shard_map/ppermute | solution.py:499
  68.8 6.9 %collective-permute-start.14 = (bf16[192,3072]{1,0:T(8,128)(2,1)}, bf16[192,3072]{1,0:T(8,128)(2,1)}, u32[]{:S(2)}, u32[]{:S(2)}) collective-permute-start(bf16[192,3072]{1,0:T(8,128)(2,1)} %collective-permute-done.6.refs_5_.refs_13_), channel_id=1, source_target_pairs={{0,1},{1,0},{2,3},{3,2},{4,5},{5,4},{6,7},{7,6},{8,9},{9,8},{10,11... | collective-permute-start | bytes 3538952 | tf_op jit(solution)/shard_map/ppermute | solution.py:499
  68.9 33.9 %collective-permute-start.13 = (bf16[192,3072]{1,0:T(8,128)(2,1)}, bf16[192,3072]{1,0:T(8,128)(2,1)}, u32[]{:S(2)}, u32[]{:S(2)}) collective-permute-start(bf16[192,3072]{1,0:T(8,128)(2,1)} %collective-permute-done.6.refs_5_.refs_13_), channel_id=1, source_target_pairs={{0,16},{16,0},{1,17},{17,1},{2,18},{18,2},{3,19},{19,3},{4,20},{20... | collective-permute-start | bytes 3538952 | tf_op jit(solution)/shard_map/ppermute | solution.py:492
  69.5 30.9 %collective-permute-start.10 = (bf16[192,3072]{1,0:T(8,128)(2,1)S(1)}, bf16[192,3072]{1,0:T(8,128)(2,1)S(1)}, u32[]{:S(2)}, u32[]{:S(2)}) collective-permute-start(bf16[192,3072]{1,0:T(8,128)(2,1)S(1)} %broadcast_select_fusion.2), channel_id=1, source_target_pairs={{0,4},{4,0},{8,12},{12,8},{1,5},{5,1},{9,13},{13,9},{2,6},{6,2},{1... | collective-permute-start | bytes 3538952 | tf_op jit(solution)/shard_map/ppermute | solution.py:482
  74.1 26.3 %collective-permute-start.11 = (bf16[1536,384]{1,0:T(8,128)(2,1)S(1)}, bf16[1536,384]{1,0:T(8,128)(2,1)S(1)}, u32[]{:S(2)}, u32[]{:S(2)}) collective-permute-start(bf16[1536,384]{1,0:T(8,128)(2,1)S(1)} %bitcast.33), channel_id=1, source_target_pairs={{4,8},{8,4},{5,9},{9,5},{6,10},{10,6},{7,11},{11,7},{20,24},{24,20... | collective-permute-start | bytes 3538952 | tf_op jit(solution)/shard_map/ppermute | solution.py:488
  74.8 28.0 %collective-permute-start.12 = (bf16[192,3072]{1,0:T(8,128)(2,1)}, bf16[192,3072]{1,0:T(8,128)(2,1)S(1)}, u32[]{:S(2)}, u32[]{:S(2)}) collective-permute-start(bf16[192,3072]{1,0:T(8,128)(2,1)} %collective-permute-done.1.refs_0_.refs_8_), channel_id=1, source_target_pairs={{0,2},{2,0},{1,3},{3,1},{4,6},{6,4},{5,7},{7,5},{8,10},{10,8},{9,1... | collective-permute-start | bytes 3538952 | tf_op jit(solution)/shard_map/ppermute | solution.py:491
  75.7 27.1 %collective-permute-start.15 = (bf16[192,3072]{1,0:T(8,128)(2,1)}, bf16[192,3072]{1,0:T(8,128)(2,1)S(1)}, u32[]{:S(2)}, u32[]{:S(2)}) collective-permute-start(bf16[192,3072]{1,0:T(8,128)(2,1)} %collective-permute-done.7.refs_1_.refs_9_), channel_id=1, source_target_pairs={{0,1},{1,0},{2,3},{3,2},{4,5},{5,4},{6,7},{7,6},{8,9},{9,8},{10,11... | collective-permute-start | bytes 3538952 | tf_op jit(solution)/shard_map/ppermute | solution.py:499
  100.4 14.3 %copy-start.2 = (bf16[192,3072]{1,0:T(8,128)(2,1)}, bf16[192,3072]{1,0:T(8,128)(2,1)S(1)}, u32[]{:S(2)}) copy-start(bf16[192,3072]{1,0:T(8,128)(2,1)S(1)} %collective-permute-done.10.refs_28_.refs_1_.refs_17_) | copy-start | bytes 3538948
  100.4 14.3 %copy-start.10 = (bf16[1536,384]{1,0:T(8,128)(2,1)}, bf16[1536,384]{1,0:T(8,128)(2,1)S(1)}, u32[]{:S(2)}) copy-start(bf16[1536,384]{1,0:T(8,128)(2,1)S(1)} %collective-permute-done.11.refs_14_.refs_22_) | copy-start | bytes 3538948
  102.8 1.0 copy-start.6
  103.8 7.0 %copy-start.7 = (bf16[192,3072]{1,0:T(8,128)(2,1)}, bf16[192,3072]{1,0:T(8,128)(2,1)S(1)}, u32[]{:S(2)}) copy-start(bf16[192,3072]{1,0:T(8,128)(2,1)S(1)} %collective-permute-done.15.refs_3_.refs_11_) | copy-start | bytes 3538948
  103.8 7.0 %collective-permute-start.20 = (bf16[192,3072]{1,0:T(8,128)(2,1)S(1)}, bf16[192,3072]{1,0:T(8,128)(2,1)S(1)}, u32[]{:S(2)}, u32[]{:S(2)}) collective-permute-start(bf16[192,3072]{1,0:T(8,128)(2,1)S(1)} %collective-permute-done.12.refs_4_.refs_12_), channel_id=1, source_target_pairs={{0,1},{1,0},{2,3},{3,2},{4,5},{5,4},{6,7},{7,6},{8,9},{9,8},{10,11... | collective-permute-start | bytes 3538952 | tf_op jit(solution)/shard_map/ppermute | solution.py:499
  103.8 31.7 %collective-permute-start.18 = (bf16[192,3072]{1,0:T(8,128)(2,1)}, bf16[192,3072]{1,0:T(8,128)(2,1)}, u32[]{:S(2)}, u32[]{:S(2)}) collective-permute-start(bf16[192,3072]{1,0:T(8,128)(2,1)} %collective-permute-done.4.refs_25_.refs_0_.refs_16_), channel_id=1, source_target_pairs={{0,2},{2,0},{1,3},{3,1},{4,6},{6,4},{5,7},{7,5},{8,10},{10,8},{9,1... | collective-permute-start | bytes 3538952 | tf_op jit(solution)/shard_map/ppermute | solution.py:491
  104.7 30.8 %collective-permute-start.19 = (bf16[192,3072]{1,0:T(8,128)(2,1)}, bf16[192,3072]{1,0:T(8,128)(2,1)}, u32[]{:S(2)}, u32[]{:S(2)}) collective-permute-start(bf16[192,3072]{1,0:T(8,128)(2,1)} %collective-permute-done.4.refs_25_.refs_0_.refs_16_), channel_id=1, source_target_pairs={{0,16},{16,0},{1,17},{17,1},{2,18},{18,2},{3,19},{19,3},{4,20},{20... | collective-permute-start | bytes 3538952 | tf_op jit(solution)/shard_map/ppermute | solution.py:492
  106.2 29.3 %collective-permute-start.16 = (bf16[1536,384]{1,0:T(8,128)(2,1)}, bf16[1536,384]{1,0:T(8,128)(2,1)}, u32[]{:S(2)}, u32[]{:S(2)}) collective-permute-start(bf16[1536,384]{1,0:T(8,128)(2,1)} %broadcast_select_fusion.1), channel_id=1, source_target_pairs={{0,4},{4,0},{8,12},{12,8},{1,5},{5,1},{9,13},{13,9},{2,6},{6,2},{1... | collective-permute-start | bytes 3538952 | tf_op jit(solution)/shard_map/ppermute | solution.py:482
  109.1 26.4 %collective-permute-start.17 = (bf16[1536,384]{1,0:T(8,128)(2,1)}, bf16[1536,384]{1,0:T(8,128)(2,1)}, u32[]{:S(2)}, u32[]{:S(2)}) collective-permute-start(bf16[1536,384]{1,0:T(8,128)(2,1)} %get-tuple-element.210.refs_11_.refs_19_.refs_10_), channel_id=1, source_target_pairs={{4,8},{8,4},{5,9},{9,5},{6,10},{10,6},{7,11},{11,7},{20,24},{24,20... | collective-permute-start | bytes 3538952 | tf_op jit(solution)/shard_map/ppermute | solution.py:488
  110.8 1.0 copy-start.8
  111.8 23.7 %collective-permute-start.21 = (bf16[192,3072]{1,0:T(8,128)(2,1)}, bf16[192,3072]{1,0:T(8,128)(2,1)}, u32[]{:S(2)}, u32[]{:S(2)}) collective-permute-start(bf16[192,3072]{1,0:T(8,128)(2,1)} %collective-permute-done.13.refs_5_.refs_13_), channel_id=1, source_target_pairs={{0,1},{1,0},{2,3},{3,2},{4,5},{5,4},{6,7},{7,6},{8,9},{9,8},{10,11... | collective-permute-start | bytes 3538952 | tf_op jit(solution)/shard_map/ppermute | solution.py:499
  117.1 18.5 %copy-start.3 = (bf16[192,3072]{1,0:T(8,128)(2,1)S(1)}, bf16[192,3072]{1,0:T(8,128)(2,1)}, u32[]{:S(2)}) copy-start(bf16[192,3072]{1,0:T(8,128)(2,1)} %copy-done.2) | copy-start | bytes 3538948
  135.5 7.2 %collective-permute-start.26 = (bf16[384,3072]{1,0:T(8,128)(2,1)}, bf16[384,3072]{1,0:T(8,128)(2,1)}, u32[]{:S(2)}, u32[]{:S(2)}) collective-permute-start(bf16[384,3072]{1,0:T(8,128)(2,1)} %pad_maximum_fusion), channel_id=1, source_target_pairs={{0,1},{1,0},{2,3},{3,2},{4,5},{5,4},{6,7},{7,6},{8,9},{9,8},{10,11... | collective-permute-start | bytes 7077896 | tf_op jit(solution)/shard_map/ppermute | solution.py:499
  135.6 31.7 %collective-permute-start.24 = (bf16[192,3072]{1,0:T(8,128)(2,1)S(1)}, bf16[192,3072]{1,0:T(8,128)(2,1)}, u32[]{:S(2)}, u32[]{:S(2)}) collective-permute-start(bf16[192,3072]{1,0:T(8,128)(2,1)S(1)} %copy-done.3), channel_id=1, source_target_pairs={{0,2},{2,0},{1,3},{3,1},{4,6},{6,4},{5,7},{7,5},{8,10},{10,8},{9,1... | collective-permute-start | bytes 3538952 | tf_op jit(solution)/shard_map/ppermute | solution.py:491
  136.9 30.5 %collective-permute-start.25 = (bf16[192,3072]{1,0:T(8,128)(2,1)S(1)}, bf16[192,3072]{1,0:T(8,128)(2,1)}, u32[]{:S(2)}, u32[]{:S(2)}) collective-permute-start(bf16[192,3072]{1,0:T(8,128)(2,1)S(1)} %copy-done.3), channel_id=1, source_target_pairs={{0,16},{16,0},{1,17},{17,1},{2,18},{18,2},{3,19},{19,3},{4,20},{20... | collective-permute-start | bytes 3538952 | tf_op jit(solution)/shard_map/ppermute | solution.py:492
  137.4 29.9 %collective-permute-start.22 = (bf16[1536,384]{1,0:T(8,128)(2,1)}, bf16[1536,384]{1,0:T(8,128)(2,1)}, u32[]{:S(2)}, u32[]{:S(2)}) collective-permute-start(bf16[1536,384]{1,0:T(8,128)(2,1)} %broadcast_select_fusion), channel_id=1, source_target_pairs={{0,4},{4,0},{8,12},{12,8},{1,5},{5,1},{9,13},{13,9},{2,6},{6,2},{1... | collective-permute-start | bytes 3538952 | tf_op jit(solution)/shard_map/ppermute | solution.py:482
  141.0 26.3 %collective-permute-start.23 = (bf16[1536,384]{1,0:T(8,128)(2,1)}, bf16[1536,384]{1,0:T(8,128)(2,1)}, u32[]{:S(2)}, u32[]{:S(2)}) collective-permute-start(bf16[1536,384]{1,0:T(8,128)(2,1)} %collective-permute-done.16.refs_27_.refs_17_), channel_id=1, source_target_pairs={{4,8},{8,4},{5,9},{9,5},{6,10},{10,6},{7,11},{11,7},{20,24},{24,20... | collective-permute-start | bytes 3538952 | tf_op jit(solution)/shard_map/ppermute | solution.py:488
  142.7 24.6 %collective-permute-start.27 = (bf16[192,3072]{1,0:T(8,128)(2,1)}, bf16[192,3072]{1,0:T(8,128)(2,1)}, u32[]{:S(2)}, u32[]{:S(2)}) collective-permute-start(bf16[192,3072]{1,0:T(8,128)(2,1)} %collective-permute-done.18.refs_4_.refs_20_), channel_id=1, source_target_pairs={{0,1},{1,0},{2,3},{3,2},{4,5},{5,4},{6,7},{7,6},{8,9},{9,8},{10,11... | collective-permute-start | bytes 3538952 | tf_op jit(solution)/shard_map/ppermute | solution.py:499
  167.3 5.5 %collective-permute-start.28 = (bf16[192,3072]{1,0:T(8,128)(2,1)}, bf16[192,3072]{1,0:T(8,128)(2,1)S(1)}, u32[]{:S(2)}, u32[]{:S(2)}) collective-permute-start(bf16[192,3072]{1,0:T(8,128)(2,1)} %collective-permute-done.24.refs_5_.refs_21_), channel_id=1, source_target_pairs={{0,1},{1,0},{2,3},{3,2},{4,5},{5,4},{6,7},{7,6},{8,9},{9,8},{10,11... | collective-permute-start | bytes 3538952 | tf_op jit(solution)/shard_map/ppermute | solution.py:499
  167.4 33.1 %collective-permute-start.32 = (bf16[192,3072]{1,0:T(8,128)(2,1)}, bf16[192,3072]{1,0:T(8,128)(2,1)}, u32[]{:S(2)}, u32[]{:S(2)}) collective-permute-start(bf16[192,3072]{1,0:T(8,128)(2,1)} %collective-permute-done.24.refs_5_.refs_21_), channel_id=1, source_target_pairs={{0,16},{16,0},{1,17},{17,1},{2,18},{18,2},{3,19},{19,3},{4,20},{20... | collective-permute-start | bytes 3538952 | tf_op jit(solution)/shard_map/ppermute | solution.py:492
  169.0 31.5 %collective-permute-start.29 = (bf16[1536,384]{1,0:T(8,128)(2,1)}, bf16[1536,384]{1,0:T(8,128)(2,1)}, u32[]{:S(2)}, u32[]{:S(2)}) collective-permute-start(bf16[1536,384]{1,0:T(8,128)(2,1)} %collective-permute-done.23.refs_16_), channel_id=1, source_target_pairs={{4,0},{8,12},{5,1},{9,13},{6,2},{10,14},{7,3},{11,15},{20,16},{24,... | collective-permute-start | bytes 3538952 | tf_op jit(solution)/shard_map/ppermute | solution.py:485
  170.3 30.2 %collective-permute-start.30 = (bf16[1536,384]{1,0:T(8,128)(2,1)}, bf16[1536,384]{1,0:T(8,128)(2,1)}, u32[]{:S(2)}, u32[]{:S(2)}) collective-permute-start(bf16[1536,384]{1,0:T(8,128)(2,1)} %collective-permute-done.22.refs_18_.refs_8_), channel_id=1, source_target_pairs={{4,8},{8,4},{5,9},{9,5},{6,10},{10,6},{7,11},{11,7},{20,24},{24,20... | collective-permute-start | bytes 3538952 | tf_op jit(solution)/shard_map/ppermute | solution.py:488
  172.0 28.5 %collective-permute-start.31 = (bf16[192,3072]{1,0:T(8,128)(2,1)}, bf16[192,3072]{1,0:T(8,128)(2,1)}, u32[]{:S(2)}, u32[]{:S(2)}) collective-permute-start(bf16[192,3072]{1,0:T(8,128)(2,1)} %collective-permute-done.19.refs_0_), channel_id=1, source_target_pairs={{0,2},{2,0},{1,3},{3,1},{4,6},{6,4},{5,7},{7,5},{8,10},{10,8},{9,1... | collective-permute-start | bytes 3538952 | tf_op jit(solution)/shard_map/ppermute | solution.py:491
  172.8 13.1 %copy-start.9 = (bf16[192,3072]{1,0:T(8,128)(2,1)}, bf16[192,3072]{1,0:T(8,128)(2,1)S(1)}, u32[]{:S(2)}) copy-start(bf16[192,3072]{1,0:T(8,128)(2,1)S(1)} %collective-permute-done.28.refs_7_.refs_23_) | copy-start | bytes 3538948
  172.8 27.7 %collective-permute-start.33 = (bf16[192,3072]{1,0:T(8,128)(2,1)}, bf16[192,3072]{1,0:T(8,128)(2,1)}, u32[]{:S(2)}, u32[]{:S(2)}) collective-permute-start(bf16[192,3072]{1,0:T(8,128)(2,1)} %collective-permute-done.19.refs_0_), channel_id=1, source_target_pairs={{0,1},{1,0},{2,3},{3,2},{4,5},{5,4},{6,7},{7,6},{8,9},{9,8},{10,11... | collective-permute-start | bytes 3538952 | tf_op jit(solution)/shard_map/ppermute | solution.py:499
  200.5 14.9 %collective-permute-start.39 = (bf16[192,3072]{1,0:T(8,128)(2,1)}, bf16[192,3072]{1,0:T(8,128)(2,1)S(1)}, u32[]{:S(2)}, u32[]{:S(2)}) collective-permute-start(bf16[192,3072]{1,0:T(8,128)(2,1)} %collective-permute-done.25.refs_1_), channel_id=1, source_target_pairs={{0,1},{1,0},{2,3},{3,2},{4,5},{5,4},{6,7},{7,6},{8,9},{9,8},{10,11... | collective-permute-start | bytes 3538952 | tf_op jit(solution)/shard_map/ppermute | solution.py:621
  200.6 17.0 %collective-permute-start.40 = (bf16[192,3072]{1,0:T(8,128)(2,1)}, bf16[192,3072]{1,0:T(8,128)(2,1)}, u32[]{:S(2)}, u32[]{:S(2)}) collective-permute-start(bf16[192,3072]{1,0:T(8,128)(2,1)} %collective-permute-done.31.refs_4_), channel_id=1, source_target_pairs={{0,1},{1,0},{2,3},{3,2},{4,5},{5,4},{6,7},{7,6},{8,9},{9,8},{10,11... | collective-permute-start | bytes 3538952 | tf_op jit(solution)/shard_map/ppermute | solution.py:621
  201.1 17.8 %collective-permute-start.41 = (bf16[192,3072]{1,0:T(8,128)(2,1)}, bf16[192,3072]{1,0:T(8,128)(2,1)}, u32[]{:S(2)}, u32[]{:S(2)}) collective-permute-start(bf16[192,3072]{1,0:T(8,128)(2,1)} %collective-permute-done.32.refs_5_), channel_id=1, source_target_pairs={{0,1},{1,0},{2,3},{3,2},{4,5},{5,4},{6,7},{7,6},{8,9},{9,8},{10,11... | collective-permute-start | bytes 3538952 | tf_op jit(solution)/shard_map/ppermute | solution.py:621
  214.0 19.9 %collective-permute-start.34 = (bf16[384,384]{1,0:T(8,128)(2,1)}, bf16[384,384]{1,0:T(8,128)(2,1)S(1)}, u32[]{:S(2)}, u32[]{:S(2)}) collective-permute-start(bf16[384,384]{1,0:T(8,128)(2,1)} %get-tuple-element.226), channel_id=1, source_target_pairs={{0,2},{2,0},{16,18},{18,16},{1,3},{3,1},{17,19},{19,17},{4,6},{6,4... | collective-permute-start | bytes 884744 | tf_op jit(solution)/shard_map/ppermute | solution.py:514
  214.9 19.0 %collective-permute-start.35 = (bf16[384,384]{1,0:T(8,128)(2,1)}, bf16[384,384]{1,0:T(8,128)(2,1)S(1)}, u32[]{:S(2)}, u32[]{:S(2)}) collective-permute-start(bf16[384,384]{1,0:T(8,128)(2,1)} %get-tuple-element.227), channel_id=1, source_target_pairs={{0,16},{2,18},{16,0},{18,2},{1,17},{3,19},{17,1},{19,3},{4,20},{6,... | collective-permute-start | bytes 884744 | tf_op jit(solution)/shard_map/ppermute | solution.py:514
  215.4 5.0 %copy-start.11 = (bf16[192,3072]{1,0:T(8,128)(2,1)}, bf16[192,3072]{1,0:T(8,128)(2,1)S(1)}, u32[]{:S(2)}) copy-start(bf16[192,3072]{1,0:T(8,128)(2,1)S(1)} %collective-permute-done.39.refs_3_) | copy-start | bytes 3538948
  215.4 18.5 %collective-permute-start.36 = (bf16[384,384]{1,0:T(8,128)(2,1)}, bf16[384,384]{1,0:T(8,128)(2,1)}, u32[]{:S(2)}, u32[]{:S(2)}) collective-permute-start(bf16[384,384]{1,0:T(8,128)(2,1)} %get-tuple-element.228), channel_id=1, source_target_pairs={{0,18},{2,16},{16,2},{18,0},{1,19},{3,17},{17,3},{19,1},{4,22},{6,... | collective-permute-start | bytes 884744 | tf_op jit(solution)/shard_map/ppermute | solution.py:514
  217.6 13.0 %collective-permute-start.37 = (bf16[384,128]{1,0:T(8,128)(2,1)}, bf16[384,128]{1,0:T(8,128)(2,1)S(1)}, u32[]{:S(2)}, u32[]{:S(2)}) collective-permute-start(bf16[384,128]{1,0:T(8,128)(2,1)} %get-tuple-element.229), channel_id=1, source_target_pairs={{4,0},{6,2},{8,12},{10,14},{20,16},{22,18},{24,28},{26,30},{5,1},{... | collective-permute-start | bytes 294920 | tf_op jit(solution)/shard_map/ppermute | solution.py:652
  218.9 13.1 %collective-permute-start.38 = (bf16[384,128]{1,0:T(8,128)(2,1)}, bf16[384,128]{1,0:T(8,128)(2,1)S(1)}, u32[]{:S(2)}, u32[]{:S(2)}) collective-permute-start(bf16[384,128]{1,0:T(8,128)(2,1)} %get-tuple-element.230), channel_id=1, source_target_pairs={{4,2},{6,0},{8,14},{10,12},{20,18},{22,16},{24,30},{26,28},{5,3},{... | collective-permute-start | bytes 294920 | tf_op jit(solution)/shard_map/ppermute | solution.py:652
  230.6 11.4 %copy-start.14 = (bf16[384,128]{1,0:T(8,128)(2,1)}, bf16[384,128]{1,0:T(8,128)(2,1)S(1)}, u32[]{:S(2)}) copy-start(bf16[384,128]{1,0:T(8,128)(2,1)S(1)} %collective-permute-done.37.refs_4_) | copy-start | bytes 294916
  230.6 9.8 %collective-permute-start.42 = (bf16[384,128]{1,0:T(8,128)(2,1)}, bf16[384,128]{1,0:T(8,128)(2,1)S(1)}, u32[]{:S(2)}, u32[]{:S(2)}) collective-permute-start(bf16[384,128]{1,0:T(8,128)(2,1)} %get-tuple-element.235), channel_id=1, source_target_pairs={{4,16},{6,18},{8,28},{10,30},{20,0},{22,2},{24,12},{26,14},{5,17},... | collective-permute-start | bytes 294920 | tf_op jit(solution)/shard_map/ppermute | solution.py:652
  231.9 10.1 %copy-start.15 = (bf16[384,128]{1,0:T(8,128)(2,1)}, bf16[384,128]{1,0:T(8,128)(2,1)S(1)}, u32[]{:S(2)}) copy-start(bf16[384,128]{1,0:T(8,128)(2,1)S(1)} %collective-permute-done.38.refs_5_) | copy-start | bytes 294916
  231.9 10.1 %collective-permute-start.43 = (bf16[384,128]{1,0:T(8,128)(2,1)}, bf16[384,128]{1,0:T(8,128)(2,1)S(1)}, u32[]{:S(2)}, u32[]{:S(2)}) collective-permute-start(bf16[384,128]{1,0:T(8,128)(2,1)} %get-tuple-element.236), channel_id=1, source_target_pairs={{4,18},{6,16},{8,30},{10,28},{20,2},{22,0},{24,14},{26,12},{5,19},... | collective-permute-start | bytes 294920 | tf_op jit(solution)/shard_map/ppermute | solution.py:652
  233.9 8.1 %copy-start.12 = (bf16[384,384]{1,0:T(8,128)(2,1)}, bf16[384,384]{1,0:T(8,128)(2,1)S(1)}, u32[]{:S(2)}) copy-start(bf16[384,384]{1,0:T(8,128)(2,1)S(1)} %collective-permute-done.34.refs_1_) | copy-start | bytes 884740
  233.9 8.1 %copy-start.13 = (bf16[384,384]{1,0:T(8,128)(2,1)}, bf16[384,384]{1,0:T(8,128)(2,1)S(1)}, u32[]{:S(2)}) copy-start(bf16[384,384]{1,0:T(8,128)(2,1)S(1)} %collective-permute-done.35.refs_2_) | copy-start | bytes 884740
  240.5 1.6 copy-start.16
  242.0 0.6 copy-start.17

commit v5 on v3

--- a/solution.py
+++ b/solution.py
@@ -273,7 +273,7 @@
         start_stage(*stage)
     for copy in carry_copies():
         copy.start()
-    ready, waiting, step = set(), [], 384
+    ready, waiting, step = set(), [], plan.step
     for index, (i, n) in enumerate(stages):
         low, high = plan.uses[i][n]
         pltpu.make_async_copy(features(i, n), features(i, n), token_sems.at[i, n]).wait()
@@ -291,8 +291,7 @@
             if n == mine[j][0] and j in plan.added[i]:
                 partial_copy(i, j).wait()
 
-        @pl.loop(0, tokens // step)
-        def _(r):
+        def project(r):
             local = pl.ds(pl.multiple_of(r * step, step), step)
             rows = pl.ds(pl.multiple_of(i * tokens + r * step, step), step)
             term = jnp.dot(
@@ -308,6 +307,11 @@
                     projected_ref[i % 2, local, :] = value.astype(jnp.bfloat16)
                 else:
                     total_ref[rows, j * wide : (j + 1) * wide] = value
+
+        if step == tokens:
+            project(0)
+        else:
+            pl.loop(0, tokens // step)(project)
 
         for j in range(low, high):
             if n != mine[j][-1]:
@@ -329,7 +333,7 @@
                 out_copy(i, j).wait()
 
 
-def run_jobs(role, tokens, wide, images, weights):
+def run_jobs(role, tokens, wide, images, weights, step=384):
     images = [
         dict(
             image,
@@ -352,6 +356,7 @@
         added=[tuple(image["sums"]) for image in images],
         finished=[image["finish"] for image in images],
         carried=[len(image["carry"][0]) for image in images],
+        step=step,
     )
     operands = [x for i in images for place in i["pieces"] for owner in place for x, _ in owner]
     slab = operands[0].shape[1] // 2
@@ -407,41 +412,62 @@
 
 
 def join_kernel(place_ref, *refs):
-    *parts, out_ref, sems = refs
+    *parts, out_ref, buf, sems = refs
     count = len(parts) // 2
     inner = place_ref[count]
     wide, head = parts[0].shape[1], parts[count].shape[1]
-
-    def copies(i, role):
+    kept = wide - head
+
+    def arrive(i):
+        return pltpu.make_async_copy(parts[i], buf.at[i], sems.at[i, 0])
+
+    def leave(i, role):
         begin = pl.multiple_of(place_ref[i] * wide, wide)
         if role:
-            yield parts[i], out_ref.at[:, pl.ds(begin, wide)], sems.at[i, 0]
-            return
-        kept = wide - head
-        yield parts[i].at[:, pl.ds(head, kept)], out_ref.at[:, pl.ds(begin, kept)], sems.at[i, 0]
-        last = pl.multiple_of(begin + kept, head)
-        yield parts[count + i], out_ref.at[:, pl.ds(last, head)], sems.at[i, 1]
+            target = out_ref.at[:, pl.ds(begin, wide)]
+            return [pltpu.make_async_copy(buf.at[i], target, sems.at[i, 1])]
+        first, last = pl.ds(begin, kept), pl.ds(pl.multiple_of(begin + kept, head), head)
+        return [
+            pltpu.make_async_copy(
+                buf.at[i, :, pl.ds(head, kept)], out_ref.at[:, first], sems.at[i, 1]
+            ),
+            pltpu.make_async_copy(parts[count + i], out_ref.at[:, last], sems.at[i, 2]),
+        ]
+
+    for i in range(count):
+        arrive(i).start()
+    for i in range(count):
+        arrive(i).wait()
+        for role in (1, 0):
+
+            @pl.when((inner == 1) == (role == 1))
+            def _():
+                for copy in leave(i, role):
+                    copy.start()
 
     for role in (1, 0):
 
         @pl.when((inner == 1) == (role == 1))
         def _():
-            every = [pltpu.make_async_copy(*c) for i in range(count) for c in copies(i, role)]
-            for copy in every:
-                copy.start()
-            for copy in every:
-                copy.wait()
+            for i in range(count):
+                for copy in leave(i, role):
+                    copy.wait()
 
 
 def join(places, inner, parts, back):
     rows, wide = parts[0].shape
-    anywhere = pl.BlockSpec(memory_space=pl.ANY)
+    anywhere, vmem = pl.BlockSpec(memory_space=pl.ANY), pl.BlockSpec(memory_space=pltpu.VMEM)
     return pl.pallas_call(
         join_kernel,
         out_shape=jax.ShapeDtypeStruct((rows, wide * len(parts)), jnp.bfloat16),
-        in_specs=[pl.BlockSpec(memory_space=pltpu.SMEM)] + [anywhere] * (2 * len(parts)),
-        out_specs=pl.BlockSpec(memory_space=pltpu.VMEM),
-        scratch_shapes=[pltpu.SemaphoreType.DMA((len(parts), 2))],
+        in_specs=[pl.BlockSpec(memory_space=pltpu.SMEM)]
+        + [anywhere] * len(parts)
+        + [vmem] * len(back),
+        out_specs=anywhere,
+        scratch_shapes=[
+            pltpu.VMEM((len(parts), *parts[0].shape), jnp.bfloat16),
+            pltpu.SemaphoreType.DMA((len(parts), 3)),
+        ],
         cost_estimate=pl.CostEstimate(
             flops=0, bytes_accessed=4 * rows * wide * len(parts), transcendentals=0
         ),
@@ -533,7 +559,7 @@
     pair3, middle3 = pair(give), middle(own1)
     beside3, across3 = beside(across1), across(beside2)
     give = pick(middle2, own1)
-    far2 = others(beside2, across2)
+    far2 = others(across2, beside2)[::-1]
     pair3, middle3, beside3, across3, pair1, pair2, own2, far2, give = wait(
         (pair3, middle3, beside3, across3, pair1, pair2, own2, far2, give)
     )
@@ -581,7 +607,7 @@
 
     pair6, middle6 = outward(middle5), middle(pair5)
     beside6, across6 = beside(across4), across(beside5)
-    far5, far_across4 = others(beside5, across4)
+    far_across4, far5 = others(across4, beside5)
     ahead0, ahead1 = run(
         [
             dict(
@@ -616,7 +642,9 @@
     )
     lent1 = (((across4, across5), (far_across4, far_across5)), ((beside6, across6), far6))
     (lent1,) = run(
-        [dict(pieces=lent1, uses=[(0, 1)] * 4, finish=(0,))], [*lent_weights, (3, 0, [middle6])]
+        [dict(pieces=lent1, uses=[(0, 1)] * 4, finish=(0,))],
+        [*lent_weights, (3, 0, [middle6])],
+        step=seqs * rows,
     )
 
     def hand_back(mixed):

time: 247 us -> 249 us (level)
  waiting for transfers between devices: 77.2 us -> 80.4 us
    ppermute x10, waiting for transfers between devices: 0.03 us -> 3.2 us  [others(): got.append(lax.ppermute(value, 'head', swap))]
  transfers between devices with their start and end apart: 44 -> 44, of which waited for: 10 -> 13; matrix products, arithmetic and copies ran while one was open for 7% -> 7% of each run, Pallas kernels for 35% -> 34%
where the time goes in v5:
time: 249 us; the launch traced here: 248 us
  Pallas kernels  93.5 us (38%)
  waiting for transfers between devices  80.4 us (32%)
  starting transfers between devices  50.5 us (20%)
  local copies, waits for them, and re-layouts  13.1 us (5%)
  other arithmetic  9.68 us (4%)
    pallas_call x6, Pallas kernels, run_jobs(): pl.pallas_call(functools.partial(job_kernel, plan), out_shape=shapes, in_...  79.3 us
    ppermute x5, waiting for transfers between devices, pair(): return lax.ppermute(value, 'dp', [(0, 1), (1, 0), (2, 3), (3, 2)])  43.8 us
    ppermute x6, waiting for transfers between devices, shared(): beside = lambda value: lax.ppermute(value, 'seq', swap)  17.5 us
    ppermute x5, starting transfers between devices, pair(): return lax.ppermute(value, 'dp', [(0, 1), (1, 0), (2, 3), (3, 2)])  15.9 us
    pallas_call x2, Pallas kernels, normalize_part(): pl.pallas_call(normalize_kernel, out_shape=[half] * 2 + [jax.ShapeDtypeSt...  11.1 us
    ppermute x6, starting transfers between devices, middle(): return lax.ppermute(value, 'dp', [(1, 2), (2, 1)])  9.16 us
    ppermute x4, waiting for transfers between devices, hand_back(): got.append(lax.ppermute(sent, ('groups', 'dp', 'seq'), steps))  8.62 us
    ppermute x6, starting transfers between devices, shared(): beside = lambda value: lax.ppermute(value, 'seq', swap)  8.2 us
  transfers between devices with their start and end apart: 44, of which 13 were waited for; matrix products, arithmetic and copies ran while one was open for 7% of the time, Pallas kernels for 34%

profile of v5, /device:TPU:0, one launch (start us, length us, event | category | flops | bytes accessed | tf_op | source)
XLA Modules:
  0.0 247.7 jit_solution(15878566195124792767)
XLA Ops:
  0.0 0.7 stack.70.place_ref
  0.7 5.7 %shard_map.37 = (bf16[192,3072]{1,0:T(8,128)(2,1)}, bf16[192,3072]{1,0:T(8,128)(2,1)}, bf16[1536,384]{1,0:T(8,128)(2,1)}) custom-call(s32[6]{0:T(128)} %stack.70.place_ref, bf16[1,384,6144]{2,1,0:T(8,128)(2,1)} %tokens_ref.2, f32[1,6144]{1,0:T(1,128)} %bitcast.41, bf16[6,1536,384]{2,1,0:T(8,128)(2,1)} %bitcast.29), custom_call_target="tpu_custom_call" | custom-call | flops 9437184 | bytes 4718592 | tf_op jit(solution)/shard_map/pallas_call | solution.py:120
  6.4 3.0 %collective-permute-start = (bf16[192,3072]{1,0:T(8,128)(2,1)}, bf16[192,3072]{1,0:T(8,128)(2,1)S(1)}, u32[]{:S(2)}, u32[]{:S(2)}) collective-permute-start(bf16[192,3072]{1,0:T(8,128)(2,1)} %get-tuple-element.124.refs_0_.refs_8_), channel_id=1, source_target_pairs={{0,2},{2,0},{1,3},{3,1},{4,6},{6,4},{5,7},{7,5},{8,10},{10,8},{9,1... | collective-permute-start | bytes 3538952 | tf_op jit(solution)/shard_map/ppermute | solution.py:503
  9.4 1.5 collective-permute-start.1
  10.9 1.6 collective-permute-start.2
  12.5 1.7 collective-permute-start.3
  14.1 2.9 %dynamic-slice_bitcast_fusion = (bf16[1536,384]{1,0:T(8,128)(2,1)}, bf16[1,1536,384]{2,1,0:T(8,128)(2,1)S(1)}) fusion(bf16[6,1536,384]{2,1,0:T(8,128)(2,1)} %bitcast.30, s32[]{:T(128)S(6)} %select_n.77, s32[]{:T(128)S(6)} %select_n.76), kind=kLoop, calls=%fused_computation.1 | loop fusion | bytes 4718600 | tf_op jit(solution)/shard_map/jit(dynamic_index_in_dim)/squeeze | solution.py:540
  17.2 1.5 copy-done.1
  18.7 1.2 broadcast_select_fusion.3
  19.9 0.6 pad_add_fusion.role_ref
  20.5 15.0 %collective-permute-done.refs_4_.refs_12_ = bf16[192,3072]{1,0:T(8,128)(2,1)S(1)} collective-permute-done((bf16[192,3072]{1,0:T(8,128)(2,1)}, bf16[192,3072]{1,0:T(8,128)(2,1)S(1)}, u32[]{:S(2)}, u32[]{:S(2)}) %collective-permute-start) | collective-permute-done | bytes 1179680 | tf_op jit(solution)/shard_map/ppermute | solution.py:503
  35.5 1.6 collective-permute-done.1.refs_0_.refs_8_
  37.1 1.2 collective-permute-start.6
  38.3 1.5 collective-permute-start.7
  39.8 3.1 %collective-permute-start.4 = (bf16[192,3072]{1,0:T(8,128)(2,1)}, bf16[192,3072]{1,0:T(8,128)(2,1)}, u32[]{:S(2)}, u32[]{:S(2)}) collective-permute-start(bf16[192,3072]{1,0:T(8,128)(2,1)} %broadcast_select_fusion.3), channel_id=1, source_target_pairs={{0,4},{4,0},{8,12},{12,8},{1,5},{5,1},{9,13},{13,9},{2,6},{6,2},{1... | collective-permute-start | bytes 3538952 | tf_op jit(solution)/shard_map/ppermute | solution.py:494
  42.9 1.7 collective-permute-start.5
  44.6 1.1 copy-done.5
  45.7 0.7 stack.73.place_ref
  46.3 2.5 %copy.8 = bf16[24,8,8,384]{3,1,2,0:T(8,128)(2,1)} copy(bf16[24,8,8,384]{3,1,0,2:T(8,128)(2,1)} %bitcast.27) | data formatting | bytes 2359296
  48.9 5.4 %shard_map.38 = (bf16[192,3072]{1,0:T(8,128)(2,1)}, bf16[192,3072]{1,0:T(8,128)(2,1)}) custom-call(s32[5]{0:T(128)} %stack.73.place_ref, bf16[1,384,6144]{2,1,0:T(8,128)(2,1)} %tokens_ref.2, f32[1,6144]{1,0:T(1,128)} %bitcast.42, bf16[6,1536,384]{2,1,0:T(8,128)(2,1)} %bitcast.31), custom_call_target="tpu_custom_call" | custom-call | flops 9437184 | bytes 4718592 | tf_op jit(solution)/shard_map/pallas_call | solution.py:120
  54.2 1.4 broadcast_select_fusion.2
  55.6 12.3 %collective-permute-done.4.refs_25_.refs_0_.refs_16_ = bf16[192,3072]{1,0:T(8,128)(2,1)} collective-permute-done((bf16[192,3072]{1,0:T(8,128)(2,1)}, bf16[192,3072]{1,0:T(8,128)(2,1)}, u32[]{:S(2)}, u32[]{:S(2)}) %collective-permute-start.4) | collective-permute-done | bytes 1179680 | tf_op jit(solution)/shard_map/ppermute | solution.py:494
  68.1 4.7 %collective-permute-start.10 = (bf16[192,3072]{1,0:T(8,128)(2,1)S(1)}, bf16[192,3072]{1,0:T(8,128)(2,1)S(1)}, u32[]{:S(2)}, u32[]{:S(2)}) collective-permute-start(bf16[192,3072]{1,0:T(8,128)(2,1)S(1)} %broadcast_select_fusion.2), channel_id=1, source_target_pairs={{0,4},{4,0},{8,12},{12,8},{1,5},{5,1},{9,13},{13,9},{2,6},{6,2},{1... | collective-permute-start | bytes 3538952 | tf_op jit(solution)/shard_map/ppermute | solution.py:494
  72.7 0.7 collective-permute-start.11
  73.4 0.9 collective-permute-start.12
  74.9 1.2 broadcast_select_fusion.1
  76.1 23.2 %collective-permute-done.10.refs_28_.refs_1_.refs_17_ = bf16[192,3072]{1,0:T(8,128)(2,1)S(1)} collective-permute-done((bf16[192,3072]{1,0:T(8,128)(2,1)S(1)}, bf16[192,3072]{1,0:T(8,128)(2,1)S(1)}, u32[]{:S(2)}, u32[]{:S(2)}) %collective-permute-start.10) | collective-permute-done | bytes 1179680 | tf_op jit(solution)/shard_map/ppermute | solution.py:494
  99.3 2.5 %collective-permute-done.12.refs_4_.refs_12_ = bf16[192,3072]{1,0:T(8,128)(2,1)S(1)} collective-permute-done((bf16[192,3072]{1,0:T(8,128)(2,1)}, bf16[192,3072]{1,0:T(8,128)(2,1)S(1)}, u32[]{:S(2)}, u32[]{:S(2)}) %collective-permute-start.12) | collective-permute-done | bytes 1179680 | tf_op jit(solution)/shard_map/ppermute | solution.py:503
  101.8 0.7 collective-permute-done.13.refs_5_.refs_13_
  102.8 1.0 collective-permute-start.18
  104.3 2.9 %collective-permute-start.16 = (bf16[1536,384]{1,0:T(8,128)(2,1)}, bf16[1536,384]{1,0:T(8,128)(2,1)}, u32[]{:S(2)}, u32[]{:S(2)}) collective-permute-start(bf16[1536,384]{1,0:T(8,128)(2,1)} %broadcast_select_fusion.1), channel_id=1, source_target_pairs={{0,4},{4,0},{8,12},{12,8},{1,5},{5,1},{9,13},{13,9},{2,6},{6,2},{1... | collective-permute-start | bytes 3538952 | tf_op jit(solution)/shard_map/ppermute | solution.py:494
  107.2 1.7 collective-permute-start.17
  108.9 1.0 copy-done.8
  109.9 2.8 %pad_maximum_fusion = bf16[384,3072]{1,0:T(8,128)(2,1)} fusion(bf16[192,3072]{1,0:T(8,128)(2,1)S(1)} %collective-permute-done.10.refs_28_.refs_1_.refs_17_, bf16[192,3072]{1,0:T(8,128)(2,1)} %collective-permute-done.4.refs_25_.refs_0_.refs_16_), kind=kLoop, calls=%fused_computation | loop fusion | flops 4718592 | bytes 4718592 | tf_op jit(solution)/shard_map/concatenate | solution.py:580
  112.7 2.5 %broadcast_select_fusion = bf16[1536,384]{1,0:T(8,128)(2,1)} fusion(bf16[1536,384]{1,0:T(8,128)(2,1)S(1)} %collective-permute-done.11.refs_14_.refs_22_, bf16[1536,384]{1,0:T(8,128)(2,1)} %get-tuple-element.210.refs_11_.refs_19_.refs_10_, pred[]{:T(512)S(6)} %or.4), kind=kLoop, calls=%fused_computation.2 | loop fusion | flops 589824 | bytes 3538945 | tf_op jit(solution)/shard_map/jit(_where)/select_n | solution.py:491
  115.2 14.6 %shard_map.39 = (bf16[384,128]{1,0:T(8,128)(2,1)}, bf16[384,128]{1,0:T(8,128)(2,1)}, f32[768,384]{1,0:T(8,128)}, f32[768,384]{1,0:T(8,128)}) custom-call(s32[2]{0:T(128)} %pad_add_fusion.role_ref, bf16[192,3072]{1,0:T(8,128)(2,1)} %get-tuple-element.124.refs_0_.refs_8_, bf16[192,3072]{1,0:T(8,128)(2,1)} %get-tuple-element.132.refs_1_.refs_9_, ...), custom_call_target="tpu_custom_call" | custom-call | flops 6341787648 | tf_op jit(solution)/shard_map/pallas_call | solution.py:383
  129.8 3.7 %collective-permute-done.16.refs_27_.refs_17_ = bf16[1536,384]{1,0:T(8,128)(2,1)} collective-permute-done((bf16[1536,384]{1,0:T(8,128)(2,1)}, bf16[1536,384]{1,0:T(8,128)(2,1)}, u32[]{:S(2)}, u32[]{:S(2)}) %collective-permute-start.16) | collective-permute-done | bytes 1179680 | tf_op jit(solution)/shard_map/ppermute | solution.py:494
  133.6 1.2 collective-permute-start.24
  134.8 1.5 collective-permute-start.25
  136.3 3.6 %collective-permute-start.22 = (bf16[1536,384]{1,0:T(8,128)(2,1)}, bf16[1536,384]{1,0:T(8,128)(2,1)}, u32[]{:S(2)}, u32[]{:S(2)}) collective-permute-start(bf16[1536,384]{1,0:T(8,128)(2,1)} %broadcast_select_fusion), channel_id=1, source_target_pairs={{0,4},{4,0},{8,12},{12,8},{1,5},{5,1},{9,13},{13,9},{2,6},{6,2},{1... | collective-permute-start | bytes 3538952 | tf_op jit(solution)/shard_map/ppermute | solution.py:494
  139.9 1.7 collective-permute-start.23
  141.7 20.0 %shard_map.40 = (bf16[384,128]{1,0:T(8,128)(2,1)}, bf16[384,128]{1,0:T(8,128)(2,1)}, f32[768,384]{1,0:T(8,128)}, f32[768,384]{1,0:T(8,128)}, f32[768,384]{1,0:T(8,128)}, /*index=5*/f32[768,384]{1,0:T(8,128)}) custom-call(s32[2]{0:T(128)} %pad_add_fusion.role_ref, bf16[192,3072]{1,0:T(8,128)(2,1)} %collective-permute-done.1.refs_0_.refs_8_, ...), custom_call_target="tpu_custom_call" | custom-call | flops 9965666304 | tf_op jit(solution)/shard_map/pallas_call | solution.py:383
  161.7 4.6 %collective-permute-done.22.refs_18_.refs_8_ = bf16[1536,384]{1,0:T(8,128)(2,1)} collective-permute-done((bf16[1536,384]{1,0:T(8,128)(2,1)}, bf16[1536,384]{1,0:T(8,128)(2,1)}, u32[]{:S(2)}, u32[]{:S(2)}) %collective-permute-start.22) | collective-permute-done | bytes 1179680 | tf_op jit(solution)/shard_map/ppermute | solution.py:494
  166.4 3.2 %collective-permute-done.28.refs_2_ = bf16[192,3072]{1,0:T(8,128)(2,1)} collective-permute-done((bf16[192,3072]{1,0:T(8,128)(2,1)}, bf16[192,3072]{1,0:T(8,128)(2,1)}, u32[]{:S(2)}, u32[]{:S(2)}) %collective-permute-start.28) | collective-permute-done | bytes 1179680 | tf_op jit(solution)/shard_map/ppermute | solution.py:511
  169.7 1.3 collective-permute-start.30
  171.0 1.7 collective-permute-start.31
  172.6 0.9 collective-permute-start.32
  174.1 13.0 %shard_map.41 = (bf16[384,128]{1,0:T(8,128)(2,1)}, bf16[384,128]{1,0:T(8,128)(2,1)}, f32[768,384]{1,0:T(8,128)}, bf16[384,128]{1,0:T(8,128)(2,1)}, bf16[384,128]{1,0:T(8,128)(2,1)}, /*index=5*/f32[768,384]{1,0:T(8,128)}) custom-call(s32[2]{0:T(128)} %pad_add_fusion.role_ref, bf16[192,3072]{1,0:T(8,128)(2,1)} %get-tuple-element.124.refs_0_.refs_8_, ...), custom_call_target="tpu_custom_call" | custom-call | flops 3623878656 | tf_op jit(solution)/shard_map/pallas_call | solution.py:383
  187.1 1.0 copy-done.9
  188.2 8.8 %shard_map.42.refs_28_ = f32[768,384]{1,0:T(8,128)} custom-call(s32[2]{0:T(128)} %pad_add_fusion.role_ref, bf16[192,3072]{1,0:T(8,128)(2,1)} %collective-permute-done.4.refs_25_.refs_0_.refs_16_, bf16[192,3072]{1,0:T(8,128)(2,1)} %copy-done.2, bf16[384,3072]{1,0:T(8,128)(2,1)} %collective-permute-done.26.refs_2_.refs_3_.refs_18_.refs_19_, ...), custom_call_target="tpu_custom_call" | custom-call | flops 2717908992 | tf_op jit(solution)/shard_map/pallas_call | solution.py:383
  196.9 4.5 %collective-permute-done.30.refs_25_ = bf16[1536,384]{1,0:T(8,128)(2,1)} collective-permute-done((bf16[1536,384]{1,0:T(8,128)(2,1)}, bf16[1536,384]{1,0:T(8,128)(2,1)}, u32[]{:S(2)}, u32[]{:S(2)}) %collective-permute-start.30) | collective-permute-done | bytes 1179680 | tf_op jit(solution)/shard_map/ppermute | solution.py:497
  202.4 12.8 %shard_map.43 = (bf16[384,384]{1,0:T(8,128)(2,1)}, bf16[384,384]{1,0:T(8,128)(2,1)}, bf16[384,384]{1,0:T(8,128)(2,1)}, bf16[384,384]{1,0:T(8,128)(2,1)}, bf16[38...) custom-call(s32[2]{0:T(128)} %pad_add_fusion.role_ref, bf16[192,3072]{1,0:T(8,128)(2,1)} %get-tuple-element.124.refs_0_.refs_8_, ...), custom_call_target="tpu_custom_call" | custom-call | flops 2717908992 | tf_op jit(solution)/shard_map/pallas_call | solution.py:383
  215.2 1.2 collective-permute-start.34
  216.9 1.9 collective-permute-start.36
  218.8 1.3 collective-permute-start.37
  220.1 1.6 collective-permute-start.38
  221.6 10.2 %shard_map.44 = (bf16[384,128]{1,0:T(8,128)(2,1)}, bf16[384,128]{1,0:T(8,128)(2,1)}) custom-call(s32[2]{0:T(128)} %pad_add_fusion.role_ref, bf16[192,3072]{1,0:T(8,128)(2,1)} %collective-permute-done.19.refs_0_, bf16[192,3072]{1,0:T(8,128)(2,1)} %collective-permute-done.25.refs_1_, bf16[192,3072]{1,0:T(8,128)(2,1)} %collective-permute-done.28.refs_2_, ...), custom_call_target="tpu_custom_call" | custom-call | flops 3623878656 | tf_op jit(solution)/shard_map/pallas_call | solution.py:383
  231.8 1.3 collective-permute-start.42
  233.2 1.3 collective-permute-start.43
  234.5 0.6 stack.63.place_ref
  235.1 6.8 %collective-permute-done.42.refs_6_ = bf16[384,128]{1,0:T(8,128)(2,1)S(1)} collective-permute-done((bf16[384,128]{1,0:T(8,128)(2,1)}, bf16[384,128]{1,0:T(8,128)(2,1)S(1)}, u32[]{:S(2)}, u32[]{:S(2)}) %collective-permute-start.42) | collective-permute-done | bytes 98336 | tf_op jit(solution)/shard_map/ppermute | solution.py:664
  241.9 1.9 collective-permute-done.43.refs_7_
  243.8 0.6 copy-done.17
  244.4 3.1 %shard_map.45 = bf16[384,1536]{1,0:T(8,128)(2,1)} custom-call(s32[5]{0:T(128)} %stack.63.place_ref, bf16[384,384]{1,0:T(8,128)(2,1)} %get-tuple-element.225.refs_0_, bf16[384,384]{1,0:T(8,128)(2,1)} %copy-done.12, bf16[384,384]{1,0:T(8,128)(2,1)} %copy-done.13, bf16[384,384]{1,0:T(8,128)(2,1)} %collective-permute-done.36.refs_3_, ...), custom_call_target="tpu_custom_call" | custom-call | bytes 2359296 | tf_op jit(solution)/shard_map/pallas_call | solution.py:460
  (81 shorter events, 4.0 us)
Async XLA Ops:
  6.4 29.2 %collective-permute-start = (bf16[192,3072]{1,0:T(8,128)(2,1)}, bf16[192,3072]{1,0:T(8,128)(2,1)S(1)}, u32[]{:S(2)}, u32[]{:S(2)}) collective-permute-start(bf16[192,3072]{1,0:T(8,128)(2,1)} %get-tuple-element.124.refs_0_.refs_8_), channel_id=1, source_target_pairs={{0,2},{2,0},{1,3},{3,1},{4,6},{6,4},{5,7},{7,5},{8,10},{10,8},{9,1... | collective-permute-start | bytes 3538952 | tf_op jit(solution)/shard_map/ppermute | solution.py:503
  9.4 27.7 %collective-permute-start.1 = (bf16[192,3072]{1,0:T(8,128)(2,1)}, bf16[192,3072]{1,0:T(8,128)(2,1)}, u32[]{:S(2)}, u32[]{:S(2)}) collective-permute-start(bf16[192,3072]{1,0:T(8,128)(2,1)} %get-tuple-element.124.refs_0_.refs_8_), channel_id=1, source_target_pairs={{0,16},{16,0},{1,17},{17,1},{2,18},{18,2},{3,19},{19,3},{4,20},{20... | collective-permute-start | bytes 3538952 | tf_op jit(solution)/shard_map/ppermute | solution.py:504
  10.9 28.9 %collective-permute-start.2 = (bf16[1536,384]{1,0:T(8,128)(2,1)}, bf16[1536,384]{1,0:T(8,128)(2,1)}, u32[]{:S(2)}, u32[]{:S(2)}) collective-permute-start(bf16[1536,384]{1,0:T(8,128)(2,1)} %get-tuple-element.128.refs_8_.refs_10_.refs_16_.refs_18_), channel_id=1, source_target_pairs={{0,4},{4,0},{8,12},{12,8},{1,5},{5,1},{9,13},{13,9},{2,6},{6,2},{1... | collective-permute-start | bytes 3538952 | tf_op jit(solution)/shard_map/ppermute | solution.py:494
  12.5 27.4 %collective-permute-start.3 = (bf16[1536,384]{1,0:T(8,128)(2,1)}, bf16[1536,384]{1,0:T(8,128)(2,1)}, u32[]{:S(2)}, u32[]{:S(2)}) collective-permute-start(bf16[1536,384]{1,0:T(8,128)(2,1)} %get-tuple-element.128.refs_8_.refs_10_.refs_16_.refs_18_), channel_id=1, source_target_pairs={{4,8},{8,4},{5,9},{9,5},{6,10},{10,6},{7,11},{11,7},{20,24},{24,20... | collective-permute-start | bytes 3538952 | tf_op jit(solution)/shard_map/ppermute | solution.py:500
  17.0 57.8 %copy-start = (bf16[1,1536,384]{2,1,0:T(8,128)(2,1)}, bf16[1,1536,384]{2,1,0:T(8,128)(2,1)S(1)}, u32[]{:S(2)}) copy-start(bf16[1,1536,384]{2,1,0:T(8,128)(2,1)S(1)} %get-tuple-element.238) | copy-start | bytes 3538948
  17.0 1.7 copy-start.1
  35.5 1.6 copy-start.4
  37.1 7.5 %collective-permute-start.8 = (bf16[192,3072]{1,0:T(8,128)(2,1)S(1)}, bf16[192,3072]{1,0:T(8,128)(2,1)S(1)}, u32[]{:S(2)}, u32[]{:S(2)}) collective-permute-start(bf16[192,3072]{1,0:T(8,128)(2,1)S(1)} %collective-permute-done.refs_4_.refs_12_), channel_id=1, source_target_pairs={{0,1},{1,0},{2,3},{3,2},{4,5},{5,4},{6,7},{7,6},{8,9},{9,8},{10,11... | collective-permute-start | bytes 3538952 | tf_op jit(solution)/shard_map/ppermute | solution.py:511
  37.1 30.9 %collective-permute-start.6 = (bf16[192,3072]{1,0:T(8,128)(2,1)}, bf16[192,3072]{1,0:T(8,128)(2,1)}, u32[]{:S(2)}, u32[]{:S(2)}) collective-permute-start(bf16[192,3072]{1,0:T(8,128)(2,1)} %get-tuple-element.132.refs_1_.refs_9_), channel_id=1, source_target_pairs={{0,2},{2,0},{1,3},{3,1},{4,6},{6,4},{5,7},{7,5},{8,10},{10,8},{9,1... | collective-permute-start | bytes 3538952 | tf_op jit(solution)/shard_map/ppermute | solution.py:503
  38.3 29.7 %collective-permute-start.7 = (bf16[192,3072]{1,0:T(8,128)(2,1)}, bf16[192,3072]{1,0:T(8,128)(2,1)}, u32[]{:S(2)}, u32[]{:S(2)}) collective-permute-start(bf16[192,3072]{1,0:T(8,128)(2,1)} %get-tuple-element.132.refs_1_.refs_9_), channel_id=1, source_target_pairs={{0,16},{16,0},{1,17},{17,1},{2,18},{18,2},{3,19},{19,3},{4,20},{20... | collective-permute-start | bytes 3538952 | tf_op jit(solution)/shard_map/ppermute | solution.py:504
  39.8 28.1 %collective-permute-start.4 = (bf16[192,3072]{1,0:T(8,128)(2,1)}, bf16[192,3072]{1,0:T(8,128)(2,1)}, u32[]{:S(2)}, u32[]{:S(2)}) collective-permute-start(bf16[192,3072]{1,0:T(8,128)(2,1)} %broadcast_select_fusion.3), channel_id=1, source_target_pairs={{0,4},{4,0},{8,12},{12,8},{1,5},{5,1},{9,13},{13,9},{2,6},{6,2},{1... | collective-permute-start | bytes 3538952 | tf_op jit(solution)/shard_map/ppermute | solution.py:494
  42.9 25.0 %collective-permute-start.5 = (bf16[1536,384]{1,0:T(8,128)(2,1)}, bf16[1536,384]{1,0:T(8,128)(2,1)}, u32[]{:S(2)}, u32[]{:S(2)}) collective-permute-start(bf16[1536,384]{1,0:T(8,128)(2,1)} %collective-permute-done.2.refs_15_.refs_16_.refs_23_.refs_26_), channel_id=1, source_target_pairs={{4,8},{8,4},{5,9},{9,5},{6,10},{10,6},{7,11},{11,7},{20,24},{24,20... | collective-permute-start | bytes 3538952 | tf_op jit(solution)/shard_map/ppermute | solution.py:500
  44.6 1.1 copy-start.5
  45.7 22.3 %collective-permute-start.9 = (bf16[192,3072]{1,0:T(8,128)(2,1)}, bf16[192,3072]{1,0:T(8,128)(2,1)}, u32[]{:S(2)}, u32[]{:S(2)}) collective-permute-start(bf16[192,3072]{1,0:T(8,128)(2,1)} %collective-permute-done.1.refs_0_.refs_8_), channel_id=1, source_target_pairs={{0,1},{1,0},{2,3},{3,2},{4,5},{5,4},{6,7},{7,6},{8,9},{9,8},{10,11... | collective-permute-start | bytes 3538952 | tf_op jit(solution)/shard_map/ppermute | solution.py:511
  68.0 6.9 %collective-permute-start.14 = (bf16[192,3072]{1,0:T(8,128)(2,1)}, bf16[192,3072]{1,0:T(8,128)(2,1)}, u32[]{:S(2)}, u32[]{:S(2)}) collective-permute-start(bf16[192,3072]{1,0:T(8,128)(2,1)} %collective-permute-done.7.refs_1_.refs_9_), channel_id=1, source_target_pairs={{0,1},{1,0},{2,3},{3,2},{4,5},{5,4},{6,7},{7,6},{8,9},{9,8},{10,11... | collective-permute-start | bytes 3538952 | tf_op jit(solution)/shard_map/ppermute | solution.py:511
  68.1 31.2 %collective-permute-start.10 = (bf16[192,3072]{1,0:T(8,128)(2,1)S(1)}, bf16[192,3072]{1,0:T(8,128)(2,1)S(1)}, u32[]{:S(2)}, u32[]{:S(2)}) collective-permute-start(bf16[192,3072]{1,0:T(8,128)(2,1)S(1)} %broadcast_select_fusion.2), channel_id=1, source_target_pairs={{0,4},{4,0},{8,12},{12,8},{1,5},{5,1},{9,13},{13,9},{2,6},{6,2},{1... | collective-permute-start | bytes 3538952 | tf_op jit(solution)/shard_map/ppermute | solution.py:494
  72.7 26.6 %collective-permute-start.11 = (bf16[1536,384]{1,0:T(8,128)(2,1)S(1)}, bf16[1536,384]{1,0:T(8,128)(2,1)S(1)}, u32[]{:S(2)}, u32[]{:S(2)}) collective-permute-start(bf16[1536,384]{1,0:T(8,128)(2,1)S(1)} %bitcast.33), channel_id=1, source_target_pairs={{4,8},{8,4},{5,9},{9,5},{6,10},{10,6},{7,11},{11,7},{20,24},{24,20... | collective-permute-start | bytes 3538952 | tf_op jit(solution)/shard_map/ppermute | solution.py:500
  73.4 28.3 %collective-permute-start.12 = (bf16[192,3072]{1,0:T(8,128)(2,1)}, bf16[192,3072]{1,0:T(8,128)(2,1)S(1)}, u32[]{:S(2)}, u32[]{:S(2)}) collective-permute-start(bf16[192,3072]{1,0:T(8,128)(2,1)} %collective-permute-done.1.refs_0_.refs_8_), channel_id=1, source_target_pairs={{0,2},{2,0},{1,3},{3,1},{4,6},{6,4},{5,7},{7,5},{8,10},{10,8},{9,1... | collective-permute-start | bytes 3538952 | tf_op jit(solution)/shard_map/ppermute | solution.py:503
  74.4 28.1 %collective-permute-start.13 = (bf16[192,3072]{1,0:T(8,128)(2,1)}, bf16[192,3072]{1,0:T(8,128)(2,1)}, u32[]{:S(2)}, u32[]{:S(2)}) collective-permute-start(bf16[192,3072]{1,0:T(8,128)(2,1)} %collective-permute-done.6.refs_5_.refs_13_), channel_id=1, source_target_pairs={{0,16},{16,0},{1,17},{17,1},{2,18},{18,2},{3,19},{19,3},{4,20},{20... | collective-permute-start | bytes 3538952 | tf_op jit(solution)/shard_map/ppermute | solution.py:504
  74.9 27.6 %collective-permute-start.15 = (bf16[192,3072]{1,0:T(8,128)(2,1)}, bf16[192,3072]{1,0:T(8,128)(2,1)S(1)}, u32[]{:S(2)}, u32[]{:S(2)}) collective-permute-start(bf16[192,3072]{1,0:T(8,128)(2,1)} %collective-permute-done.6.refs_5_.refs_13_), channel_id=1, source_target_pairs={{0,1},{1,0},{2,3},{3,2},{4,5},{5,4},{6,7},{7,6},{8,9},{9,8},{10,11... | collective-permute-start | bytes 3538952 | tf_op jit(solution)/shard_map/ppermute | solution.py:511
  99.3 13.4 %copy-start.2 = (bf16[192,3072]{1,0:T(8,128)(2,1)}, bf16[192,3072]{1,0:T(8,128)(2,1)S(1)}, u32[]{:S(2)}) copy-start(bf16[192,3072]{1,0:T(8,128)(2,1)S(1)} %collective-permute-done.10.refs_28_.refs_1_.refs_17_) | copy-start | bytes 3538948
  99.3 13.4 %copy-start.10 = (bf16[1536,384]{1,0:T(8,128)(2,1)}, bf16[1536,384]{1,0:T(8,128)(2,1)S(1)}, u32[]{:S(2)}) copy-start(bf16[1536,384]{1,0:T(8,128)(2,1)S(1)} %collective-permute-done.11.refs_14_.refs_22_) | copy-start | bytes 3538948
  101.8 1.0 copy-start.6
  102.8 6.1 %copy-start.7 = (bf16[192,3072]{1,0:T(8,128)(2,1)}, bf16[192,3072]{1,0:T(8,128)(2,1)S(1)}, u32[]{:S(2)}) copy-start(bf16[192,3072]{1,0:T(8,128)(2,1)S(1)} %collective-permute-done.15.refs_7_.refs_15_) | copy-start | bytes 3538948
  102.8 6.1 %collective-permute-start.20 = (bf16[192,3072]{1,0:T(8,128)(2,1)S(1)}, bf16[192,3072]{1,0:T(8,128)(2,1)S(1)}, u32[]{:S(2)}, u32[]{:S(2)}) collective-permute-start(bf16[192,3072]{1,0:T(8,128)(2,1)S(1)} %collective-permute-done.12.refs_4_.refs_12_), channel_id=1, source_target_pairs={{0,1},{1,0},{2,3},{3,2},{4,5},{5,4},{6,7},{7,6},{8,9},{9,8},{10,11... | collective-permute-start | bytes 3538952 | tf_op jit(solution)/shard_map/ppermute | solution.py:511
  102.8 30.8 %collective-permute-start.18 = (bf16[192,3072]{1,0:T(8,128)(2,1)}, bf16[192,3072]{1,0:T(8,128)(2,1)}, u32[]{:S(2)}, u32[]{:S(2)}) collective-permute-start(bf16[192,3072]{1,0:T(8,128)(2,1)} %collective-permute-done.4.refs_25_.refs_0_.refs_16_), channel_id=1, source_target_pairs={{0,2},{2,0},{1,3},{3,1},{4,6},{6,4},{5,7},{7,5},{8,10},{10,8},{9,1... | collective-permute-start | bytes 3538952 | tf_op jit(solution)/shard_map/ppermute | solution.py:503
  103.8 29.8 %collective-permute-start.19 = (bf16[192,3072]{1,0:T(8,128)(2,1)}, bf16[192,3072]{1,0:T(8,128)(2,1)}, u32[]{:S(2)}, u32[]{:S(2)}) collective-permute-start(bf16[192,3072]{1,0:T(8,128)(2,1)} %collective-permute-done.4.refs_25_.refs_0_.refs_16_), channel_id=1, source_target_pairs={{0,16},{16,0},{1,17},{17,1},{2,18},{18,2},{3,19},{19,3},{4,20},{20... | collective-permute-start | bytes 3538952 | tf_op jit(solution)/shard_map/ppermute | solution.py:504
  104.3 29.2 %collective-permute-start.16 = (bf16[1536,384]{1,0:T(8,128)(2,1)}, bf16[1536,384]{1,0:T(8,128)(2,1)}, u32[]{:S(2)}, u32[]{:S(2)}) collective-permute-start(bf16[1536,384]{1,0:T(8,128)(2,1)} %broadcast_select_fusion.1), channel_id=1, source_target_pairs={{0,4},{4,0},{8,12},{12,8},{1,5},{5,1},{9,13},{13,9},{2,6},{6,2},{1... | collective-permute-start | bytes 3538952 | tf_op jit(solution)/shard_map/ppermute | solution.py:494
  107.2 26.3 %collective-permute-start.17 = (bf16[1536,384]{1,0:T(8,128)(2,1)}, bf16[1536,384]{1,0:T(8,128)(2,1)}, u32[]{:S(2)}, u32[]{:S(2)}) collective-permute-start(bf16[1536,384]{1,0:T(8,128)(2,1)} %get-tuple-element.210.refs_11_.refs_19_.refs_10_), channel_id=1, source_target_pairs={{4,8},{8,4},{5,9},{9,5},{6,10},{10,6},{7,11},{11,7},{20,24},{24,20... | collective-permute-start | bytes 3538952 | tf_op jit(solution)/shard_map/ppermute | solution.py:500
  108.9 1.0 copy-start.8
  109.9 23.6 %collective-permute-start.21 = (bf16[192,3072]{1,0:T(8,128)(2,1)}, bf16[192,3072]{1,0:T(8,128)(2,1)}, u32[]{:S(2)}, u32[]{:S(2)}) collective-permute-start(bf16[192,3072]{1,0:T(8,128)(2,1)} %collective-permute-done.13.refs_5_.refs_13_), channel_id=1, source_target_pairs={{0,1},{1,0},{2,3},{3,2},{4,5},{5,4},{6,7},{7,6},{8,9},{9,8},{10,11... | collective-permute-start | bytes 3538952 | tf_op jit(solution)/shard_map/ppermute | solution.py:511
  115.2 18.4 %copy-start.3 = (bf16[192,3072]{1,0:T(8,128)(2,1)S(1)}, bf16[192,3072]{1,0:T(8,128)(2,1)}, u32[]{:S(2)}) copy-start(bf16[192,3072]{1,0:T(8,128)(2,1)} %copy-done.2) | copy-start | bytes 3538948
  133.5 8.1 %collective-permute-start.26 = (bf16[384,3072]{1,0:T(8,128)(2,1)}, bf16[384,3072]{1,0:T(8,128)(2,1)}, u32[]{:S(2)}, u32[]{:S(2)}) collective-permute-start(bf16[384,3072]{1,0:T(8,128)(2,1)} %pad_maximum_fusion), channel_id=1, source_target_pairs={{0,1},{1,0},{2,3},{3,2},{4,5},{5,4},{6,7},{7,6},{8,9},{9,8},{10,11... | collective-permute-start | bytes 7077896 | tf_op jit(solution)/shard_map/ppermute | solution.py:511
  133.6 32.6 %collective-permute-start.24 = (bf16[192,3072]{1,0:T(8,128)(2,1)S(1)}, bf16[192,3072]{1,0:T(8,128)(2,1)}, u32[]{:S(2)}, u32[]{:S(2)}) collective-permute-start(bf16[192,3072]{1,0:T(8,128)(2,1)S(1)} %copy-done.3), channel_id=1, source_target_pairs={{0,2},{2,0},{1,3},{3,1},{4,6},{6,4},{5,7},{7,5},{8,10},{10,8},{9,1... | collective-permute-start | bytes 3538952 | tf_op jit(solution)/shard_map/ppermute | solution.py:503
  134.8 31.5 %collective-permute-start.25 = (bf16[192,3072]{1,0:T(8,128)(2,1)S(1)}, bf16[192,3072]{1,0:T(8,128)(2,1)}, u32[]{:S(2)}, u32[]{:S(2)}) collective-permute-start(bf16[192,3072]{1,0:T(8,128)(2,1)S(1)} %copy-done.3), channel_id=1, source_target_pairs={{0,16},{16,0},{1,17},{17,1},{2,18},{18,2},{3,19},{19,3},{4,20},{20... | collective-permute-start | bytes 3538952 | tf_op jit(solution)/shard_map/ppermute | solution.py:504
  136.3 29.9 %collective-permute-start.22 = (bf16[1536,384]{1,0:T(8,128)(2,1)}, bf16[1536,384]{1,0:T(8,128)(2,1)}, u32[]{:S(2)}, u32[]{:S(2)}) collective-permute-start(bf16[1536,384]{1,0:T(8,128)(2,1)} %broadcast_select_fusion), channel_id=1, source_target_pairs={{0,4},{4,0},{8,12},{12,8},{1,5},{5,1},{9,13},{13,9},{2,6},{6,2},{1... | collective-permute-start | bytes 3538952 | tf_op jit(solution)/shard_map/ppermute | solution.py:494
  139.9 26.3 %collective-permute-start.23 = (bf16[1536,384]{1,0:T(8,128)(2,1)}, bf16[1536,384]{1,0:T(8,128)(2,1)}, u32[]{:S(2)}, u32[]{:S(2)}) collective-permute-start(bf16[1536,384]{1,0:T(8,128)(2,1)} %collective-permute-done.16.refs_27_.refs_17_), channel_id=1, source_target_pairs={{4,8},{8,4},{5,9},{9,5},{6,10},{10,6},{7,11},{11,7},{20,24},{24,20... | collective-permute-start | bytes 3538952 | tf_op jit(solution)/shard_map/ppermute | solution.py:500
  141.7 24.6 %collective-permute-start.27 = (bf16[192,3072]{1,0:T(8,128)(2,1)}, bf16[192,3072]{1,0:T(8,128)(2,1)}, u32[]{:S(2)}, u32[]{:S(2)}) collective-permute-start(bf16[192,3072]{1,0:T(8,128)(2,1)} %collective-permute-done.18.refs_4_.refs_20_), channel_id=1, source_target_pairs={{0,1},{1,0},{2,3},{3,2},{4,5},{5,4},{6,7},{7,6},{8,9},{9,8},{10,11... | collective-permute-start | bytes 3538952 | tf_op jit(solution)/shard_map/ppermute | solution.py:511
  166.3 3.3 %collective-permute-start.28 = (bf16[192,3072]{1,0:T(8,128)(2,1)}, bf16[192,3072]{1,0:T(8,128)(2,1)}, u32[]{:S(2)}, u32[]{:S(2)}) collective-permute-start(bf16[192,3072]{1,0:T(8,128)(2,1)} %collective-permute-done.19.refs_0_), channel_id=1, source_target_pairs={{0,1},{1,0},{2,3},{3,2},{4,5},{5,4},{6,7},{7,6},{8,9},{9,8},{10,11... | collective-permute-start | bytes 3538952 | tf_op jit(solution)/shard_map/ppermute | solution.py:511
  169.5 17.6 %collective-permute-start.29 = (bf16[192,3072]{1,0:T(8,128)(2,1)}, bf16[192,3072]{1,0:T(8,128)(2,1)S(1)}, u32[]{:S(2)}, u32[]{:S(2)}) collective-permute-start(bf16[192,3072]{1,0:T(8,128)(2,1)} %collective-permute-done.24.refs_5_.refs_21_), channel_id=1, source_target_pairs={{0,1},{1,0},{2,3},{3,2},{4,5},{5,4},{6,7},{7,6},{8,9},{9,8},{10,11... | collective-permute-start | bytes 3538952 | tf_op jit(solution)/shard_map/ppermute | solution.py:511
  169.7 31.7 %collective-permute-start.30 = (bf16[1536,384]{1,0:T(8,128)(2,1)}, bf16[1536,384]{1,0:T(8,128)(2,1)}, u32[]{:S(2)}, u32[]{:S(2)}) collective-permute-start(bf16[1536,384]{1,0:T(8,128)(2,1)} %collective-permute-done.23.refs_16_), channel_id=1, source_target_pairs={{4,0},{8,12},{5,1},{9,13},{6,2},{10,14},{7,3},{11,15},{20,16},{24,... | collective-permute-start | bytes 3538952 | tf_op jit(solution)/shard_map/ppermute | solution.py:497
  171.0 30.4 %collective-permute-start.31 = (bf16[1536,384]{1,0:T(8,128)(2,1)}, bf16[1536,384]{1,0:T(8,128)(2,1)}, u32[]{:S(2)}, u32[]{:S(2)}) collective-permute-start(bf16[1536,384]{1,0:T(8,128)(2,1)} %collective-permute-done.22.refs_18_.refs_8_), channel_id=1, source_target_pairs={{4,8},{8,4},{5,9},{9,5},{6,10},{10,6},{7,11},{11,7},{20,24},{24,20... | collective-permute-start | bytes 3538952 | tf_op jit(solution)/shard_map/ppermute | solution.py:500
  172.6 28.7 %collective-permute-start.32 = (bf16[192,3072]{1,0:T(8,128)(2,1)}, bf16[192,3072]{1,0:T(8,128)(2,1)}, u32[]{:S(2)}, u32[]{:S(2)}) collective-permute-start(bf16[192,3072]{1,0:T(8,128)(2,1)} %collective-permute-done.19.refs_0_), channel_id=1, source_target_pairs={{0,2},{2,0},{1,3},{3,1},{4,6},{6,4},{5,7},{7,5},{8,10},{10,8},{9,1... | collective-permute-start | bytes 3538952 | tf_op jit(solution)/shard_map/ppermute | solution.py:503
  173.6 28.3 %collective-permute-start.33 = (bf16[192,3072]{1,0:T(8,128)(2,1)}, bf16[192,3072]{1,0:T(8,128)(2,1)}, u32[]{:S(2)}, u32[]{:S(2)}) collective-permute-start(bf16[192,3072]{1,0:T(8,128)(2,1)} %collective-permute-done.24.refs_5_.refs_21_), channel_id=1, source_target_pairs={{0,16},{16,0},{1,17},{17,1},{2,18},{18,2},{3,19},{19,3},{4,20},{20... | collective-permute-start | bytes 3538952 | tf_op jit(solution)/shard_map/ppermute | solution.py:504
  187.1 1.0 copy-start.9
  201.9 15.0 %collective-permute-start.39 = (bf16[192,3072]{1,0:T(8,128)(2,1)}, bf16[192,3072]{1,0:T(8,128)(2,1)S(1)}, u32[]{:S(2)}, u32[]{:S(2)}) collective-permute-start(bf16[192,3072]{1,0:T(8,128)(2,1)} %collective-permute-done.25.refs_1_), channel_id=1, source_target_pairs={{0,1},{1,0},{2,3},{3,2},{4,5},{5,4},{6,7},{7,6},{8,9},{9,8},{10,11... | collective-permute-start | bytes 3538952 | tf_op jit(solution)/shard_map/ppermute | solution.py:633
  201.9 16.9 %collective-permute-start.40 = (bf16[192,3072]{1,0:T(8,128)(2,1)}, bf16[192,3072]{1,0:T(8,128)(2,1)}, u32[]{:S(2)}, u32[]{:S(2)}) collective-permute-start(bf16[192,3072]{1,0:T(8,128)(2,1)} %collective-permute-done.32.refs_4_), channel_id=1, source_target_pairs={{0,1},{1,0},{2,3},{3,2},{4,5},{5,4},{6,7},{7,6},{8,9},{9,8},{10,11... | collective-permute-start | bytes 3538952 | tf_op jit(solution)/shard_map/ppermute | solution.py:633
  202.4 17.7 %collective-permute-start.41 = (bf16[192,3072]{1,0:T(8,128)(2,1)}, bf16[192,3072]{1,0:T(8,128)(2,1)}, u32[]{:S(2)}, u32[]{:S(2)}) collective-permute-start(bf16[192,3072]{1,0:T(8,128)(2,1)} %collective-permute-done.33.refs_5_), channel_id=1, source_target_pairs={{0,1},{1,0},{2,3},{3,2},{4,5},{5,4},{6,7},{7,6},{8,9},{9,8},{10,11... | collective-permute-start | bytes 3538952 | tf_op jit(solution)/shard_map/ppermute | solution.py:633
  215.2 19.9 %collective-permute-start.34 = (bf16[384,384]{1,0:T(8,128)(2,1)}, bf16[384,384]{1,0:T(8,128)(2,1)S(1)}, u32[]{:S(2)}, u32[]{:S(2)}) collective-permute-start(bf16[384,384]{1,0:T(8,128)(2,1)} %get-tuple-element.226), channel_id=1, source_target_pairs={{0,2},{2,0},{16,18},{18,16},{1,3},{3,1},{17,19},{19,17},{4,6},{6,4... | collective-permute-start | bytes 884744 | tf_op jit(solution)/shard_map/ppermute | solution.py:526
  216.4 18.8 %collective-permute-start.35 = (bf16[384,384]{1,0:T(8,128)(2,1)}, bf16[384,384]{1,0:T(8,128)(2,1)S(1)}, u32[]{:S(2)}, u32[]{:S(2)}) collective-permute-start(bf16[384,384]{1,0:T(8,128)(2,1)} %get-tuple-element.227), channel_id=1, source_target_pairs={{0,16},{2,18},{16,0},{18,2},{1,17},{3,19},{17,1},{19,3},{4,20},{6,... | collective-permute-start | bytes 884744 | tf_op jit(solution)/shard_map/ppermute | solution.py:526
  216.9 4.8 %copy-start.11 = (bf16[192,3072]{1,0:T(8,128)(2,1)}, bf16[192,3072]{1,0:T(8,128)(2,1)S(1)}, u32[]{:S(2)}) copy-start(bf16[192,3072]{1,0:T(8,128)(2,1)S(1)} %collective-permute-done.39.refs_3_) | copy-start | bytes 3538948
  216.9 18.3 %collective-permute-start.36 = (bf16[384,384]{1,0:T(8,128)(2,1)}, bf16[384,384]{1,0:T(8,128)(2,1)}, u32[]{:S(2)}, u32[]{:S(2)}) collective-permute-start(bf16[384,384]{1,0:T(8,128)(2,1)} %get-tuple-element.228), channel_id=1, source_target_pairs={{0,18},{2,16},{16,2},{18,0},{1,19},{3,17},{17,3},{19,1},{4,22},{6,... | collective-permute-start | bytes 884744 | tf_op jit(solution)/shard_map/ppermute | solution.py:526
  218.8 13.0 %collective-permute-start.37 = (bf16[384,128]{1,0:T(8,128)(2,1)}, bf16[384,128]{1,0:T(8,128)(2,1)S(1)}, u32[]{:S(2)}, u32[]{:S(2)}) collective-permute-start(bf16[384,128]{1,0:T(8,128)(2,1)} %get-tuple-element.229), channel_id=1, source_target_pairs={{4,0},{6,2},{8,12},{10,14},{20,16},{22,18},{24,28},{26,30},{5,1},{... | collective-permute-start | bytes 294920 | tf_op jit(solution)/shard_map/ppermute | solution.py:664
  220.1 13.1 %collective-permute-start.38 = (bf16[384,128]{1,0:T(8,128)(2,1)}, bf16[384,128]{1,0:T(8,128)(2,1)S(1)}, u32[]{:S(2)}, u32[]{:S(2)}) collective-permute-start(bf16[384,128]{1,0:T(8,128)(2,1)} %get-tuple-element.230), channel_id=1, source_target_pairs={{4,2},{6,0},{8,14},{10,12},{20,18},{22,16},{24,30},{26,28},{5,3},{... | collective-permute-start | bytes 294920 | tf_op jit(solution)/shard_map/ppermute | solution.py:664
  231.8 11.9 %copy-start.14 = (bf16[384,128]{1,0:T(8,128)(2,1)}, bf16[384,128]{1,0:T(8,128)(2,1)S(1)}, u32[]{:S(2)}) copy-start(bf16[384,128]{1,0:T(8,128)(2,1)S(1)} %collective-permute-done.37.refs_4_) | copy-start | bytes 294916
  231.8 10.1 %collective-permute-start.42 = (bf16[384,128]{1,0:T(8,128)(2,1)}, bf16[384,128]{1,0:T(8,128)(2,1)S(1)}, u32[]{:S(2)}, u32[]{:S(2)}) collective-permute-start(bf16[384,128]{1,0:T(8,128)(2,1)} %get-tuple-element.235), channel_id=1, source_target_pairs={{4,16},{6,18},{8,28},{10,30},{20,0},{22,2},{24,12},{26,14},{5,17},... | collective-permute-start | bytes 294920 | tf_op jit(solution)/shard_map/ppermute | solution.py:664
  233.1 10.6 %copy-start.15 = (bf16[384,128]{1,0:T(8,128)(2,1)}, bf16[384,128]{1,0:T(8,128)(2,1)S(1)}, u32[]{:S(2)}) copy-start(bf16[384,128]{1,0:T(8,128)(2,1)S(1)} %collective-permute-done.38.refs_5_) | copy-start | bytes 294916
  233.2 10.6 %collective-permute-start.43 = (bf16[384,128]{1,0:T(8,128)(2,1)}, bf16[384,128]{1,0:T(8,128)(2,1)S(1)}, u32[]{:S(2)}, u32[]{:S(2)}) collective-permute-start(bf16[384,128]{1,0:T(8,128)(2,1)} %get-tuple-element.236), channel_id=1, source_target_pairs={{4,18},{6,16},{8,30},{10,28},{20,2},{22,0},{24,14},{26,12},{5,19},... | collective-permute-start | bytes 294920 | tf_op jit(solution)/shard_map/ppermute | solution.py:664
  235.1 8.7 %copy-start.12 = (bf16[384,384]{1,0:T(8,128)(2,1)}, bf16[384,384]{1,0:T(8,128)(2,1)S(1)}, u32[]{:S(2)}) copy-start(bf16[384,384]{1,0:T(8,128)(2,1)S(1)} %collective-permute-done.34.refs_1_) | copy-start | bytes 884740
  235.1 8.7 %copy-start.13 = (bf16[384,384]{1,0:T(8,128)(2,1)}, bf16[384,384]{1,0:T(8,128)(2,1)S(1)}, u32[]{:S(2)}) copy-start(bf16[384,384]{1,0:T(8,128)(2,1)S(1)} %collective-permute-done.35.refs_2_) | copy-start | bytes 884740
  241.9 1.9 copy-start.16
  243.7 0.6 copy-start.17
